TPU v7x, 128 devices: a whole 4x4x4 slice. The times are simulated.
128 devices in a mesh: row: 32 (over z, x, core), col: 4 (over y).
Axes of the slice: x: 4, y: 4, z: 4, core: 2. Of those that a mesh axis runs over, the one named last changes fastest.
Arguments:
- features: bfloat16 [32768, 256], P(('col', 'row')), may hold values from -6 to 6
- cotangent: bfloat16 [32768, 256], P(('row', 'col')), may hold values from -6 to 6
- weight: bfloat16 [256, 256], replicated, may hold values from -0.375 to 0.375
- tile_values: bfloat16 [32, 4, 384, 128, 128], P('row', 'col'), may hold values from 0 to 0.011962891
- tile_rows: int32 [32, 4, 384], P('row', 'col'), may hold values from 0 to 7, as said below
- tile_cols: int32 [32, 4, 384], P('row', 'col'), may hold values from 0 to 63, as said below
- tile_count: int32 [32, 4], P('row', 'col'), may hold values from 128 to 384, as said below
Outputs:
- activated: bfloat16 [32768, 256], P(('row', 'col'))
- weight_grad: float32 [256, 256], replicated
- feature_grad: bfloat16 [32768, 256], P(('col', 'row'))
Inputs may be any that keep to these rules, and one draw needn't show every extreme that they name: On each device the first tile_count entries, with tile_cols, name distinct tiles in increasing order of tile_rows * 64 + tile_cols; all entries of a device are distinct tiles. `tile_cols`: see tile_rows. `tile_count`: some device has 384 nonzero tiles.
All inputs are finite; a program needn't handle non-finite values.
Results may differ from a plain program's by a relative error of at most 0.0065.
Values may be sent and summed in bfloat16 or wider, within the bound.
No kernel may reach another device: no remote copies, remote signals or barrier semaphores. Data moves between devices by JAX's collectives and lax.ppermute only.
A program may use at most 192 MiB of HBM per device.

v0:
```python
import jax
import jax.numpy as jnp
from jax import lax
from jax.sharding import PartitionSpec as P

block_turns = 12


def block_sum(values, rows_idx, cols_idx, count, source, out_blocks, forward):
    cap, tile = (values.shape[0], values.shape[1])
    feat = source.shape[1]
    in_blocks = source.shape[0] // tile
    flat_source = source.reshape(in_blocks, tile * feat)
    width = cap // block_turns
    slots = jnp.arange(cap, dtype=jnp.int32)
    xs = (
        values.reshape(block_turns, width, tile, tile),
        rows_idx.reshape(block_turns, width),
        cols_idx.reshape(block_turns, width),
        slots.reshape(block_turns, width),
    )
    in_ids = jnp.arange(in_blocks, dtype=jnp.int32)
    out_ids = jnp.arange(out_blocks, dtype=jnp.int32)

    def step(total, item):
        vals, rws, cls, slt = item
        live = slt < count
        if forward:
            source_idx, target_idx = (cls, rws)
        else:
            source_idx, target_idx = (rws, cls)
        pick_table = (source_idx[:, None] == in_ids[None, :]).astype(source.dtype)
        picked = jnp.dot(pick_table, flat_source, preferred_element_type=jnp.float32)
        picked = picked.astype(source.dtype).reshape(-1, tile, feat)
        if forward:
            prod = jnp.einsum("bij,bjf->bif", vals, picked, preferred_element_type=jnp.float32)
        else:
            prod = jnp.einsum("bji,bjf->bif", vals, picked, preferred_element_type=jnp.float32)
        place_table = ((out_ids[:, None] == target_idx[None, :]) & live[None, :]).astype(
            jnp.float32
        )
        added = jnp.dot(
            place_table,
            prod.reshape(-1, tile * feat),
            preferred_element_type=jnp.float32,
            precision=lax.Precision.HIGHEST,
        )
        return (total + added, None)

    start = jnp.zeros((out_blocks, tile * feat), jnp.float32)
    total, _ = lax.scan(step, start, xs)
    return total.reshape(out_blocks * tile, feat)


def body(features, cotangent, weight, tile_values, tile_rows, tile_cols, tile_count):
    values = tile_values[0, 0]
    rows_idx = tile_rows[0, 0]
    cols_idx = tile_cols[0, 0]
    count = tile_count[0, 0]
    tile = values.shape[1]
    rows_dev = features.shape[0]
    row_blocks = rows_dev * lax.axis_size("col") // tile
    band = lax.all_gather(features, "row", axis=0, tiled=True)
    col_blocks = band.shape[0] // tile
    partial_value = block_sum(values, rows_idx, cols_idx, count, band, row_blocks, True)
    agg = lax.psum_scatter(partial_value, "col", scatter_dimension=0, tiled=True).astype(
        jnp.bfloat16
    )
    pre = jnp.dot(agg, weight, preferred_element_type=jnp.float32)
    sigma = jax.nn.sigmoid(pre)
    activated = (pre * sigma).astype(jnp.bfloat16)
    dz = (cotangent.astype(jnp.float32) * sigma * (1.0 + pre * (1.0 - sigma))).astype(jnp.bfloat16)
    local_grad = jnp.dot(agg.T, dz, preferred_element_type=jnp.float32)
    back = jnp.dot(dz, weight.T, preferred_element_type=jnp.float32).astype(jnp.bfloat16)
    back_rows = lax.all_gather(back, "col", axis=0, tiled=True)
    weight_grad = lax.psum(local_grad, ("row", "col")) / rows_dev
    transposed = block_sum(values, rows_idx, cols_idx, count, back_rows, col_blocks, False)
    feature_grad = lax.psum_scatter(transposed, "row", scatter_dimension=0, tiled=True).astype(
        jnp.bfloat16
    )
    return (activated, weight_grad, feature_grad)


def solution(mesh):
    return jax.shard_map(
        body,
        mesh=mesh,
        in_specs=(
            P(("col", "row"), None),
            P(("row", "col"), None),
            P(),
            P("row", "col", None, None, None),
            P("row", "col", None),
            P("row", "col", None),
            P("row", "col"),
        ),
        out_specs=(P(("row", "col"), None), P(), P(("col", "row"), None)),
        check_vma=False,
    )
```

profile of v0, /device:TPU:0, one launch (start us, length us, event | category | flops | bytes accessed | tf_op | source)
XLA Modules:
  0.0 538.5 jit_solution(15657080376195936589)
XLA Ops:
  9.5 49.6 %all-gather.2.cloned.1.call-done = bf16[8192,256]{1,0:T(8,128)(2,1)} async-done(((bf16[256,256]{1,0:T(8,128)(2,1)}), bf16[8192,256]{1,0:T(8,128)(2,1)}) %all-gather.2.cloned.1.call-update) | async-done | bytes 4194320 | tf_op jit(solution)/shard_map/all_gather | solution.py:63
  59.2 7.5 %reshape.53 = bf16[64,32768]{1,0:T(8,128)(2,1)} reshape(bf16[8192,256]{1,0:T(8,128)(2,1)} %all-gather.2.cloned.1.call-done) | data formatting | bytes 8388608 | tf_op jit(solution)/shard_map/reshape | solution.py:13
  66.6 126.9 %while.22 = (s32[]{:T(128)}, f32[8,32768]{1,0:T(8,128)S(1)}, s32[12,32]{1,0:T(8,128)S(1)}, s32[12,32]{1,0:T(8,128)S(1)}, s32[]{:T(128)}, /*index=5*/bf16[12,32,1...) while((s32[]{:T(128)}, f32[8,32768]{1,0:T(8,128)S(1)}, ...), condition=%wide.region_1.2_spmd.clone, body=%wide.region_0.1_spmd.clone.sunk | while | flops 504891936 | bytes 32506948 | solution.py:51
  194.8 16.7 %copy.10 = bf16[1,1,384,128,128]{3,4,2,1,0:T(8,128)(2,1)} copy(bf16[1,1,384,128,128]{4,3,2,1,0:T(8,128)(2,1)} %bitcast.90) | data formatting | bytes 25165824 | tf_op args[3]
  211.5 6.2 %reduce-scatter.3.cloned.1.call-done = f32[256,256]{1,0:T(8,128)} async-done(((f32[1024,256]{1,0:T(8,128)}), f32[256,256]{1,0:T(8,128)}) %reduce-scatter.3.cloned.1.call-update) | async-done | bytes 262160 | tf_op jit(solution)/shard_map/reduce_scatter | solution.py:66
  221.8 13.0 %all_gather.7 = bf16[1024,256]{1,0:T(8,128)(2,1)S(1)} all-gather(bf16[256,256]{1,0:T(8,128)(2,1)S(1)} %convolution_convert_fusion.2), channel_id=1, replica_groups=mesh['row'=32,'col'=4] {'col'}, dimensions={0}, use_global_device_ids=true | all-gather | bytes 655360 | tf_op jit(solution)/shard_map/all_gather | solution.py:75
  235.0 193.4 %while.23 = (s32[]{:T(128)}, f32[64,32768]{1,0:T(8,128)}, s32[12,32]{1,0:T(8,128)S(1)}, s32[12,32]{1,0:T(8,128)S(1)}, s32[]{:T(128)}, /*index=5*/bf16[12,32,128,...) while((s32[]{:T(128)}, f32[64,32768]{1,0:T(8,128)}, ...), condition=%wide.region_5.6_spmd.clone, body=%wide.region_4.5_spmd.clone.sunk | while | flops 1095766272 | bytes 102237328 | solution.py:51
  241.5 6.4 %convolution_add_fusion.5 = f32[64,32768]{1,0:T(8,128)S(1)} fusion(f32[32,32768]{1,0:T(8,128)S(1)} %bitcast.82, f32[64,32768]{1,0:T(8,128)S(1)} %bitcast.84, pred[]{:T(512)S(6)} %compare.7, s32[32]{0:T(128)S(1)} %get-tuple-element.322, pred[32]{0:T(512)(128)(4,1)S(1)} %compare_bitcast_fusion.5), kind=kOutput, calls=%fused_computation.22.clone.1 | convolution fusion | flops 809504768 | bytes 20971680 | tf_op jit(solution)/shard_map/while/body/eval_jaxpr/dot_general | solution.py:42
  248.0 3.2 copy-done.2
  257.6 6.5 %convolution_add_fusion.5 = f32[64,32768]{1,0:T(8,128)S(1)} fusion(f32[32,32768]{1,0:T(8,128)S(1)} %bitcast.82, f32[64,32768]{1,0:T(8,128)S(1)} %bitcast.84, pred[]{:T(512)S(6)} %compare.7, s32[32]{0:T(128)S(1)} %get-tuple-element.322, pred[32]{0:T(512)(128)(4,1)S(1)} %compare_bitcast_fusion.5), kind=kOutput, calls=%fused_computation.22.clone.1 | convolution fusion | flops 809504768 | bytes 20971680 | tf_op jit(solution)/shard_map/while/body/eval_jaxpr/dot_general | solution.py:42
  264.1 3.2 copy-done.2
  273.8 6.5 %convolution_add_fusion.5 = f32[64,32768]{1,0:T(8,128)S(1)} fusion(f32[32,32768]{1,0:T(8,128)S(1)} %bitcast.82, f32[64,32768]{1,0:T(8,128)S(1)} %bitcast.84, pred[]{:T(512)S(6)} %compare.7, s32[32]{0:T(128)S(1)} %get-tuple-element.322, pred[32]{0:T(512)(128)(4,1)S(1)} %compare_bitcast_fusion.5), kind=kOutput, calls=%fused_computation.22.clone.1 | convolution fusion | flops 809504768 | bytes 20971680 | tf_op jit(solution)/shard_map/while/body/eval_jaxpr/dot_general | solution.py:42
  280.3 3.2 copy-done.2
  290.0 6.4 %convolution_add_fusion.5 = f32[64,32768]{1,0:T(8,128)S(1)} fusion(f32[32,32768]{1,0:T(8,128)S(1)} %bitcast.82, f32[64,32768]{1,0:T(8,128)S(1)} %bitcast.84, pred[]{:T(512)S(6)} %compare.7, s32[32]{0:T(128)S(1)} %get-tuple-element.322, pred[32]{0:T(512)(128)(4,1)S(1)} %compare_bitcast_fusion.5), kind=kOutput, calls=%fused_computation.22.clone.1 | convolution fusion | flops 809504768 | bytes 20971680 | tf_op jit(solution)/shard_map/while/body/eval_jaxpr/dot_general | solution.py:42
  306.1 6.4 %convolution_add_fusion.5 = f32[64,32768]{1,0:T(8,128)S(1)} fusion(f32[32,32768]{1,0:T(8,128)S(1)} %bitcast.82, f32[64,32768]{1,0:T(8,128)S(1)} %bitcast.84, pred[]{:T(512)S(6)} %compare.7, s32[32]{0:T(128)S(1)} %get-tuple-element.322, pred[32]{0:T(512)(128)(4,1)S(1)} %compare_bitcast_fusion.5), kind=kOutput, calls=%fused_computation.22.clone.1 | convolution fusion | flops 809504768 | bytes 20971680 | tf_op jit(solution)/shard_map/while/body/eval_jaxpr/dot_general | solution.py:42
  322.2 6.4 %convolution_add_fusion.5 = f32[64,32768]{1,0:T(8,128)S(1)} fusion(f32[32,32768]{1,0:T(8,128)S(1)} %bitcast.82, f32[64,32768]{1,0:T(8,128)S(1)} %bitcast.84, pred[]{:T(512)S(6)} %compare.7, s32[32]{0:T(128)S(1)} %get-tuple-element.322, pred[32]{0:T(512)(128)(4,1)S(1)} %compare_bitcast_fusion.5), kind=kOutput, calls=%fused_computation.22.clone.1 | convolution fusion | flops 809504768 | bytes 20971680 | tf_op jit(solution)/shard_map/while/body/eval_jaxpr/dot_general | solution.py:42
  338.3 6.4 %convolution_add_fusion.5 = f32[64,32768]{1,0:T(8,128)S(1)} fusion(f32[32,32768]{1,0:T(8,128)S(1)} %bitcast.82, f32[64,32768]{1,0:T(8,128)S(1)} %bitcast.84, pred[]{:T(512)S(6)} %compare.7, s32[32]{0:T(128)S(1)} %get-tuple-element.322, pred[32]{0:T(512)(128)(4,1)S(1)} %compare_bitcast_fusion.5), kind=kOutput, calls=%fused_computation.22.clone.1 | convolution fusion | flops 809504768 | bytes 20971680 | tf_op jit(solution)/shard_map/while/body/eval_jaxpr/dot_general | solution.py:42
  354.4 6.4 %convolution_add_fusion.5 = f32[64,32768]{1,0:T(8,128)S(1)} fusion(f32[32,32768]{1,0:T(8,128)S(1)} %bitcast.82, f32[64,32768]{1,0:T(8,128)S(1)} %bitcast.84, pred[]{:T(512)S(6)} %compare.7, s32[32]{0:T(128)S(1)} %get-tuple-element.322, pred[32]{0:T(512)(128)(4,1)S(1)} %compare_bitcast_fusion.5), kind=kOutput, calls=%fused_computation.22.clone.1 | convolution fusion | flops 809504768 | bytes 20971680 | tf_op jit(solution)/shard_map/while/body/eval_jaxpr/dot_general | solution.py:42
  370.5 6.4 %convolution_add_fusion.5 = f32[64,32768]{1,0:T(8,128)S(1)} fusion(f32[32,32768]{1,0:T(8,128)S(1)} %bitcast.82, f32[64,32768]{1,0:T(8,128)S(1)} %bitcast.84, pred[]{:T(512)S(6)} %compare.7, s32[32]{0:T(128)S(1)} %get-tuple-element.322, pred[32]{0:T(512)(128)(4,1)S(1)} %compare_bitcast_fusion.5), kind=kOutput, calls=%fused_computation.22.clone.1 | convolution fusion | flops 809504768 | bytes 20971680 | tf_op jit(solution)/shard_map/while/body/eval_jaxpr/dot_general | solution.py:42
  386.6 6.4 %convolution_add_fusion.5 = f32[64,32768]{1,0:T(8,128)S(1)} fusion(f32[32,32768]{1,0:T(8,128)S(1)} %bitcast.82, f32[64,32768]{1,0:T(8,128)S(1)} %bitcast.84, pred[]{:T(512)S(6)} %compare.7, s32[32]{0:T(128)S(1)} %get-tuple-element.322, pred[32]{0:T(512)(128)(4,1)S(1)} %compare_bitcast_fusion.5), kind=kOutput, calls=%fused_computation.22.clone.1 | convolution fusion | flops 809504768 | bytes 20971680 | tf_op jit(solution)/shard_map/while/body/eval_jaxpr/dot_general | solution.py:42
  402.7 6.4 %convolution_add_fusion.5 = f32[64,32768]{1,0:T(8,128)S(1)} fusion(f32[32,32768]{1,0:T(8,128)S(1)} %bitcast.82, f32[64,32768]{1,0:T(8,128)S(1)} %bitcast.84, pred[]{:T(512)S(6)} %compare.7, s32[32]{0:T(128)S(1)} %get-tuple-element.322, pred[32]{0:T(512)(128)(4,1)S(1)} %compare_bitcast_fusion.5), kind=kOutput, calls=%fused_computation.22.clone.1 | convolution fusion | flops 809504768 | bytes 20971680 | tf_op jit(solution)/shard_map/while/body/eval_jaxpr/dot_general | solution.py:42
  418.8 6.4 %convolution_add_fusion.5 = f32[64,32768]{1,0:T(8,128)S(1)} fusion(f32[32,32768]{1,0:T(8,128)S(1)} %bitcast.82, f32[64,32768]{1,0:T(8,128)S(1)} %bitcast.84, pred[]{:T(512)S(6)} %compare.7, s32[32]{0:T(128)S(1)} %get-tuple-element.322, pred[32]{0:T(512)(128)(4,1)S(1)} %compare_bitcast_fusion.5), kind=kOutput, calls=%fused_computation.22.clone.1 | convolution fusion | flops 809504768 | bytes 20971680 | tf_op jit(solution)/shard_map/while/body/eval_jaxpr/dot_general | solution.py:42
  428.4 9.3 %reshape.56 = f32[8192,256]{1,0:T(8,128)} reshape(f32[64,32768]{1,0:T(8,128)} %get-tuple-element.108) | data formatting | bytes 16777216 | tf_op jit(solution)/shard_map/reshape | solution.py:52
  439.5 90.8 %reduce-scatter.5.cloned.1.call-done = f32[256,256]{1,0:T(8,128)} async-done(((f32[8192,256]{1,0:T(8,128)}), f32[256,256]{1,0:T(8,128)}) %reduce-scatter.5.cloned.1.call-update) | async-done | bytes 262160 | tf_op jit(solution)/shard_map/reduce_scatter | solution.py:78
  (266 shorter events, 243.2 us)
Async XLA Ops:
  7.2 210.5 %copy-start = (bf16[256,256]{1,0:T(8,128)(2,1)S(1)}, bf16[256,256]{1,0:T(8,128)(2,1)}, u32[]{:S(2)}) copy-start(bf16[256,256]{1,0:T(8,128)(2,1)} %param.13) | copy-start | bytes 393220
  7.2 52.0 %all-gather.2.cloned.1.call-start = ((), (), s32[]{:S(2)}) async-start(), calls=%async_computation.2 | async-start | bytes 4325376 | tf_op jit(solution)/shard_map/all_gather | solution.py:63
  7.9 209.8 %reduce-scatter.3.cloned.1.call-start = ((), (), s32[]{:S(2)}) async-start(), calls=%async_computation.3 | async-start | bytes 1310720 | tf_op jit(solution)/shard_map/reduce_scatter | solution.py:66
  194.7 243.1 %all-reduce.2.cloned.1.call-start = ((), (), s32[]{:S(2)}) async-start(), calls=%async_computation.4 | async-start | bytes 524288 | tf_op jit(solution)/shard_map/psum | solution.py:76
  194.7 23.0 %copy-start.3 = (bf16[256,256]{1,0:T(8,128)(2,1)S(1)}, bf16[256,256]{1,0:T(8,128)(2,1)}, u32[]{:S(2)}) copy-start(bf16[256,256]{1,0:T(8,128)(2,1)} %param.12) | copy-start | bytes 393220
  221.7 308.6 %reduce-scatter.5.cloned.1.call-start = ((), (), s32[]{:S(2)}) async-start(), calls=%async_computation.5 | async-start | bytes 8650752 | tf_op jit(solution)/shard_map/reduce_scatter | solution.py:78
  237.0 4.5 slice-start
  247.9 3.2 copy-start.2
  253.1 4.6 slice-start
  264.1 3.2 copy-start.2
  269.3 4.5 slice-start
  280.3 3.2 copy-start.2
  285.4 4.5 slice-start
  296.4 3.2 copy-start.2
  301.5 4.6 slice-start
  312.5 3.2 copy-start.2
  317.7 4.5 slice-start
  333.8 4.5 slice-start
  349.9 4.5 slice-start
  366.0 4.5 slice-start
  382.1 4.5 slice-start
  398.2 4.5 slice-start
  414.3 4.5 slice-start
  437.7 94.2 %copy-start.1 = (bf16[256,256]{1,0:T(8,128)(2,1)S(1)}, bf16[256,256]{1,0:T(8,128)(2,1)}, u32[]{:S(2)}) copy-start(bf16[256,256]{1,0:T(8,128)(2,1)} %param.13) | copy-start | bytes 393220
  (19 other events, 51.9 us)
Sparse Core Ops, SparseCore 0:
  10.3 48.8 all-gather.1
  194.8 22.8 reduce-scatter.2
  223.7 141.6 all-reduce.1
  437.9 92.3 reduce-scatter.4
where the time goes:
time: 541 us; the launch traced here: 538 us
  matrix products  198 us (37%)
  waiting for transfers between devices  147 us (27%)
  local copies, waits for them, and re-layouts  144 us (27%)
  other arithmetic  20.5 us (4%)
  between operations  13.8 us (3%)
  blocking collectives  13 us (2%)
    while x120, local copies, waits for them, and re-layouts  109 us
    dot_general x24, matrix products, step(): jnp.dot(place_table, prod.reshape(-1, tile * feat), preferred_element_typ...  102 us
    reduce_scatter x1, waiting for transfers between devices, body(): lax.psum_scatter(transposed, 'row', scatter_dimension=0, tiled=True)  90.8 us
    all_gather x1, waiting for transfers between devices, body(): band = lax.all_gather(features, 'row', axis=0, tiled=True)  49.6 us
    dot_general x24, matrix products, step(): jnp.dot(pick_table, flat_source, preferred_element_type=jnp.float32)  44.2 us
    dot_general x12, matrix products, step(): jnp.einsum('bji,bjf->bif', vals, picked, preferred_element_type=jnp.float32)  25 us
    dot_general x12, matrix products, step(): jnp.einsum('bij,bjf->bif', vals, picked, preferred_element_type=jnp.float32)  23.2 us
    unnamed x7, local copies, waits for them, and re-layouts  16.7 us
  transfers between devices with their start and end apart: 4, of which 3 were waited for; matrix products, arithmetic and copies ran while one was open for 34% of the time, Pallas kernels for 0%

commit v1 on v0

v1 whole, which is shorter than its diff:
```python
import functools

import jax
import jax.numpy as jnp
from jax import lax
from jax.experimental import pallas as pl
from jax.experimental.pallas import tpu as pltpu
from jax.sharding import Mesh
from jax.sharding import PartitionSpec as P

F32 = jnp.float32
BF16 = jnp.bfloat16
TILE = 128
FEAT = 256
NODE = 256
HALF = 128
ROWS = 1024
NCT = 64
CAP = 384
MIB = 1 << 20
PZ, PX, PC, PY = 0, 1, 2, 3


def shape(s, dt):
    return jax.ShapeDtypeStruct(s, dt)


VSPEC = pl.BlockSpec(memory_space=pltpu.VMEM)
SSPEC = pl.BlockSpec(memory_space=pltpu.SMEM)
ASPEC = pl.BlockSpec(memory_space=pl.ANY)


def in_vmem(x):
    return pltpu.with_memory_space_constraint(x, pltpu.VMEM)


def call(kernel, outs, in_specs, scratch=(), flops=0, nbytes=0, limit=16, aliases=None):
    return pl.pallas_call(
        kernel,
        out_shape=outs,
        in_specs=in_specs,
        out_specs=jax.tree.map(lambda _: VSPEC, outs),
        scratch_shapes=list(scratch),
        input_output_aliases=aliases or {},
        cost_estimate=pl.CostEstimate(flops=flops, bytes_accessed=nbytes, transcendentals=0),
        compiler_params=pltpu.CompilerParams(vmem_limit_bytes=limit * MIB),
    )


def place_tiles(lo, hi, tv, rows, cols, dense, sem):
    def copy(s):
        return pltpu.make_async_copy(
            tv.at[s],
            dense.at[cols[s], pl.ds(pl.multiple_of(rows[s] * TILE, TILE), TILE), :],
            sem,
        )

    def start(s, _):
        copy(s).start()
        return 0

    def wait(s, _):
        copy(s).wait()
        return 0

    lax.fori_loop(lo, hi, start, 0)
    lax.fori_loop(lo, hi, wait, 0)


def dense_first(part, tv, rows, cols, count, dense, sem):
    @pl.loop(0, NCT)
    def _(c):
        dense[c] = jnp.zeros((ROWS, TILE), BF16)

    place_tiles(0, jnp.minimum(count[0], part), tv, rows, cols, dense, sem)


def dense_rest(part, tv, rows, cols, count, given, dense, sem):
    del given
    place_tiles(jnp.minimum(count[0], part), count[0], tv, rows, cols, dense, sem)


def columns(dense, z, x, core, dz, dx):
    b = lax.rem(z + dz, 4) * 8 + lax.rem(x + dx, 4) * 2 + core
    return dense[2 * b], dense[2 * b + 1]


def forward_sum(dense, near, far, z, x, core, acc, add):
    for dz in range(4):
        lhs, rhs = [], []
        for dx in range(4):
            lhs += columns(dense, z, x, core, dz, dx)
            if dz == 0:
                rhs.append(near[dx * NODE : (dx + 1) * NODE])
            elif dx == 0:
                rhs.append(near[(3 + dz) * NODE : (4 + dz) * NODE])
            else:
                i = (dz - 1) * 384 + (dx - 1) * HALF
                j = 1152 + (dx - 1) * 384 + (dz - 1) * HALF
                rhs += [far[i : i + HALF], far[j : j + HALF]]
        term = jnp.dot(
            jnp.concatenate(lhs, axis=1),
            jnp.concatenate(rhs, axis=0),
            preferred_element_type=F32,
        )
        if dz == 0 and not add:
            acc[...] = term
        else:
            acc[...] += term


def forward_own(pos, dense, near, far, acc):
    forward_sum(dense, near, far, pos[PZ], pos[PX], pos[PC], acc, False)


def forward_other(pos, dense, near, far, given, own, s1, s2, s3, acc):
    acc[...] = given[...]
    forward_sum(dense, near, far, pos[PZ], pos[PX], 1 - pos[PC], acc, True)
    y = pos[PY]
    for d, out in enumerate((own, s1, s2, s3)):
        row = pl.multiple_of(lax.rem(y + d, 4) * NODE, NODE)
        out[...] = acc[pl.ds(row, NODE), :].astype(out.dtype)


def middle(pos, own, r1, r2, r3, w, cot, act, bt, q, m1, m2, m3, lg):
    agg = (own[...] + r1[...].astype(F32) + r2[...].astype(F32) + r3[...].astype(F32)).astype(BF16)
    pre = jnp.dot(agg, w[...], preferred_element_type=F32)
    sg = jax.nn.sigmoid(pre)
    act[...] = (pre * sg).astype(BF16)
    dz = (cot[...].astype(F32) * sg * (1.0 + pre * (1.0 - sg))).astype(BF16)
    back = lax.dot_general(w[...], dz, (((1,), (1,)), ((), ())), preferred_element_type=F32).astype(
        BF16
    )
    lg[...] = lax.dot_general(agg, dz, (((0,), (0,)), ((), ())), preferred_element_type=F32)
    bt[...] = back
    y = pos[PY]
    for d, out in enumerate((q, m1, m2, m3)):
        row = pl.multiple_of(lax.rem(y + d, 4) * 64, 64)
        piece = lg[pl.ds(row, 64), :]
        if d == 0:
            out[...] = piece
        else:
            out[:NODE] = back
            out[NODE:] = piece.astype(BF16)


def back_all(bt):
    return jnp.concatenate([bt[0], bt[1], bt[2], bt[3]], axis=1)


def backward_block(dense, lhs, z, x, core, dz, dx):
    rhs = jnp.concatenate(columns(dense, z, x, core, dz, dx), axis=1)
    return jnp.dot(lhs, rhs, preferred_element_type=F32)


def backward_other(pos, dense, own, r1, r2, r3, q, out, bt, qown, qsum):
    z, x, core, y = pos[PZ], pos[PX], pos[PC], pos[PY]
    bt[y] = own[...]
    total = q[...]
    for d, r in ((1, r1), (2, r2), (3, r3)):
        bt[lax.rem(y + 4 - d, 4)] = r[:NODE]
        total += r[NODE:].astype(F32)
    qsum[...] = total
    qown[...] = qsum[pl.ds(pl.multiple_of(core * 32, 32), 32), :]
    out[16 * NODE :] = qsum[pl.ds(pl.multiple_of((1 - core) * 32, 32), 32), :].astype(BF16)
    lhs = back_all(bt)

    @pl.loop(0, 16)
    def _(i):
        row = pl.multiple_of(i * NODE, NODE)
        g = backward_block(dense, lhs, z, x, 1 - core, i % 4, i // 4)
        out[pl.ds(row, NODE), :] = g.astype(BF16)


def backward_own(pos, dense, bt, got, qown, x0, z0, x1, x2, x3, z1, z2, z3, qs):
    z, x, core = pos[PZ], pos[PX], pos[PC]
    qs[...] = qown[...] + got[16 * NODE :].astype(F32)
    lhs = back_all(bt)
    xs, zs = (x0, x1, x2, x3), (z0, z1, z2, z3)
    for dx in range(4):
        for dz in range(4):
            i = (dx * 4 + dz) * NODE
            g = backward_block(dense, lhs, z, x, core, dz, dx) + got[i : i + NODE].astype(F32)
            xs[dx][dz * HALF : (dz + 1) * HALF] = g[:HALF].astype(xs[dx].dtype)
            zs[dz][dx * HALF : (dx + 1) * HALF] = g[HALF:].astype(zs[dz].dtype)


def first_sum(x0, x1, x2, x3, z0, z1, z2, z3, t0, a1, a2, a3, t1, b1, b2, b3):
    for parts, outs in (((x0, x1, x2, x3), (t0, a1, a2, a3)), ((z0, z1, z2, z3), (t1, b1, b2, b3))):
        for d in range(4):
            at = slice(d * HALF, (d + 1) * HALF)
            s = parts[0][at]
            for p in parts[1:]:
                s += p[at].astype(F32)
            outs[d][...] = s.astype(outs[d].dtype)


def last_sum(t0, a1, a2, a3, t1, b1, b2, b3, out):
    h0, h1 = t0[...], t1[...]
    for p in (a1, a2, a3):
        h0 += p[...].astype(F32)
    for p in (b1, b2, b3):
        h1 += p[...].astype(F32)
    out[...] = jnp.concatenate([h0, h1], axis=0).T.astype(BF16)


def ring_sum(axis, pos, own, r1, r2, r3, out, held):
    i = pos[axis]
    for d, r in enumerate((own, r1, r2, r3)):
        held[lax.rem(i + 4 - d, 4)] = r[...]
    out[...] = (held[0] + held[1]) + (held[2] + held[3])


def weight_rows(pos, own, r1, r2, r3, out):
    y = pos[PY]
    for d, r in enumerate((own, r1, r2, r3)):
        row = pl.multiple_of(lax.rem(y + 4 - d, 4) * 64, 64)
        out[pl.ds(row, 64), :] = r[...] * (1.0 / NODE)


def weight_pair(pos, own, other, out):
    core = pos[PC]
    out[pl.ds(pl.multiple_of(core * 32, 32), 32), :] = own[...]
    out[pl.ds(pl.multiple_of((1 - core) * 32, 32), 32), :] = other[...]


def send(v, axis, d, n=4):
    return lax.ppermute(v, axis, [(i, (i + d) % n) for i in range(n)])


def body(features, cotangent, weight, tile_values, tile_rows, tile_cols, tile_count):
    tv, rows, cols, count = tile_values[0, 0], tile_rows[0, 0], tile_cols[0, 0], tile_count[0]
    pos = jnp.stack([lax.axis_index(a) for a in ("z", "x", "core", "y")]).astype(jnp.int32)
    big = NCT * ROWS * TILE

    px = [send(features, "x", -d) for d in (1, 2, 3)]
    pz = [send(features, "z", -d) for d in (1, 2, 3)]
    part = 128
    dense_out = pltpu.VMEM((NCT, ROWS, TILE), BF16)
    dense = call(
        functools.partial(dense_first, part),
        dense_out,
        [ASPEC, SSPEC, SSPEC, SSPEC],
        [pltpu.SemaphoreType.DMA],
        nbytes=12 * MIB,
    )(tv, rows, cols, count)
    fx = jnp.concatenate([p[:HALF] for p in px], axis=0)
    fz = jnp.concatenate([p[HALF:] for p in pz], axis=0)
    zf = [send(fx, "z", -d) for d in (1, 2, 3)]
    xf = [send(fz, "x", -d) for d in (1, 2, 3)]
    near = jnp.concatenate([features] + px + pz, axis=0)
    near_other = send(near, "core", 1, 2)
    dense = call(
        functools.partial(dense_rest, part),
        dense_out,
        [ASPEC, SSPEC, SSPEC, SSPEC, VSPEC],
        [pltpu.SemaphoreType.DMA],
        nbytes=24 * MIB,
        aliases={4: 0},
    )(tv, rows, cols, count, in_vmem(dense))
    dense = in_vmem(dense)
    far = jnp.concatenate(zf + xf, axis=0)
    far_other = send(far, "core", 1, 2)

    acc = call(
        forward_own,
        shape((ROWS, FEAT), F32),
        [SSPEC, VSPEC, VSPEC, VSPEC],
        flops=big * FEAT,
        nbytes=big,
    )(pos, dense, near, far)
    block = shape((NODE, FEAT), BF16)
    own, s1, s2, s3 = call(
        forward_other,
        [shape((NODE, FEAT), F32), block, block, block],
        [SSPEC] + [VSPEC] * 4,
        [pltpu.VMEM((ROWS, FEAT), F32)],
        flops=big * FEAT,
        nbytes=big,
    )(pos, dense, near_other, far_other, acc)
    r = [send(s, "y", d) for d, s in ((1, s1), (2, s2), (3, s3))]

    packed = shape((NODE + 64, FEAT), BF16)
    activated, bt, q, m1, m2, m3 = call(
        middle,
        [block, block, shape((64, FEAT), F32), packed, packed, packed],
        [SSPEC] + [VSPEC] * 6,
        [pltpu.VMEM((FEAT, FEAT), F32)],
        flops=6 * FEAT**3,
        nbytes=MIB,
    )(pos, own, *r, weight, cotangent)
    r = [send(m, "y", d) for d, m in ((1, m1), (2, m2), (3, m3))]

    other, bt, qown = call(
        backward_other,
        [shape((16 * NODE + 32, FEAT), BF16), shape((4, FEAT, NODE), BF16), shape((32, FEAT), F32)],
        [SSPEC] + [VSPEC] * 6,
        [pltpu.VMEM((64, FEAT), F32)],
        flops=big * FEAT,
        nbytes=big,
    )(pos, dense, bt, *r, q)
    got = send(other, "core", 1, 2)
    long, longf = shape((4 * HALF, FEAT), BF16), shape((4 * HALF, FEAT), F32)
    x0, z0, x1, x2, x3, z1, z2, z3, qs = call(
        backward_own,
        [longf, longf] + [long] * 6 + [shape((32, FEAT), F32)],
        [SSPEC] + [VSPEC] * 4,
        flops=big * FEAT,
        nbytes=big,
    )(pos, dense, bt, got, qown)
    rx = [send(v, "x", d) for d, v in ((1, x1), (2, x2), (3, x3))]
    rz = [send(v, "z", d) for d, v in ((1, z1), (2, z2), (3, z3))]

    def ring(axis, place, v):
        got = [send(v, axis, d) for d in (1, 2, 3)]
        return call(
            functools.partial(ring_sum, place),
            shape(v.shape, F32),
            [SSPEC] + [VSPEC] * 4,
            [pltpu.VMEM((4,) + v.shape, F32)],
            nbytes=MIB // 4,
        )(pos, v, *got)

    qs = ring("z", PZ, ring("x", PX, qs))
    pair = call(weight_pair, shape((64, FEAT), F32), [SSPEC, VSPEC, VSPEC], nbytes=MIB // 8)(
        pos, qs, send(qs, "core", 1, 2)
    )
    weight_grad = call(
        weight_rows, shape((FEAT, FEAT), F32), [SSPEC] + [VSPEC] * 4, nbytes=MIB // 2
    )(pos, pair, *[send(pair, "y", d) for d in (1, 2, 3)])

    short, shortf = shape((HALF, FEAT), BF16), shape((HALF, FEAT), F32)
    t0, a1, a2, a3, t1, b1, b2, b3 = call(
        first_sum,
        [shortf, short, short, short] * 2,
        [VSPEC] * 8,
        nbytes=4 * MIB,
    )(x0, *rx, z0, *rz)
    ra = [send(v, "z", d) for d, v in ((1, a1), (2, a2), (3, a3))]
    rb = [send(v, "x", d) for d, v in ((1, b1), (2, b2), (3, b3))]
    feature_grad = call(last_sum, block, [VSPEC] * 8, nbytes=MIB)(t0, *ra, t1, *rb)
    return activated, weight_grad, feature_grad


def solution(mesh):
    parts = Mesh(mesh.devices.reshape(4, 4, 2, 4), ("z", "x", "core", "y"))
    row = ("z", "x", "core")
    return jax.shard_map(
        body,
        mesh=parts,
        in_specs=(
            P(("y",) + row, None),
            P(row + ("y",), None),
            P(),
            P(row, "y", None, None, None),
            P(row, "y", None),
            P(row, "y", None),
            P(row, "y"),
        ),
        out_specs=(P(row + ("y",), None), P(), P(("y",) + row, None)),
        check_vma=False,
    )
```

time: 541 us -> 157 us (0.29)
  matrix products: 198 us -> 0 us
  local copies, waits for them, and re-layouts: 144 us -> 5.73 us
  waiting for transfers between devices: 147 us -> 45.2 us
  starting transfers between devices: 0.16 us -> 57.5 us
  Pallas kernels: 0 us -> 45 us
  other arithmetic: 20.5 us -> 0.15 us
  blocking collectives: 13 us -> 0 us
  between operations: 13.8 us -> 1.7 us
    dot_general x75 -> x0, matrix products: 198 us -> none  [the longest x24 102 us: step(): jnp.dot(place_table, prod.reshape(-1, tile * feat), preferred_element_typ...]
    while x120 -> x0, local copies, waits for them, and re-layouts: 109 us -> none
    reduce_scatter x2 -> x0, waiting for transfers between devices: 97.1 us -> none  [the longest x1 90.8 us: body(): lax.psum_scatter(transposed, 'row', scatter_dimension=0, tiled=True)]
    ppermute x0 -> x43, starting transfers between devices: none -> 57.5 us  [send(): return lax.ppermute(v, axis, [(i, (i + d) % n) for i in range(n)])]
    all_gather x1 -> x0, waiting for transfers between devices: 49.6 us -> none  [body(): band = lax.all_gather(features, 'row', axis=0, tiled=True)]
    ppermute x0 -> x43, waiting for transfers between devices: none -> 45.2 us  [send(): return lax.ppermute(v, axis, [(i, (i + d) % n) for i in range(n)])]
    pallas_call x0 -> x13, Pallas kernels: none -> 45 us  [the longest x1 14.2 us: body(): call(functools.partial(dense_rest, part), dense_out, [ASPEC, SSPEC, SSPEC...]
    reshape x4 -> x0, local copies, waits for them, and re-layouts: 18.1 us -> none  [the longest x2 10.4 us: block_sum(): return total.reshape(out_blocks * tile, feat)]
  transfers between devices with their start and end apart: 4 -> 43, of which waited for: 3 -> 19; matrix products, arithmetic and copies ran while one was open for 34% -> 1% of each run, Pallas kernels for 0% -> 20%
where the time goes in v1:
time: 157 us; the launch traced here: 155 us
  starting transfers between devices  57.5 us (37%)
  waiting for transfers between devices  45.2 us (29%)
  Pallas kernels  45 us (29%)
  local copies, waits for them, and re-layouts  5.73 us (4%)
  between operations  1.7 us (1%)
    ppermute x43, starting transfers between devices, send(): return lax.ppermute(v, axis, [(i, (i + d) % n) for i in range(n)])  57.5 us
    ppermute x43, waiting for transfers between devices, send(): return lax.ppermute(v, axis, [(i, (i + d) % n) for i in range(n)])  45.2 us
    pallas_call x1, Pallas kernels, body(): call(functools.partial(dense_rest, part), dense_out, [ASPEC, SSPEC, SSPEC...  14.2 us
    pallas_call x1, Pallas kernels, body(): call(functools.partial(dense_first, part), dense_out, [ASPEC, SSPEC, SSPE...  10.3 us
    unnamed x21, local copies, waits for them, and re-layouts  5.67 us
    pallas_call x1, Pallas kernels, body(): call(backward_other, [shape((16 * NODE + 32, FEAT), BF16), shape((4, FEAT...  5.63 us
    pallas_call x1, Pallas kernels, body(): call(forward_other, [shape((NODE, FEAT), F32), block, block, block], [SSP...  3.72 us
  transfers between devices with their start and end apart: 43, of which 19 were waited for; matrix products, arithmetic and copies ran while one was open for 1% of the time, Pallas kernels for 20%

profile of v1, /device:TPU:0, one launch (start us, length us, event | category | flops | bytes accessed | tf_op | source)
XLA Modules:
  0.0 155.3 jit_solution(9079923870503534316)
XLA Ops:
  2.3 2.7 %collective-permute-start.1 = (bf16[256,256]{1,0:T(8,128)(2,1)}, bf16[256,256]{1,0:T(8,128)(2,1)S(1)}, u32[]{:S(2)}, u32[]{:S(2)}) collective-permute-start(bf16[256,256]{1,0:T(8,128)(2,1)} %param.7), channel_id=1, source_target_pairs={{0,16},{8,24},{16,0},{24,8},{1,17},{9,25},{17,1},{25,9},{2,18},{10... | collective-permute-start | bytes 393224 | tf_op jit(solution)/shard_map/ppermute | solution.py:228
  6.4 4.0 %collective-permute-start.3 = (bf16[256,256]{1,0:T(8,128)(2,1)}, bf16[256,256]{1,0:T(8,128)(2,1)S(1)}, u32[]{:S(2)}, u32[]{:S(2)}) collective-permute-start(bf16[256,256]{1,0:T(8,128)(2,1)} %param.7), channel_id=1, source_target_pairs={{0,96},{32,0},{64,32},{96,64},{1,97},{33,1},{65,33},{97,65},{2,98}... | collective-permute-start | bytes 393224 | tf_op jit(solution)/shard_map/ppermute | solution.py:228
  12.8 2.6 %collective-permute-start.7 = (bf16[384,256]{1,0:T(8,128)(2,1)S(1)}, bf16[384,256]{1,0:T(8,128)(2,1)S(1)}, u32[]{:S(2)}, u32[]{:S(2)}) collective-permute-start(bf16[384,256]{1,0:T(8,128)(2,1)S(1)} %pad_maximum_fusion), channel_id=1, source_target_pairs={{0,96},{32,0},{64,32},{96,64},{1,97},{33,1},{65,33},{97,65},{2,98}... | collective-permute-start | bytes 589832 | tf_op jit(solution)/shard_map/ppermute | solution.py:228
  24.8 2.8 %collective-permute-done.9 = bf16[384,256]{1,0:T(8,128)(2,1)S(1)} collective-permute-done((bf16[384,256]{1,0:T(8,128)(2,1)S(1)}, bf16[384,256]{1,0:T(8,128)(2,1)S(1)}, u32[]{:S(2)}, u32[]{:S(2)}) %collective-permute-start.9) | collective-permute-done | bytes 196640 | tf_op jit(solution)/shard_map/ppermute | solution.py:228
  27.7 3.6 %collective-permute-done.12 = bf16[384,256]{1,0:T(8,128)(2,1)S(1)} collective-permute-done((bf16[384,256]{1,0:T(8,128)(2,1)S(1)}, bf16[384,256]{1,0:T(8,128)(2,1)S(1)}, u32[]{:S(2)}, u32[]{:S(2)}) %collective-permute-start.12) | collective-permute-done | bytes 196640 | tf_op jit(solution)/shard_map/ppermute | solution.py:228
  32.7 4.6 %copy-done = bf16[1,1,384,128,128]{4,3,2,1,0:T(8,128)(2,1)S(1)} copy-done((bf16[1,1,384,128,128]{4,3,2,1,0:T(8,128)(2,1)S(1)}, bf16[1,1,384,128,128]{4,3,2,1,0:T(8,128)(2,1)}, u32[]{:S(2)}) %copy-start) | copy-done | bytes 12582936
  37.2 10.3 %shard_map.94.given = bf16[64,1024,128]{2,1,0:T(8,128)(2,1)S(1)} custom-call(bf16[384,128,128]{2,1,0:T(8,128)(2,1)S(1)} %bitcast.8, s32[384]{0:T(512)S(1)} %reduce.rows, s32[384]{0:T(512)S(1)} %reduce.1.cols, s32[1]{0:T(128)} %bitcast.6.count), custom_call_target="tpu_custom_call" | custom-call | bytes 12582912 | tf_op jit(solution)/shard_map/pallas_call | solution.py:240
  47.6 14.2 %shard_map.95.dense = bf16[64,1024,128]{2,1,0:T(8,128)(2,1)S(1)} custom-call(bf16[384,128,128]{2,1,0:T(8,128)(2,1)S(1)} %bitcast.9, s32[384]{0:T(512)S(1)} %reduce.rows, s32[384]{0:T(512)S(1)} %reduce.1.cols, s32[1]{0:T(128)} %bitcast.7.count, bf16[64,1024,128]{2,1,0:T(8,128)(2,1)S(1)} %shard_map.94.given), custom_call_target="tpu_custom_call", output_to_operand_aliasing={{}: (4, {})} | custom-call | bytes 25165824 | tf_op jit(solution)/shard_map/pallas_call | solution.py:253
  61.9 2.9 %shard_map.96.given = f32[1024,256]{1,0:T(8,128)S(1)} custom-call(s32[4]{0:T(128)S(1)} %pad_add_fusion.pos, bf16[64,1024,128]{2,1,0:T(8,128)(2,1)S(1)} %shard_map.95.dense, bf16[1792,256]{1,0:T(8,128)(2,1)S(1)} %constant_dynamic-update-slice_fusion.near, bf16[2304,256]{1,0:T(8,128)(2,1)S(1)} %constant_dynamic-update-slice_fusion.7.far), custom_call_target="tpu_custom_call" | custom-call | flops 2147483648 | bytes 8388608 | tf_op jit(solution)/shard_map/pallas_call | solution.py:265
  64.8 3.7 %shard_map.97 = (f32[256,256]{1,0:T(8,128)S(1)}, bf16[256,256]{1,0:T(8,128)(2,1)S(1)}, bf16[256,256]{1,0:T(8,128)(2,1)S(1)}, bf16[256,256]{1,0:T(8,128)(2,1)S(1)}) custom-call(s32[4]{0:T(128)S(1)} %pad_add_fusion.pos, bf16[64,1024,128]{2,1,0:T(8,128)(2,1)S(1)} %shard_map.95.dense, bf16[1792,256]{1,0:T(8,128)(2,1)} %collective-permute-done.6.near, ...), custom_call_target="tpu_custom_call" | custom-call | flops 2147483648 | bytes 8388608 | tf_op jit(solution)/shard_map/pallas_call | solution.py:273
  68.7 3.1 %collective-permute-start.16 = (bf16[256,256]{1,0:T(8,128)(2,1)S(1)}, bf16[256,256]{1,0:T(8,128)(2,1)S(1)}, u32[]{:S(2)}, u32[]{:S(2)}) collective-permute-start(bf16[256,256]{1,0:T(8,128)(2,1)S(1)} %get-tuple-element.36), channel_id=1, source_target_pairs={{0,3},{1,0},{2,1},{3,2},{4,7},{5,4},{6,5},{7,6},{8,11},{9,8},{10,9... | collective-permute-start | bytes 393224 | tf_op jit(solution)/shard_map/ppermute | solution.py:228
  71.8 7.0 %collective-permute-done.14.r1 = bf16[256,256]{1,0:T(8,128)(2,1)S(1)} collective-permute-done((bf16[256,256]{1,0:T(8,128)(2,1)S(1)}, bf16[256,256]{1,0:T(8,128)(2,1)S(1)}, u32[]{:S(2)}, u32[]{:S(2)}) %collective-permute-start.14) | collective-permute-done | bytes 131104 | tf_op jit(solution)/shard_map/ppermute | solution.py:228
  81.9 3.2 %collective-permute-start.18 = (bf16[320,256]{1,0:T(8,128)(2,1)S(1)}, bf16[320,256]{1,0:T(8,128)(2,1)S(1)}, u32[]{:S(2)}, u32[]{:S(2)}) collective-permute-start(bf16[320,256]{1,0:T(8,128)(2,1)S(1)} %get-tuple-element.40), channel_id=1, source_target_pairs={{0,2},{1,3},{2,0},{3,1},{4,6},{5,7},{6,4},{7,5},{8,10},{9,11},{10,... | collective-permute-start | bytes 491528 | tf_op jit(solution)/shard_map/ppermute | solution.py:228
  87.4 2.7 %collective-permute-done.18.r2 = bf16[320,256]{1,0:T(8,128)(2,1)S(1)} collective-permute-done((bf16[320,256]{1,0:T(8,128)(2,1)S(1)}, bf16[320,256]{1,0:T(8,128)(2,1)S(1)}, u32[]{:S(2)}, u32[]{:S(2)}) %collective-permute-start.18) | collective-permute-done | bytes 163872 | tf_op jit(solution)/shard_map/ppermute | solution.py:228
  90.4 5.6 %shard_map.99 = (bf16[4128,256]{1,0:T(8,128)(2,1)S(1)}, bf16[4,256,256]{2,1,0:T(8,128)(2,1)S(1)}, f32[32,256]{1,0:T(8,128)S(1)}) custom-call(s32[4]{0:T(128)S(1)} %pad_add_fusion.pos, bf16[64,1024,128]{2,1,0:T(8,128)(2,1)S(1)} %shard_map.95.dense, bf16[256,256]{1,0:T(8,128)(2,1)S(1)} %get-tuple-element.38.own, ...), custom_call_target="tpu_custom_call" | custom-call | flops 2147483648 | bytes 8388608 | tf_op jit(solution)/shard_map/pallas_call | solution.py:294
  96.3 4.2 %collective-permute-done.20.got = bf16[4128,256]{1,0:T(8,128)(2,1)S(1)} collective-permute-done((bf16[4128,256]{1,0:T(8,128)(2,1)S(1)}, bf16[4128,256]{1,0:T(8,128)(2,1)S(1)}, u32[]{:S(2)}, u32[]{:S(2)}) %collective-permute-start.20) | collective-permute-done | bytes 2113568 | tf_op jit(solution)/shard_map/ppermute | solution.py:228
  100.5 2.9 %shard_map.100 = (f32[512,256]{1,0:T(8,128)S(1)}, f32[512,256]{1,0:T(8,128)S(1)}, bf16[512,256]{1,0:T(8,128)(2,1)S(1)}, bf16[512,256]{1,0:T(8,128)(2,1)S(1)}, bf...) custom-call(s32[4]{0:T(128)S(1)} %pad_add_fusion.pos, ...), custom_call_target="tpu_custom_call" | custom-call | flops 2147483648 | bytes 8388608 | tf_op jit(solution)/shard_map/pallas_call | solution.py:304
  103.4 3.2 %collective-permute-start.21 = (f32[32,256]{1,0:T(8,128)S(1)}, f32[32,256]{1,0:T(8,128)S(1)}, u32[]{:S(2)}, u32[]{:S(2)}) collective-permute-start(f32[32,256]{1,0:T(8,128)S(1)} %get-tuple-element.46.own), channel_id=1, source_target_pairs={{0,8},{8,16},{16,24},{24,0},{1,9},{9,17},{17,25},{25,1},{2,10},{10... | collective-permute-start | bytes 98312 | tf_op jit(solution)/shard_map/ppermute | solution.py:228
  109.4 4.6 %collective-permute-done.21.r1 = f32[32,256]{1,0:T(8,128)S(1)} collective-permute-done((f32[32,256]{1,0:T(8,128)S(1)}, f32[32,256]{1,0:T(8,128)S(1)}, u32[]{:S(2)}, u32[]{:S(2)}) %collective-permute-start.21) | collective-permute-done | bytes 32800 | tf_op jit(solution)/shard_map/ppermute | solution.py:228
  115.3 4.7 %collective-permute-start.25 = (f32[32,256]{1,0:T(8,128)S(1)}, f32[32,256]{1,0:T(8,128)S(1)}, u32[]{:S(2)}, u32[]{:S(2)}) collective-permute-start(f32[32,256]{1,0:T(8,128)S(1)} %shard_map.101.own), channel_id=1, source_target_pairs={{0,64},{32,96},{64,0},{96,32},{1,65},{33,97},{65,1},{97,33},{2,66}... | collective-permute-start | bytes 98312 | tf_op jit(solution)/shard_map/ppermute | solution.py:228
  126.1 3.5 %collective-permute-start.35 = (bf16[512,256]{1,0:T(8,128)(2,1)S(1)}, bf16[512,256]{1,0:T(8,128)(2,1)S(1)}, u32[]{:S(2)}, u32[]{:S(2)}) collective-permute-start(bf16[512,256]{1,0:T(8,128)(2,1)S(1)} %get-tuple-element.53), channel_id=1, source_target_pairs={{0,64},{32,96},{64,0},{96,32},{1,65},{33,97},{65,1},{97,33},{2,66}... | collective-permute-start | bytes 786440 | tf_op jit(solution)/shard_map/ppermute | solution.py:228
  130.2 4.6 %collective-permute-done.32.x2 = bf16[512,256]{1,0:T(8,128)(2,1)S(1)} collective-permute-done((bf16[512,256]{1,0:T(8,128)(2,1)S(1)}, bf16[512,256]{1,0:T(8,128)(2,1)S(1)}, u32[]{:S(2)}, u32[]{:S(2)}) %collective-permute-start.32) | collective-permute-done | bytes 262176 | tf_op jit(solution)/shard_map/ppermute | solution.py:228
  142.3 3.1 %collective-permute-start.38 = (bf16[128,256]{1,0:T(8,128)(2,1)S(1)}, bf16[128,256]{1,0:T(8,128)(2,1)S(1)}, u32[]{:S(2)}, u32[]{:S(2)}) collective-permute-start(bf16[128,256]{1,0:T(8,128)(2,1)S(1)} %get-tuple-element.57), channel_id=1, source_target_pairs={{0,64},{32,96},{64,0},{96,32},{1,65},{33,97},{65,1},{97,33},{2,66}... | collective-permute-start | bytes 196616 | tf_op jit(solution)/shard_map/ppermute | solution.py:228
  147.2 3.1 %collective-permute-start.41 = (bf16[128,256]{1,0:T(8,128)(2,1)S(1)}, bf16[128,256]{1,0:T(8,128)(2,1)S(1)}, u32[]{:S(2)}, u32[]{:S(2)}) collective-permute-start(bf16[128,256]{1,0:T(8,128)(2,1)S(1)} %get-tuple-element.61), channel_id=1, source_target_pairs={{0,16},{8,24},{16,0},{24,8},{1,17},{9,25},{17,1},{25,9},{2,18},{10... | collective-permute-start | bytes 196616 | tf_op jit(solution)/shard_map/ppermute | solution.py:228
  (109 shorter events, 46.7 us)
Async XLA Ops:
  0.6 9.9 %collective-permute-start.2 = (bf16[256,256]{1,0:T(8,128)(2,1)}, bf16[256,256]{1,0:T(8,128)(2,1)S(1)}, u32[]{:S(2)}, u32[]{:S(2)}) collective-permute-start(bf16[256,256]{1,0:T(8,128)(2,1)} %param.7), channel_id=1, source_target_pairs={{0,8},{8,16},{16,24},{24,0},{1,9},{9,17},{17,25},{25,1},{2,10},{10... | collective-permute-start | bytes 393224 | tf_op jit(solution)/shard_map/ppermute | solution.py:228
  2.3 10.4 %collective-permute-start.1 = (bf16[256,256]{1,0:T(8,128)(2,1)}, bf16[256,256]{1,0:T(8,128)(2,1)S(1)}, u32[]{:S(2)}, u32[]{:S(2)}) collective-permute-start(bf16[256,256]{1,0:T(8,128)(2,1)} %param.7), channel_id=1, source_target_pairs={{0,16},{8,24},{16,0},{24,8},{1,17},{9,25},{17,1},{25,9},{2,18},{10... | collective-permute-start | bytes 393224 | tf_op jit(solution)/shard_map/ppermute | solution.py:228
  6.4 13.0 %collective-permute-start.3 = (bf16[256,256]{1,0:T(8,128)(2,1)}, bf16[256,256]{1,0:T(8,128)(2,1)S(1)}, u32[]{:S(2)}, u32[]{:S(2)}) collective-permute-start(bf16[256,256]{1,0:T(8,128)(2,1)} %param.7), channel_id=1, source_target_pairs={{0,96},{32,0},{64,32},{96,64},{1,97},{33,1},{65,33},{97,65},{2,98}... | collective-permute-start | bytes 393224 | tf_op jit(solution)/shard_map/ppermute | solution.py:228
  10.5 9.0 %collective-permute-start.4 = (bf16[256,256]{1,0:T(8,128)(2,1)}, bf16[256,256]{1,0:T(8,128)(2,1)S(1)}, u32[]{:S(2)}, u32[]{:S(2)}) collective-permute-start(bf16[256,256]{1,0:T(8,128)(2,1)} %param.7), channel_id=1, source_target_pairs={{0,64},{32,96},{64,0},{96,32},{1,65},{33,97},{65,1},{97,33},{2,66}... | collective-permute-start | bytes 393224 | tf_op jit(solution)/shard_map/ppermute | solution.py:228
  10.5 8.9 %collective-permute-start.5 = (bf16[256,256]{1,0:T(8,128)(2,1)}, bf16[256,256]{1,0:T(8,128)(2,1)S(1)}, u32[]{:S(2)}, u32[]{:S(2)}) collective-permute-start(bf16[256,256]{1,0:T(8,128)(2,1)} %param.7), channel_id=1, source_target_pairs={{0,32},{32,64},{64,96},{96,0},{1,33},{33,65},{65,97},{97,1},{2,34}... | collective-permute-start | bytes 393224 | tf_op jit(solution)/shard_map/ppermute | solution.py:228
  12.8 11.1 %collective-permute-start.7 = (bf16[384,256]{1,0:T(8,128)(2,1)S(1)}, bf16[384,256]{1,0:T(8,128)(2,1)S(1)}, u32[]{:S(2)}, u32[]{:S(2)}) collective-permute-start(bf16[384,256]{1,0:T(8,128)(2,1)S(1)} %pad_maximum_fusion), channel_id=1, source_target_pairs={{0,96},{32,0},{64,32},{96,64},{1,97},{33,1},{65,33},{97,65},{2,98}... | collective-permute-start | bytes 589832 | tf_op jit(solution)/shard_map/ppermute | solution.py:228
  15.4 9.3 %collective-permute-start.8 = (bf16[384,256]{1,0:T(8,128)(2,1)S(1)}, bf16[384,256]{1,0:T(8,128)(2,1)S(1)}, u32[]{:S(2)}, u32[]{:S(2)}) collective-permute-start(bf16[384,256]{1,0:T(8,128)(2,1)S(1)} %pad_maximum_fusion), channel_id=1, source_target_pairs={{0,64},{32,96},{64,0},{96,32},{1,65},{33,97},{65,1},{97,33},{2,66}... | collective-permute-start | bytes 589832 | tf_op jit(solution)/shard_map/ppermute | solution.py:228
  19.4 8.2 %collective-permute-start.9 = (bf16[384,256]{1,0:T(8,128)(2,1)S(1)}, bf16[384,256]{1,0:T(8,128)(2,1)S(1)}, u32[]{:S(2)}, u32[]{:S(2)}) collective-permute-start(bf16[384,256]{1,0:T(8,128)(2,1)S(1)} %pad_maximum_fusion), channel_id=1, source_target_pairs={{0,32},{32,64},{64,96},{96,0},{1,33},{33,65},{65,97},{97,1},{2,34}... | collective-permute-start | bytes 589832 | tf_op jit(solution)/shard_map/ppermute | solution.py:228
  31.2 33.5 %collective-permute-start.13 = (bf16[2304,256]{1,0:T(8,128)(2,1)S(1)}, bf16[2304,256]{1,0:T(8,128)(2,1)S(1)}, u32[]{:S(2)}, u32[]{:S(2)}) collective-permute-start(bf16[2304,256]{1,0:T(8,128)(2,1)S(1)} %constant_dynamic-update-slice_fusion.7.far), channel_id=1, source_target_pairs={{0,4},{4,0},{1,5},{5,1},{2,6},{6,2},{3,7},{7,3},{8,12},{12,8},{9,1... | collective-permute-start | bytes 3538952 | tf_op jit(solution)/shard_map/ppermute | solution.py:228
  31.4 33.4 %collective-permute-start.6 = (bf16[1792,256]{1,0:T(8,128)(2,1)S(1)}, bf16[1792,256]{1,0:T(8,128)(2,1)}, u32[]{:S(2)}, u32[]{:S(2)}) collective-permute-start(bf16[1792,256]{1,0:T(8,128)(2,1)S(1)} %constant_dynamic-update-slice_fusion.near), channel_id=1, source_target_pairs={{0,4},{4,0},{1,5},{5,1},{2,6},{6,2},{3,7},{7,3},{8,12},{12,8},{9,1... | collective-permute-start | bytes 2752520 | tf_op jit(solution)/shard_map/ppermute | solution.py:228
  68.5 10.4 %collective-permute-start.14 = (bf16[256,256]{1,0:T(8,128)(2,1)S(1)}, bf16[256,256]{1,0:T(8,128)(2,1)S(1)}, u32[]{:S(2)}, u32[]{:S(2)}) collective-permute-start(bf16[256,256]{1,0:T(8,128)(2,1)S(1)} %get-tuple-element.34), channel_id=1, source_target_pairs={{0,1},{1,2},{2,3},{3,0},{4,5},{5,6},{6,7},{7,4},{8,9},{9,10},{10,1... | collective-permute-start | bytes 393224 | tf_op jit(solution)/shard_map/ppermute | solution.py:228
  68.6 10.3 %collective-permute-start.15 = (bf16[256,256]{1,0:T(8,128)(2,1)S(1)}, bf16[256,256]{1,0:T(8,128)(2,1)S(1)}, u32[]{:S(2)}, u32[]{:S(2)}) collective-permute-start(bf16[256,256]{1,0:T(8,128)(2,1)S(1)} %get-tuple-element.35), channel_id=1, source_target_pairs={{0,2},{1,3},{2,0},{3,1},{4,6},{5,7},{6,4},{7,5},{8,10},{9,11},{10,... | collective-permute-start | bytes 393224 | tf_op jit(solution)/shard_map/ppermute | solution.py:228
  68.7 10.7 %collective-permute-start.16 = (bf16[256,256]{1,0:T(8,128)(2,1)S(1)}, bf16[256,256]{1,0:T(8,128)(2,1)S(1)}, u32[]{:S(2)}, u32[]{:S(2)}) collective-permute-start(bf16[256,256]{1,0:T(8,128)(2,1)S(1)} %get-tuple-element.36), channel_id=1, source_target_pairs={{0,3},{1,0},{2,1},{3,2},{4,7},{5,4},{6,5},{7,6},{8,11},{9,8},{10,9... | collective-permute-start | bytes 393224 | tf_op jit(solution)/shard_map/ppermute | solution.py:228
  81.9 8.2 %collective-permute-start.18 = (bf16[320,256]{1,0:T(8,128)(2,1)S(1)}, bf16[320,256]{1,0:T(8,128)(2,1)S(1)}, u32[]{:S(2)}, u32[]{:S(2)}) collective-permute-start(bf16[320,256]{1,0:T(8,128)(2,1)S(1)} %get-tuple-element.40), channel_id=1, source_target_pairs={{0,2},{1,3},{2,0},{3,1},{4,6},{5,7},{6,4},{7,5},{8,10},{9,11},{10,... | collective-permute-start | bytes 491528 | tf_op jit(solution)/shard_map/ppermute | solution.py:228
  103.4 26.3 %collective-permute-start.31 = (bf16[512,256]{1,0:T(8,128)(2,1)S(1)}, bf16[512,256]{1,0:T(8,128)(2,1)S(1)}, u32[]{:S(2)}, u32[]{:S(2)}) collective-permute-start(bf16[512,256]{1,0:T(8,128)(2,1)S(1)} %get-tuple-element.48), channel_id=1, source_target_pairs={{0,8},{8,16},{16,24},{24,0},{1,9},{9,17},{17,25},{25,1},{2,10},{10... | collective-permute-start | bytes 786440 | tf_op jit(solution)/shard_map/ppermute | solution.py:228
  103.4 10.5 %collective-permute-start.21 = (f32[32,256]{1,0:T(8,128)S(1)}, f32[32,256]{1,0:T(8,128)S(1)}, u32[]{:S(2)}, u32[]{:S(2)}) collective-permute-start(f32[32,256]{1,0:T(8,128)S(1)} %get-tuple-element.46.own), channel_id=1, source_target_pairs={{0,8},{8,16},{16,24},{24,0},{1,9},{9,17},{17,25},{25,1},{2,10},{10... | collective-permute-start | bytes 98312 | tf_op jit(solution)/shard_map/ppermute | solution.py:228
  124.6 10.2 %collective-permute-start.32 = (bf16[512,256]{1,0:T(8,128)(2,1)S(1)}, bf16[512,256]{1,0:T(8,128)(2,1)S(1)}, u32[]{:S(2)}, u32[]{:S(2)}) collective-permute-start(bf16[512,256]{1,0:T(8,128)(2,1)S(1)} %get-tuple-element.49), channel_id=1, source_target_pairs={{0,16},{8,24},{16,0},{24,8},{1,17},{9,25},{17,1},{25,9},{2,18},{10... | collective-permute-start | bytes 786440 | tf_op jit(solution)/shard_map/ppermute | solution.py:228
  125.1 12.9 %collective-permute-start.33 = (bf16[512,256]{1,0:T(8,128)(2,1)S(1)}, bf16[512,256]{1,0:T(8,128)(2,1)S(1)}, u32[]{:S(2)}, u32[]{:S(2)}) collective-permute-start(bf16[512,256]{1,0:T(8,128)(2,1)S(1)} %get-tuple-element.50), channel_id=1, source_target_pairs={{0,24},{8,0},{16,8},{24,16},{1,25},{9,1},{17,9},{25,17},{2,26},{10... | collective-permute-start | bytes 786440 | tf_op jit(solution)/shard_map/ppermute | solution.py:228
  125.4 14.7 %collective-permute-start.34 = (bf16[512,256]{1,0:T(8,128)(2,1)S(1)}, bf16[512,256]{1,0:T(8,128)(2,1)S(1)}, u32[]{:S(2)}, u32[]{:S(2)}) collective-permute-start(bf16[512,256]{1,0:T(8,128)(2,1)S(1)} %get-tuple-element.52), channel_id=1, source_target_pairs={{0,32},{32,64},{64,96},{96,0},{1,33},{33,65},{65,97},{97,1},{2,34}... | collective-permute-start | bytes 786440 | tf_op jit(solution)/shard_map/ppermute | solution.py:228
  126.1 15.8 %collective-permute-start.35 = (bf16[512,256]{1,0:T(8,128)(2,1)S(1)}, bf16[512,256]{1,0:T(8,128)(2,1)S(1)}, u32[]{:S(2)}, u32[]{:S(2)}) collective-permute-start(bf16[512,256]{1,0:T(8,128)(2,1)S(1)} %get-tuple-element.53), channel_id=1, source_target_pairs={{0,64},{32,96},{64,0},{96,32},{1,65},{33,97},{65,1},{97,33},{2,66}... | collective-permute-start | bytes 786440 | tf_op jit(solution)/shard_map/ppermute | solution.py:228
  129.6 12.3 %collective-permute-start.36 = (bf16[512,256]{1,0:T(8,128)(2,1)S(1)}, bf16[512,256]{1,0:T(8,128)(2,1)S(1)}, u32[]{:S(2)}, u32[]{:S(2)}) collective-permute-start(bf16[512,256]{1,0:T(8,128)(2,1)S(1)} %get-tuple-element.54), channel_id=1, source_target_pairs={{0,96},{32,0},{64,32},{96,64},{1,97},{33,1},{65,33},{97,65},{2,98}... | collective-permute-start | bytes 786440 | tf_op jit(solution)/shard_map/ppermute | solution.py:228
  134.8 10.5 %collective-permute-start.28 = (f32[64,256]{1,0:T(8,128)S(1)}, f32[64,256]{1,0:T(8,128)S(1)}, u32[]{:S(2)}, u32[]{:S(2)}) collective-permute-start(f32[64,256]{1,0:T(8,128)S(1)} %shard_map.103.own), channel_id=1, source_target_pairs={{0,1},{1,2},{2,3},{3,0},{4,5},{5,6},{6,7},{7,4},{8,9},{9,10},{10,1... | collective-permute-start | bytes 196616 | tf_op jit(solution)/shard_map/ppermute | solution.py:228
  138.0 8.4 %collective-permute-start.29 = (f32[64,256]{1,0:T(8,128)S(1)}, f32[64,256]{1,0:T(8,128)S(1)}, u32[]{:S(2)}, u32[]{:S(2)}) collective-permute-start(f32[64,256]{1,0:T(8,128)S(1)} %shard_map.103.own), channel_id=1, source_target_pairs={{0,2},{1,3},{2,0},{3,1},{4,6},{5,7},{6,4},{7,5},{8,10},{9,11},{10,... | collective-permute-start | bytes 196616 | tf_op jit(solution)/shard_map/ppermute | solution.py:228
  142.3 10.1 %collective-permute-start.38 = (bf16[128,256]{1,0:T(8,128)(2,1)S(1)}, bf16[128,256]{1,0:T(8,128)(2,1)S(1)}, u32[]{:S(2)}, u32[]{:S(2)}) collective-permute-start(bf16[128,256]{1,0:T(8,128)(2,1)S(1)} %get-tuple-element.57), channel_id=1, source_target_pairs={{0,64},{32,96},{64,0},{96,32},{1,65},{33,97},{65,1},{97,33},{2,66}... | collective-permute-start | bytes 196616 | tf_op jit(solution)/shard_map/ppermute | solution.py:228
  (24 other events, 167.2 us)

commit v2 on v0

v2 whole, which is shorter than its diff:
```python
import functools

import jax
import jax.numpy as jnp
from jax import lax
from jax.experimental import pallas as pl
from jax.experimental.pallas import tpu as pltpu
from jax.sharding import Mesh
from jax.sharding import PartitionSpec as P

F32 = jnp.float32
BF16 = jnp.bfloat16
TILE = 128
FEAT = 256
NODE = 256
HALF = 128
ROWS = 1024
NCT = 64
CAP = 384
MIB = 1 << 20
PZ, PX, PC, P1, P2, PY, PY1, PY2, PY3 = range(9)
RING = ("z", "x", "core")


def shape(s, dt):
    return jax.ShapeDtypeStruct(s, dt)


VSPEC = pl.BlockSpec(memory_space=pltpu.VMEM)
SSPEC = pl.BlockSpec(memory_space=pltpu.SMEM)
ASPEC = pl.BlockSpec(memory_space=pl.ANY)


def in_vmem(x):
    return pltpu.with_memory_space_constraint(x, pltpu.VMEM)


def call(kernel, outs, in_specs, scratch=(), flops=0, nbytes=0, limit=16, aliases=None):
    return pl.pallas_call(
        kernel,
        out_shape=outs,
        in_specs=in_specs,
        out_specs=jax.tree.map(lambda _: VSPEC, outs),
        scratch_shapes=list(scratch),
        input_output_aliases=aliases or {},
        cost_estimate=pl.CostEstimate(flops=flops, bytes_accessed=nbytes, transcendentals=0),
        compiler_params=pltpu.CompilerParams(vmem_limit_bytes=limit * MIB),
    )


DENSE = pltpu.VMEM((NCT, ROWS, TILE), BF16)
SIZE = NCT * ROWS * TILE


def dense_call(kernel, outs, dense, pos, *rest, scratch=(), cost=1000):
    n = 2 + len(rest)

    def wrapped(*refs):
        kernel(*refs[:n], *refs[n + 1 :])

    return call(
        wrapped,
        [DENSE] + outs,
        [SSPEC] + [VSPEC] * (n - 1),
        scratch,
        flops=cost,
        nbytes=cost,
        aliases={1: 0},
    )(pos, in_vmem(dense), *rest)


def dense_block(tv, rows, cols, count, dense, done, sem):
    def copy(s):
        return pltpu.make_async_copy(
            tv.at[s],
            dense.at[cols[s], pl.ds(pl.multiple_of(rows[s] * TILE, TILE), TILE), :],
            sem,
        )

    def start(s, _):
        copy(s).start()
        return 0

    def wait(s, _):
        copy(s).wait()
        return 0

    @pl.loop(0, NCT)
    def _(c):
        dense[c] = jnp.zeros((ROWS, TILE), BF16)

    lax.fori_loop(0, count[0], start, 0)
    lax.fori_loop(0, count[0], wait, 0)
    done[...] = jnp.zeros_like(done)


def column_tile(pos, core, e, d):
    z = lax.rem(pos[PZ] + d + core * (e - d), 4)
    x = lax.rem(pos[PX] + e + core * (d - e), 4)
    return 2 * (z * 8 + x * 2 + core)


def forward_own(pos, dense, near, far, done, acc):
    del done
    for d in range(4):
        lhs = []
        for e in range(4):
            c = column_tile(pos, pos[PC], e, d)
            lhs += [dense[c], dense[c + 1]]
        rhs = near[...] if d == 0 else far[(d - 1) * ROWS : d * ROWS]
        term = jnp.dot(jnp.concatenate(lhs, axis=1), rhs, preferred_element_type=F32)
        if d == 0:
            acc[...] = term
        else:
            acc[...] += term


def forward_other(blocks, pos, dense, near, far, given, *outs):
    rows = [pl.ds(pl.multiple_of(pos[b] * NODE, NODE), NODE) for b in blocks]
    total = jnp.concatenate([given[r, :] for r in rows], axis=0)
    for d in range(4):
        lhs = []
        for e in range(4):
            c = column_tile(pos, 1 - pos[PC], e, d)
            lhs += [jnp.concatenate([dense[c + i, r, :] for r in rows], axis=0) for i in range(2)]
        rhs = near[...] if d == 0 else far[(d - 1) * ROWS : d * ROWS]
        total += jnp.dot(jnp.concatenate(lhs, axis=1), rhs, preferred_element_type=F32)
    n = total.shape[0] // len(outs)
    for i, out in enumerate(outs):
        out[...] = total[i * n : (i + 1) * n].astype(out.dtype)


def middle(pos, own, r1, r2, r3, w, cot, act, bt, q, m1, m2, m3, lg):
    agg = (own[...] + r1[...].astype(F32) + r2[...].astype(F32) + r3[...].astype(F32)).astype(BF16)
    pre = jnp.dot(agg, w[...], preferred_element_type=F32)
    sg = jax.nn.sigmoid(pre)
    act[...] = (pre * sg).astype(BF16)
    dz = (cot[...].astype(F32) * sg * (1.0 + pre * (1.0 - sg))).astype(BF16)
    back = lax.dot_general(w[...], dz, (((1,), (1,)), ((), ())), preferred_element_type=F32).astype(
        BF16
    )
    lg[...] = lax.dot_general(agg, dz, (((0,), (0,)), ((), ())), preferred_element_type=F32)
    bt[...] = back
    for p, out in ((PY, q), (PY1, m1), (PY2, m2), (PY3, m3)):
        piece = lg[pl.ds(pl.multiple_of(pos[p] * 64, 64), 64), :]
        if p == PY:
            out[...] = piece
        else:
            out[:NODE] = back
            out[NODE:] = piece.astype(BF16)


FIRST, LAST = (2, 1), (3, 0)


def back_all(bt):
    return jnp.concatenate([bt[0], bt[1], bt[2], bt[3]], axis=1)


def backward_block(dense, lhs, pos, core, e, d):
    c = column_tile(pos, core, e, d)
    rhs = jnp.concatenate([dense[c], dense[c + 1]], axis=1)
    return jnp.dot(lhs, rhs, preferred_element_type=F32)


def two_parts(v):
    hi = v.astype(BF16)
    return hi, (v - hi.astype(F32)).astype(BF16)


def backward_other(distances, dense, lhs, pos, out):
    for k, e in enumerate(distances):
        for d in range(4):
            i = (k * 4 + d) * NODE
            out[i : i + NODE] = backward_block(dense, lhs, pos, 1 - pos[PC], e, d).astype(BF16)


def backward_other_first(pos, dense, own, r1, r2, r3, q, out, bt, qown, qsum):
    core, y = pos[PC], pos[PY]
    bt[y] = own[...]
    total = q[...]
    for d, r in ((1, r1), (2, r2), (3, r3)):
        bt[lax.rem(y + 4 - d, 4)] = r[:NODE]
        total += r[NODE:].astype(F32)
    qsum[...] = total
    qown[...] = qsum[pl.ds(pl.multiple_of(core * 32, 32), 32), :]
    out[8 * NODE :] = qsum[pl.ds(pl.multiple_of((1 - core) * 32, 32), 32), :].astype(BF16)
    backward_other(FIRST, dense, back_all(bt), pos, out)


def backward_other_last(pos, dense, bt, out):
    backward_other(LAST, dense, back_all(bt), pos, out)


def backward_own(distances, dense, lhs, pos, got, outs, hi, lo):
    for k, (e, out) in enumerate(zip(distances, outs, strict=True)):
        for d in range(4):
            i = (k * 4 + d) * NODE
            g = backward_block(dense, lhs, pos, pos[PC], e, d) + got[i : i + NODE].astype(F32)
            out[d * NODE : (d + 1) * NODE] = g.astype(out.dtype)
        if e:
            out[4 * NODE : 4 * NODE + 32] = hi
            out[4 * NODE + 32 :] = lo


def backward_own_first(pos, dense, bt, got, qown, x2, x1, qs):
    hi, lo = two_parts(qown[...] + got[8 * NODE :].astype(F32))
    qs[...] = hi.astype(F32) + lo.astype(F32)
    backward_own(FIRST, dense, back_all(bt), pos, got, (x2, x1), hi, lo)


def backward_own_last(pos, dense, bt, got, qs, x3, x0):
    hi, lo = two_parts(qs[...])
    backward_own(LAST, dense, back_all(bt), pos, got, (x3, x0), hi, lo)


def ring_sum(place, own, received, held):
    held[place] = own
    for d, (hi, lo) in received:
        held[lax.rem(place + 4 - d, 4)] = hi.astype(F32) + lo.astype(F32)
    return (held[0] + held[1]) + (held[2] + held[3])


def weight_parts(received, at):
    return [(d, (r[at : at + 32], r[at + 32 :])) for d, r in enumerate(received, 1)]


def first_sum(pos, x0, r1, r2, r3, qs, t0, t1, t2, t3, qt, held):
    hi, lo = two_parts(ring_sum(pos[P1], qs[...], weight_parts((r1, r2, r3), 4 * NODE), held))
    qt[...] = hi.astype(F32) + lo.astype(F32)
    for d, out in enumerate((t0, t1, t2, t3)):
        at = slice(d * NODE, (d + 1) * NODE)
        s = x0[at]
        for r in (r1, r2, r3):
            s += r[at].astype(F32)
        if d:
            out[:NODE] = s.astype(BF16)
            out[NODE : NODE + 32] = hi
            out[NODE + 32 :] = lo
        else:
            out[...] = s


def weight_sum(pos, r1, r2, r3, qt, qu, held):
    qu[...] = ring_sum(pos[P2], qt[...], weight_parts((r1, r2, r3), NODE), held)


def last_sum(t0, r1, r2, r3, out):
    s = t0[...]
    for r in (r1, r2, r3):
        s += r[:NODE].astype(F32)
    out[...] = s.T.astype(BF16)


def weight_rows(pos, own, r1, r2, r3, out):
    core = pos[PC]
    for p, r in ((PY, own), (PY3, r1), (PY2, r2), (PY1, r3)):
        for c, at in ((core, 0), (1 - core, 32)):
            row = pl.multiple_of(pos[p] * 64 + c * 32, 32)
            out[pl.ds(row, 32), :] = r[at : at + 32] * (1.0 / NODE)


def send(v, axis, d, n=4):
    return lax.ppermute(v, axis, [(i, (i + d) % n) for i in range(n)])


def send_by_core(v, stage, d):
    pairs = []
    for z in range(4):
        for x in range(4):
            for core in range(2):
                if core == stage:
                    to = z, (x + d) % 4
                else:
                    to = (z + d) % 4, x
                pairs.append((z * 8 + x * 2 + core, to[0] * 8 + to[1] * 2 + core))
    return lax.ppermute(v, RING, pairs)


def body(features, cotangent, weight, tile_values, tile_rows, tile_cols, tile_count):
    tv, rows, cols, count = tile_values[0, 0], tile_rows[0, 0], tile_cols[0, 0], tile_count[0]
    z, x, core, y = (lax.axis_index(a) for a in ("z", "x", "core", "y"))
    zero = core == 0
    places = [z, x, core, jnp.where(zero, x, z), jnp.where(zero, z, x)]
    places += [lax.rem(y + d, 4) for d in range(4)]
    pos = jnp.stack(places).astype(jnp.int32)
    tv = pltpu.with_memory_space_constraint(tv, pltpu.HBM)

    near = {d: send_by_core(features, 0, -d) for d in (2, 1, 3)}
    near = jnp.concatenate([features] + [near[d] for d in (1, 2, 3)], axis=0)
    near, count, pos = lax.optimization_barrier((near, count, pos))
    far = {d: send_by_core(near, 1, -d) for d in (2, 1, 3)}
    near_other = send(near, "core", 1, 2)
    dense, done = call(
        dense_block,
        [DENSE, shape((8, 128), F32)],
        [ASPEC, SSPEC, SSPEC, SSPEC],
        [pltpu.SemaphoreType.DMA],
        nbytes=24 * MIB,
    )(tv, rows, cols, count)
    far = jnp.concatenate([far[d] for d in (1, 2, 3)], axis=0)
    far, done = lax.optimization_barrier((far, done))
    far_other = send(far, "core", 1, 2)

    dense, acc = dense_call(forward_own, [shape((ROWS, FEAT), F32)], dense, pos, near, far, done)
    block, blockf = shape((NODE, FEAT), BF16), shape((NODE, FEAT), F32)

    def other_columns(dense, blocks, outs):
        kernel = functools.partial(forward_other, blocks)
        return dense_call(kernel, outs, dense, pos, near_other, far_other, acc)

    dense, s2, s1 = other_columns(dense, (PY2, PY1), [block, block])
    r2, r1 = send(s2, "y", 2), send(s1, "y", 1)
    dense, s3, own = other_columns(dense, (PY3, PY), [block, blockf])
    r3 = send(s3, "y", 3)

    packed = shape((NODE + 64, FEAT), BF16)
    activated, bt, q, m1, m2, m3 = call(
        middle,
        [block, block, shape((64, FEAT), F32), packed, packed, packed],
        [SSPEC] + [VSPEC] * 6,
        [pltpu.VMEM((FEAT, FEAT), F32)],
        flops=6 * FEAT**3,
        nbytes=MIB,
    )(pos, own, r1, r2, r3, weight, cotangent)
    r = {d: send(m, "y", d) for d, m in ((2, m2), (1, m1), (3, m3))}

    piece = shape((32, FEAT), F32)
    dense, other, bt, qown = dense_call(
        backward_other_first,
        [shape((8 * NODE + 32, FEAT), BF16), shape((4, FEAT, NODE), BF16), piece],
        dense, pos, bt, r[1], r[2], r[3], q,
        scratch=[pltpu.VMEM((64, FEAT), F32)],
    )
    got_first = send(other, "core", 1, 2)
    dense, other = dense_call(
        backward_other_last, [shape((8 * NODE, FEAT), BF16)], dense, pos, bt,
    )
    got_last = send(other, "core", 1, 2)
    long = shape((4 * NODE + 64, FEAT), BF16)
    dense, x2, x1, qs = dense_call(
        backward_own_first, [long, long, piece], dense, pos, bt, got_first, qown,
    )
    r = {2: send_by_core(x2, 0, 2), 1: send_by_core(x1, 0, 1)}
    dense, x3, x0 = dense_call(
        backward_own_last,
        [long, shape((4 * NODE, FEAT), F32)],
        dense, pos, bt, got_last, qs,
    )
    r[3] = send_by_core(x3, 0, 3)
    t0, t1, t2, t3, qt = call(
        first_sum,
        [blockf, packed, packed, packed, piece],
        [SSPEC] + [VSPEC] * 5,
        [pltpu.VMEM((4, 32, FEAT), F32)],
        nbytes=4 * MIB,
    )(pos, x0, r[1], r[2], r[3], qs)
    r = {d: send_by_core(v, 1, d) for d, v in ((2, t2), (1, t1), (3, t3))}
    qu = call(
        weight_sum,
        piece,
        [SSPEC] + [VSPEC] * 4,
        [pltpu.VMEM((4, 32, FEAT), F32)],
        nbytes=MIB // 4,
    )(pos, r[1], r[2], r[3], qt)
    pair = jnp.concatenate([qu, send(qu, "core", 1, 2)], axis=0)
    feature_grad = call(last_sum, block, [VSPEC] * 4, nbytes=MIB)(t0, r[1], r[2], r[3])
    r = {d: send(pair, "y", d) for d in (2, 1, 3)}
    weight_grad = call(
        weight_rows, shape((FEAT, FEAT), F32), [SSPEC] + [VSPEC] * 4, nbytes=MIB // 2
    )(pos, pair, r[1], r[2], r[3])
    return activated, weight_grad, feature_grad


def solution(mesh):
    parts = Mesh(mesh.devices.reshape(4, 4, 2, 4), ("z", "x", "core", "y"))
    return jax.shard_map(
        body,
        mesh=parts,
        in_specs=(
            P(("y",) + RING, None),
            P(RING + ("y",), None),
            P(),
            P(RING, "y", None, None, None),
            P(RING, "y", None),
            P(RING, "y", None),
            P(RING, "y"),
        ),
        out_specs=(P(RING + ("y",), None), P(), P(("y",) + RING, None)),
        check_vma=False,
    )
```

time: 541 us -> 111 us (0.21)
  matrix products: 198 us -> 0 us
  local copies, waits for them, and re-layouts: 144 us -> 0.1 us
  waiting for transfers between devices: 147 us -> 47.6 us
  starting transfers between devices: 0.16 us -> 33 us
  Pallas kernels: 0 us -> 26.3 us
  other arithmetic: 20.5 us -> 2.44 us
  blocking collectives: 13 us -> 0 us
  between operations: 13.8 us -> 1.43 us
    dot_general x75 -> x0, matrix products: 198 us -> none  [the longest x24 102 us: step(): jnp.dot(place_table, prod.reshape(-1, tile * feat), preferred_element_typ...]
    while x120 -> x0, local copies, waits for them, and re-layouts: 109 us -> none
    reduce_scatter x2 -> x0, waiting for transfers between devices: 97.1 us -> none  [the longest x1 90.8 us: body(): lax.psum_scatter(transposed, 'row', scatter_dimension=0, tiled=True)]
    all_gather x1 -> x0, waiting for transfers between devices: 49.6 us -> none  [body(): band = lax.all_gather(features, 'row', axis=0, tiled=True)]
    ppermute x0 -> x26, waiting for transfers between devices: none -> 47.6 us  [the longest x12 25.9 us: send_by_core(): return lax.ppermute(v, RING, pairs)]
    ppermute x0 -> x26, starting transfers between devices: none -> 33 us  [the longest x12 19.7 us: send_by_core(): return lax.ppermute(v, RING, pairs)]
    pallas_call x0 -> x13, Pallas kernels: none -> 26.3 us  [the longest x7 13.8 us: dense_call(): call(wrapped, [DENSE] + outs, [SSPEC] + [VSPEC] * (n - 1), scratch, flops...]
    reshape x4 -> x0, local copies, waits for them, and re-layouts: 18.1 us -> none  [the longest x2 10.4 us: block_sum(): return total.reshape(out_blocks * tile, feat)]
  transfers between devices with their start and end apart: 4 -> 26, of which waited for: 3 -> 20; matrix products, arithmetic and copies ran while one was open for 34% -> 1% of each run, Pallas kernels for 0% -> 13%
where the time goes in v2:
time: 111 us
  waiting for transfers between devices  47.6 us (43%)
  starting transfers between devices  33 us (30%)
  Pallas kernels  26.3 us (24%)
  other arithmetic  2.44 us (2%)
  between operations  1.43 us (1%)
    ppermute x12, waiting for transfers between devices, send_by_core(): return lax.ppermute(v, RING, pairs)  25.9 us
    ppermute x14, waiting for transfers between devices, send(): return lax.ppermute(v, axis, [(i, (i + d) % n) for i in range(n)])  21.7 us
    ppermute x12, starting transfers between devices, send_by_core(): return lax.ppermute(v, RING, pairs)  19.7 us
    pallas_call x7, Pallas kernels, dense_call(): call(wrapped, [DENSE] + outs, [SSPEC] + [VSPEC] * (n - 1), scratch, flops...  13.8 us
    ppermute x14, starting transfers between devices, send(): return lax.ppermute(v, axis, [(i, (i + d) % n) for i in range(n)])  13.3 us
    pallas_call x1, Pallas kernels, body(): call(dense_block, [DENSE, shape((8, 128), F32)], [ASPEC, SSPEC, SSPEC, SS...  7.61 us
  transfers between devices with their start and end apart: 26, of which 20 were waited for; matrix products, arithmetic and copies ran while one was open for 1% of the time, Pallas kernels for 13%

profile of v2, /device:TPU:0, one launch (start us, length us, event | category | flops | bytes accessed | tf_op | source)
XLA Modules:
  0.0 110.9 jit_solution(1109780483033671164)
XLA Ops:
  0.6 3.2 %collective-permute-start.1 = (bf16[256,256]{1,0:T(8,128)(2,1)}, bf16[256,256]{1,0:T(8,128)(2,1)S(1)}, u32[]{:S(2)}, u32[]{:S(2)}) collective-permute-start(bf16[256,256]{1,0:T(8,128)(2,1)} %param.7), channel_id=1, source_target_pairs={{0,16},{4,68},{8,24},{12,76},{16,0},{20,84},{24,8},{28,92},{32,48}... | collective-permute-start | bytes 393224 | tf_op jit(solution)/shard_map/ppermute | solution.py:277
  9.0 2.4 %collective-permute-done.2 = bf16[256,256]{1,0:T(8,128)(2,1)S(1)} collective-permute-done((bf16[256,256]{1,0:T(8,128)(2,1)}, bf16[256,256]{1,0:T(8,128)(2,1)S(1)}, u32[]{:S(2)}, u32[]{:S(2)}) %collective-permute-start.2) | collective-permute-done | bytes 131104 | tf_op jit(solution)/shard_map/ppermute | solution.py:277
  12.3 2.0 %collective-permute-start.5 = (bf16[1024,256]{1,0:T(8,128)(2,1)S(1)}, bf16[1024,256]{1,0:T(8,128)(2,1)S(1)}, u32[]{:S(2)}, u32[]{:S(2)}) collective-permute-start(bf16[1024,256]{1,0:T(8,128)(2,1)S(1)} %pad_maximum_fusion.1.refs_2_), channel_id=1, source_target_pairs={{0,32},{4,12},{8,40},{12,20},{16,48},{20,28},{24,56},{28,4},{32,64... | collective-permute-start | bytes 1572872 | tf_op jit(solution)/shard_map/ppermute | solution.py:277
  14.3 3.6 %collective-permute-start.4 = (bf16[1024,256]{1,0:T(8,128)(2,1)S(1)}, bf16[1024,256]{1,0:T(8,128)(2,1)S(1)}, u32[]{:S(2)}, u32[]{:S(2)}) collective-permute-start(bf16[1024,256]{1,0:T(8,128)(2,1)S(1)} %pad_maximum_fusion.1.refs_2_), channel_id=1, source_target_pairs={{0,64},{4,20},{8,72},{12,28},{16,80},{20,4},{24,88},{28,12},{32,96... | collective-permute-start | bytes 1572872 | tf_op jit(solution)/shard_map/ppermute | solution.py:277
  20.9 7.6 %shard_map.94 = (bf16[64,1024,128]{2,1,0:T(8,128)(2,1)S(1)}, f32[8,128]{1,0:T(8,128)S(1)}) custom-call(bf16[384,128,128]{2,1,0:T(8,128)(2,1)} %bitcast.12, s32[384]{0:T(512)S(1)} %reduce.rows, s32[384]{0:T(512)S(1)} %reduce.1.cols, s32[1]{0:T(128)} %bitcast.11.count), custom_call_target="tpu_custom_call" | custom-call | bytes 25165824 | tf_op jit(solution)/shard_map/pallas_call | solution.py:294
  28.5 2.1 %collective-permute-done.4 = bf16[1024,256]{1,0:T(8,128)(2,1)S(1)} collective-permute-done((bf16[1024,256]{1,0:T(8,128)(2,1)S(1)}, bf16[1024,256]{1,0:T(8,128)(2,1)S(1)}, u32[]{:S(2)}, u32[]{:S(2)}) %collective-permute-start.4) | collective-permute-done | bytes 524320 | tf_op jit(solution)/shard_map/ppermute | solution.py:277
  31.3 2.9 %shard_map.95 = (bf16[64,1024,128]{2,1,0:T(8,128)(2,1)S(1)}, f32[1024,256]{1,0:T(8,128)S(1)}) custom-call(s32[9]{0:T(128)S(1)} %stack.39.refs_0_.pos, bf16[64,1024,128]{2,1,0:T(8,128)(2,1)S(1)} %get-tuple-element.43.refs_1_, bf16[1024,256]{1,0:T(8,128)(2,1)S(1)} %pad_maximum_fusion.1.refs_2_, ...), custom_call_target="tpu_custom_call", output_to_operand_aliasing={{0}: (1, {})} | custom-call | flops 1000 | bytes 1000 | tf_op jit(solution)/shard_map/pallas_call | solution.py:61
  35.0 1.8 %shard_map.96 = (bf16[64,1024,128]{2,1,0:T(8,128)(2,1)S(1)}, bf16[256,256]{1,0:T(8,128)(2,1)S(1)}, bf16[256,256]{1,0:T(8,128)(2,1)S(1)}) custom-call(s32[9]{0:T(128)S(1)} %stack.39.refs_0_.pos, bf16[64,1024,128]{2,1,0:T(8,128)(2,1)S(1)} %get-tuple-element.48.refs_1_, ...), custom_call_target="tpu_custom_call", output_to_operand_aliasing={{0}: (1, {})} | custom-call | flops 1000 | bytes 1000 | tf_op jit(solution)/shard_map/pallas_call | solution.py:61
  36.8 1.8 %shard_map.97 = (bf16[64,1024,128]{2,1,0:T(8,128)(2,1)S(1)}, bf16[256,256]{1,0:T(8,128)(2,1)S(1)}, f32[256,256]{1,0:T(8,128)S(1)}) custom-call(s32[9]{0:T(128)S(1)} %stack.39.refs_0_.pos, bf16[64,1024,128]{2,1,0:T(8,128)(2,1)S(1)} %get-tuple-element.50.refs_1_, ...), custom_call_target="tpu_custom_call", output_to_operand_aliasing={{0}: (1, {})} | custom-call | flops 1000 | bytes 1000 | tf_op jit(solution)/shard_map/pallas_call | solution.py:61
  38.6 3.1 %collective-permute-start.10 = (bf16[256,256]{1,0:T(8,128)(2,1)S(1)}, bf16[256,256]{1,0:T(8,128)(2,1)S(1)}, u32[]{:S(2)}, u32[]{:S(2)}) collective-permute-start(bf16[256,256]{1,0:T(8,128)(2,1)S(1)} %get-tuple-element.54), channel_id=1, source_target_pairs={{0,3},{1,0},{2,1},{3,2},{4,7},{5,4},{6,5},{7,6},{8,11},{9,8},{10,9... | collective-permute-start | bytes 393224 | tf_op jit(solution)/shard_map/ppermute | solution.py:264
  41.7 2.2 %collective-permute-start.9 = (bf16[256,256]{1,0:T(8,128)(2,1)S(1)}, bf16[256,256]{1,0:T(8,128)(2,1)S(1)}, u32[]{:S(2)}, u32[]{:S(2)}) collective-permute-start(bf16[256,256]{1,0:T(8,128)(2,1)S(1)} %get-tuple-element.53), channel_id=1, source_target_pairs={{0,2},{1,3},{2,0},{3,1},{4,6},{5,7},{6,4},{7,5},{8,10},{9,11},{10,... | collective-permute-start | bytes 393224 | tf_op jit(solution)/shard_map/ppermute | solution.py:264
  44.7 6.2 %collective-permute-done.8.r1 = bf16[256,256]{1,0:T(8,128)(2,1)S(1)} collective-permute-done((bf16[256,256]{1,0:T(8,128)(2,1)S(1)}, bf16[256,256]{1,0:T(8,128)(2,1)S(1)}, u32[]{:S(2)}, u32[]{:S(2)}) %collective-permute-start.8) | collective-permute-done | bytes 131104 | tf_op jit(solution)/shard_map/ppermute | solution.py:264
  52.4 1.9 %collective-permute-start.12 = (bf16[320,256]{1,0:T(8,128)(2,1)S(1)}, bf16[320,256]{1,0:T(8,128)(2,1)S(1)}, u32[]{:S(2)}, u32[]{:S(2)}) collective-permute-start(bf16[320,256]{1,0:T(8,128)(2,1)S(1)} %get-tuple-element.59), channel_id=1, source_target_pairs={{0,2},{1,3},{2,0},{3,1},{4,6},{5,7},{6,4},{7,5},{8,10},{9,11},{10,... | collective-permute-start | bytes 491528 | tf_op jit(solution)/shard_map/ppermute | solution.py:264
  55.7 6.8 %collective-permute-done.11.refs_3_ = bf16[320,256]{1,0:T(8,128)(2,1)S(1)} collective-permute-done((bf16[320,256]{1,0:T(8,128)(2,1)S(1)}, bf16[320,256]{1,0:T(8,128)(2,1)S(1)}, u32[]{:S(2)}, u32[]{:S(2)}) %collective-permute-start.11) | collective-permute-done | bytes 163872 | tf_op jit(solution)/shard_map/ppermute | solution.py:264
  63.1 1.8 %shard_map.99 = (bf16[64,1024,128]{2,1,0:T(8,128)(2,1)S(1)}, bf16[2080,256]{1,0:T(8,128)(2,1)S(1)}, bf16[4,256,256]{2,1,0:T(8,128)(2,1)S(1)}, f32[32,256]{1,0:T(8,128)S(1)}) custom-call(s32[9]{0:T(128)S(1)} %stack.39.refs_0_.pos, bf16[64,1024,128]{2,1,0:T(8,128)(2,1)S(1)} %get-tuple-element.56.refs_1_, ...), custom_call_target="tpu_custom_call", output_to_operand_aliasing={{0}: (1, {})} | custom-call | flops 1000 | bytes 1000 | tf_op jit(solution)/shard_map/pallas_call | solution.py:61
  65.0 1.8 %shard_map.100 = (bf16[64,1024,128]{2,1,0:T(8,128)(2,1)S(1)}, bf16[2048,256]{1,0:T(8,128)(2,1)S(1)}) custom-call(s32[9]{0:T(128)S(1)} %stack.39.refs_0_.pos, bf16[64,1024,128]{2,1,0:T(8,128)(2,1)S(1)} %get-tuple-element.62.refs_1_, bf16[4,256,256]{2,1,0:T(8,128)(2,1)S(1)} %get-tuple-element.63.refs_2_), custom_call_target="tpu_custom_call", output_to_operand_aliasing={{0}: (1, {})} | custom-call | flops 1000 | bytes 1000 | tf_op jit(solution)/shard_map/pallas_call | solution.py:61
  67.7 1.8 %shard_map.101 = (bf16[64,1024,128]{2,1,0:T(8,128)(2,1)S(1)}, bf16[1088,256]{1,0:T(8,128)(2,1)S(1)}, bf16[1088,256]{1,0:T(8,128)(2,1)S(1)}, f32[32,256]{1,0:T(8,128)S(1)}) custom-call(s32[9]{0:T(128)S(1)} %stack.39.refs_0_.pos, bf16[64,1024,128]{2,1,0:T(8,128)(2,1)S(1)} %get-tuple-element.64.refs_1_, ...), custom_call_target="tpu_custom_call", output_to_operand_aliasing={{0}: (1, {})} | custom-call | flops 1000 | bytes 1000 | tf_op jit(solution)/shard_map/pallas_call | solution.py:61
  69.9 1.8 %shard_map.102 = (bf16[64,1024,128]{2,1,0:T(8,128)(2,1)S(1)}, bf16[1088,256]{1,0:T(8,128)(2,1)S(1)}, f32[1024,256]{1,0:T(8,128)S(1)}) custom-call(s32[9]{0:T(128)S(1)} %stack.39.refs_0_.pos, bf16[64,1024,128]{2,1,0:T(8,128)(2,1)S(1)} %get-tuple-element.67.refs_1_, ...), custom_call_target="tpu_custom_call", output_to_operand_aliasing={{0}: (1, {})} | custom-call | flops 1000 | bytes 1000 | tf_op jit(solution)/shard_map/pallas_call | solution.py:61
  74.4 6.9 %collective-permute-done.18.r3 = bf16[1088,256]{1,0:T(8,128)(2,1)S(1)} collective-permute-done((bf16[1088,256]{1,0:T(8,128)(2,1)S(1)}, bf16[1088,256]{1,0:T(8,128)(2,1)S(1)}, u32[]{:S(2)}, u32[]{:S(2)}) %collective-permute-start.18) | collective-permute-done | bytes 557088 | tf_op jit(solution)/shard_map/ppermute | solution.py:277
  81.3 7.5 %collective-permute-done.16.r1 = bf16[1088,256]{1,0:T(8,128)(2,1)S(1)} collective-permute-done((bf16[1088,256]{1,0:T(8,128)(2,1)S(1)}, bf16[1088,256]{1,0:T(8,128)(2,1)S(1)}, u32[]{:S(2)}, u32[]{:S(2)}) %collective-permute-start.16) | collective-permute-done | bytes 557088 | tf_op jit(solution)/shard_map/ppermute | solution.py:277
  91.3 2.1 %collective-permute-start.20 = (bf16[320,256]{1,0:T(8,128)(2,1)S(1)}, bf16[320,256]{1,0:T(8,128)(2,1)S(1)}, u32[]{:S(2)}, u32[]{:S(2)}) collective-permute-start(bf16[320,256]{1,0:T(8,128)(2,1)S(1)} %get-tuple-element.75), channel_id=1, source_target_pairs={{0,64},{4,20},{8,72},{12,28},{16,80},{20,4},{24,88},{28,12},{32,96... | collective-permute-start | bytes 491528 | tf_op jit(solution)/shard_map/ppermute | solution.py:277
  96.3 2.1 %collective-permute-done.20.r2 = bf16[320,256]{1,0:T(8,128)(2,1)S(1)} collective-permute-done((bf16[320,256]{1,0:T(8,128)(2,1)S(1)}, bf16[320,256]{1,0:T(8,128)(2,1)S(1)}, u32[]{:S(2)}, u32[]{:S(2)}) %collective-permute-start.20) | collective-permute-done | bytes 163872 | tf_op jit(solution)/shard_map/ppermute | solution.py:277
  100.8 2.3 %collective-permute-start.25 = (f32[64,256]{1,0:T(8,128)S(1)}, f32[64,256]{1,0:T(8,128)S(1)}, u32[]{:S(2)}, u32[]{:S(2)}) collective-permute-start(f32[64,256]{1,0:T(8,128)S(1)} %pad_maximum_fusion.2.own), channel_id=1, source_target_pairs={{0,3},{1,0},{2,1},{3,2},{4,7},{5,4},{6,5},{7,6},{8,11},{9,8},{10,9... | collective-permute-start | bytes 196616 | tf_op jit(solution)/shard_map/ppermute | solution.py:264
  106.2 3.0 %collective-permute-done.24.r2 = f32[64,256]{1,0:T(8,128)S(1)} collective-permute-done((f32[64,256]{1,0:T(8,128)S(1)}, f32[64,256]{1,0:T(8,128)S(1)}, u32[]{:S(2)}, u32[]{:S(2)}) %collective-permute-start.24) | collective-permute-done | bytes 65568 | tf_op jit(solution)/shard_map/ppermute | solution.py:264
  (51 shorter events, 30.6 us)
Async XLA Ops:
  0.6 6.8 %collective-permute-start.1 = (bf16[256,256]{1,0:T(8,128)(2,1)}, bf16[256,256]{1,0:T(8,128)(2,1)S(1)}, u32[]{:S(2)}, u32[]{:S(2)}) collective-permute-start(bf16[256,256]{1,0:T(8,128)(2,1)} %param.7), channel_id=1, source_target_pairs={{0,16},{4,68},{8,24},{12,76},{16,0},{20,84},{24,8},{28,92},{32,48}... | collective-permute-start | bytes 393224 | tf_op jit(solution)/shard_map/ppermute | solution.py:277
  3.8 5.2 %collective-permute-start = (bf16[256,256]{1,0:T(8,128)(2,1)}, bf16[256,256]{1,0:T(8,128)(2,1)S(1)}, u32[]{:S(2)}, u32[]{:S(2)}) collective-permute-start(bf16[256,256]{1,0:T(8,128)(2,1)} %param.7), channel_id=1, source_target_pairs={{0,24},{4,100},{8,0},{12,108},{16,8},{20,116},{24,16},{28,124},{32... | collective-permute-start | bytes 393224 | tf_op jit(solution)/shard_map/ppermute | solution.py:277
  5.0 6.4 %collective-permute-start.2 = (bf16[256,256]{1,0:T(8,128)(2,1)}, bf16[256,256]{1,0:T(8,128)(2,1)S(1)}, u32[]{:S(2)}, u32[]{:S(2)}) collective-permute-start(bf16[256,256]{1,0:T(8,128)(2,1)} %param.7), channel_id=1, source_target_pairs={{0,8},{4,36},{8,16},{12,44},{16,24},{20,52},{24,0},{28,60},{32,40}... | collective-permute-start | bytes 393224 | tf_op jit(solution)/shard_map/ppermute | solution.py:277
  12.3 16.3 %collective-permute-start.5 = (bf16[1024,256]{1,0:T(8,128)(2,1)S(1)}, bf16[1024,256]{1,0:T(8,128)(2,1)S(1)}, u32[]{:S(2)}, u32[]{:S(2)}) collective-permute-start(bf16[1024,256]{1,0:T(8,128)(2,1)S(1)} %pad_maximum_fusion.1.refs_2_), channel_id=1, source_target_pairs={{0,32},{4,12},{8,40},{12,20},{16,48},{20,28},{24,56},{28,4},{32,64... | collective-permute-start | bytes 1572872 | tf_op jit(solution)/shard_map/ppermute | solution.py:277
  14.3 16.4 %collective-permute-start.4 = (bf16[1024,256]{1,0:T(8,128)(2,1)S(1)}, bf16[1024,256]{1,0:T(8,128)(2,1)S(1)}, u32[]{:S(2)}, u32[]{:S(2)}) collective-permute-start(bf16[1024,256]{1,0:T(8,128)(2,1)S(1)} %pad_maximum_fusion.1.refs_2_), channel_id=1, source_target_pairs={{0,64},{4,20},{8,72},{12,28},{16,80},{20,4},{24,88},{28,12},{32,96... | collective-permute-start | bytes 1572872 | tf_op jit(solution)/shard_map/ppermute | solution.py:277
  17.9 12.8 %collective-permute-start.3 = (bf16[1024,256]{1,0:T(8,128)(2,1)S(1)}, bf16[1024,256]{1,0:T(8,128)(2,1)S(1)}, u32[]{:S(2)}, u32[]{:S(2)}) collective-permute-start(bf16[1024,256]{1,0:T(8,128)(2,1)S(1)} %pad_maximum_fusion.1.refs_2_), channel_id=1, source_target_pairs={{0,96},{4,28},{8,104},{12,4},{16,112},{20,12},{24,120},{28,20},{32... | collective-permute-start | bytes 1572872 | tf_op jit(solution)/shard_map/ppermute | solution.py:277
  30.7 4.2 %collective-permute-start.7 = (bf16[3072,256]{1,0:T(8,128)(2,1)S(1)}, bf16[3072,256]{1,0:T(8,128)(2,1)S(1)}, u32[]{:S(2)}, u32[]{:S(2)}) collective-permute-start(bf16[3072,256]{1,0:T(8,128)(2,1)S(1)} %pad_maximum_fusion.refs_3_), channel_id=1, source_target_pairs={{0,4},{4,0},{1,5},{5,1},{2,6},{6,2},{3,7},{7,3},{8,12},{12,8},{9,1... | collective-permute-start | bytes 4718600 | tf_op jit(solution)/shard_map/ppermute | solution.py:264
  30.8 4.1 %collective-permute-start.6 = (bf16[1024,256]{1,0:T(8,128)(2,1)S(1)}, bf16[1024,256]{1,0:T(8,128)(2,1)S(1)}, u32[]{:S(2)}, u32[]{:S(2)}) collective-permute-start(bf16[1024,256]{1,0:T(8,128)(2,1)S(1)} %pad_maximum_fusion.1.refs_2_), channel_id=1, source_target_pairs={{0,4},{4,0},{1,5},{5,1},{2,6},{6,2},{3,7},{7,3},{8,12},{12,8},{9,1... | collective-permute-start | bytes 1572872 | tf_op jit(solution)/shard_map/ppermute | solution.py:264
  38.6 6.1 %collective-permute-start.10 = (bf16[256,256]{1,0:T(8,128)(2,1)S(1)}, bf16[256,256]{1,0:T(8,128)(2,1)S(1)}, u32[]{:S(2)}, u32[]{:S(2)}) collective-permute-start(bf16[256,256]{1,0:T(8,128)(2,1)S(1)} %get-tuple-element.54), channel_id=1, source_target_pairs={{0,3},{1,0},{2,1},{3,2},{4,7},{5,4},{6,5},{7,6},{8,11},{9,8},{10,9... | collective-permute-start | bytes 393224 | tf_op jit(solution)/shard_map/ppermute | solution.py:264
  41.7 9.3 %collective-permute-start.8 = (bf16[256,256]{1,0:T(8,128)(2,1)S(1)}, bf16[256,256]{1,0:T(8,128)(2,1)S(1)}, u32[]{:S(2)}, u32[]{:S(2)}) collective-permute-start(bf16[256,256]{1,0:T(8,128)(2,1)S(1)} %get-tuple-element.52), channel_id=1, source_target_pairs={{0,1},{1,2},{2,3},{3,0},{4,5},{5,6},{6,7},{7,4},{8,9},{9,10},{10,1... | collective-permute-start | bytes 393224 | tf_op jit(solution)/shard_map/ppermute | solution.py:264
  41.7 9.3 %collective-permute-start.9 = (bf16[256,256]{1,0:T(8,128)(2,1)S(1)}, bf16[256,256]{1,0:T(8,128)(2,1)S(1)}, u32[]{:S(2)}, u32[]{:S(2)}) collective-permute-start(bf16[256,256]{1,0:T(8,128)(2,1)S(1)} %get-tuple-element.53), channel_id=1, source_target_pairs={{0,2},{1,3},{2,0},{3,1},{4,6},{5,7},{6,4},{7,5},{8,10},{9,11},{10,... | collective-permute-start | bytes 393224 | tf_op jit(solution)/shard_map/ppermute | solution.py:264
  52.4 10.0 %collective-permute-start.11 = (bf16[320,256]{1,0:T(8,128)(2,1)S(1)}, bf16[320,256]{1,0:T(8,128)(2,1)S(1)}, u32[]{:S(2)}, u32[]{:S(2)}) collective-permute-start(bf16[320,256]{1,0:T(8,128)(2,1)S(1)} %get-tuple-element.58), channel_id=1, source_target_pairs={{0,1},{1,2},{2,3},{3,0},{4,5},{5,6},{6,7},{7,4},{8,9},{9,10},{10,1... | collective-permute-start | bytes 491528 | tf_op jit(solution)/shard_map/ppermute | solution.py:264
  52.4 10.0 %collective-permute-start.12 = (bf16[320,256]{1,0:T(8,128)(2,1)S(1)}, bf16[320,256]{1,0:T(8,128)(2,1)S(1)}, u32[]{:S(2)}, u32[]{:S(2)}) collective-permute-start(bf16[320,256]{1,0:T(8,128)(2,1)S(1)} %get-tuple-element.59), channel_id=1, source_target_pairs={{0,2},{1,3},{2,0},{3,1},{4,6},{5,7},{6,4},{7,5},{8,10},{9,11},{10,... | collective-permute-start | bytes 491528 | tf_op jit(solution)/shard_map/ppermute | solution.py:264
  54.3 8.8 %collective-permute-start.13 = (bf16[320,256]{1,0:T(8,128)(2,1)S(1)}, bf16[320,256]{1,0:T(8,128)(2,1)S(1)}, u32[]{:S(2)}, u32[]{:S(2)}) collective-permute-start(bf16[320,256]{1,0:T(8,128)(2,1)S(1)} %get-tuple-element.60), channel_id=1, source_target_pairs={{0,3},{1,0},{2,1},{3,2},{4,7},{5,4},{6,5},{7,6},{8,11},{9,8},{10,9... | collective-permute-start | bytes 491528 | tf_op jit(solution)/shard_map/ppermute | solution.py:264
  66.8 3.0 %collective-permute-start.15 = (bf16[2048,256]{1,0:T(8,128)(2,1)S(1)}, bf16[2048,256]{1,0:T(8,128)(2,1)S(1)}, u32[]{:S(2)}, u32[]{:S(2)}) collective-permute-start(bf16[2048,256]{1,0:T(8,128)(2,1)S(1)} %get-tuple-element.68), channel_id=1, source_target_pairs={{0,4},{4,0},{1,5},{5,1},{2,6},{6,2},{3,7},{7,3},{8,12},{12,8},{9,1... | collective-permute-start | bytes 3145736 | tf_op jit(solution)/shard_map/ppermute | solution.py:264
  71.7 9.6 %collective-permute-start.18 = (bf16[1088,256]{1,0:T(8,128)(2,1)S(1)}, bf16[1088,256]{1,0:T(8,128)(2,1)S(1)}, u32[]{:S(2)}, u32[]{:S(2)}) collective-permute-start(bf16[1088,256]{1,0:T(8,128)(2,1)S(1)} %get-tuple-element.73), channel_id=1, source_target_pairs={{0,24},{4,100},{8,0},{12,108},{16,8},{20,116},{24,16},{28,124},{32... | collective-permute-start | bytes 1671176 | tf_op jit(solution)/shard_map/ppermute | solution.py:277
  72.1 16.7 %collective-permute-start.16 = (bf16[1088,256]{1,0:T(8,128)(2,1)S(1)}, bf16[1088,256]{1,0:T(8,128)(2,1)S(1)}, u32[]{:S(2)}, u32[]{:S(2)}) collective-permute-start(bf16[1088,256]{1,0:T(8,128)(2,1)S(1)} %get-tuple-element.71), channel_id=1, source_target_pairs={{0,8},{4,36},{8,16},{12,44},{16,24},{20,52},{24,0},{28,60},{32,40}... | collective-permute-start | bytes 1671176 | tf_op jit(solution)/shard_map/ppermute | solution.py:277
  73.8 15.0 %collective-permute-start.17 = (bf16[1088,256]{1,0:T(8,128)(2,1)S(1)}, bf16[1088,256]{1,0:T(8,128)(2,1)S(1)}, u32[]{:S(2)}, u32[]{:S(2)}) collective-permute-start(bf16[1088,256]{1,0:T(8,128)(2,1)S(1)} %get-tuple-element.72), channel_id=1, source_target_pairs={{0,16},{4,68},{8,24},{12,76},{16,0},{20,84},{24,8},{28,92},{32,48}... | collective-permute-start | bytes 1671176 | tf_op jit(solution)/shard_map/ppermute | solution.py:277
  89.7 6.6 %collective-permute-start.19 = (bf16[320,256]{1,0:T(8,128)(2,1)S(1)}, bf16[320,256]{1,0:T(8,128)(2,1)S(1)}, u32[]{:S(2)}, u32[]{:S(2)}) collective-permute-start(bf16[320,256]{1,0:T(8,128)(2,1)S(1)} %get-tuple-element.74), channel_id=1, source_target_pairs={{0,32},{4,12},{8,40},{12,20},{16,48},{20,28},{24,56},{28,4},{32,64... | collective-permute-start | bytes 491528 | tf_op jit(solution)/shard_map/ppermute | solution.py:277
  91.3 7.1 %collective-permute-start.20 = (bf16[320,256]{1,0:T(8,128)(2,1)S(1)}, bf16[320,256]{1,0:T(8,128)(2,1)S(1)}, u32[]{:S(2)}, u32[]{:S(2)}) collective-permute-start(bf16[320,256]{1,0:T(8,128)(2,1)S(1)} %get-tuple-element.75), channel_id=1, source_target_pairs={{0,64},{4,20},{8,72},{12,28},{16,80},{20,4},{24,88},{28,12},{32,96... | collective-permute-start | bytes 491528 | tf_op jit(solution)/shard_map/ppermute | solution.py:277
  93.4 5.5 %collective-permute-start.21 = (bf16[320,256]{1,0:T(8,128)(2,1)S(1)}, bf16[320,256]{1,0:T(8,128)(2,1)S(1)}, u32[]{:S(2)}, u32[]{:S(2)}) collective-permute-start(bf16[320,256]{1,0:T(8,128)(2,1)S(1)} %get-tuple-element.76), channel_id=1, source_target_pairs={{0,96},{4,28},{8,104},{12,4},{16,112},{20,12},{24,120},{28,20},{32... | collective-permute-start | bytes 491528 | tf_op jit(solution)/shard_map/ppermute | solution.py:277
  100.8 5.5 %collective-permute-start.25 = (f32[64,256]{1,0:T(8,128)S(1)}, f32[64,256]{1,0:T(8,128)S(1)}, u32[]{:S(2)}, u32[]{:S(2)}) collective-permute-start(f32[64,256]{1,0:T(8,128)S(1)} %pad_maximum_fusion.2.own), channel_id=1, source_target_pairs={{0,3},{1,0},{2,1},{3,2},{4,7},{5,4},{6,5},{7,6},{8,11},{9,8},{10,9... | collective-permute-start | bytes 196616 | tf_op jit(solution)/shard_map/ppermute | solution.py:264
  103.1 6.1 %collective-permute-start.24 = (f32[64,256]{1,0:T(8,128)S(1)}, f32[64,256]{1,0:T(8,128)S(1)}, u32[]{:S(2)}, u32[]{:S(2)}) collective-permute-start(f32[64,256]{1,0:T(8,128)S(1)} %pad_maximum_fusion.2.own), channel_id=1, source_target_pairs={{0,2},{1,3},{2,0},{3,1},{4,6},{5,7},{6,4},{7,5},{8,10},{9,11},{10,... | collective-permute-start | bytes 196616 | tf_op jit(solution)/shard_map/ppermute | solution.py:264
  103.1 6.5 %collective-permute-start.23 = (f32[64,256]{1,0:T(8,128)S(1)}, f32[64,256]{1,0:T(8,128)S(1)}, u32[]{:S(2)}, u32[]{:S(2)}) collective-permute-start(f32[64,256]{1,0:T(8,128)S(1)} %pad_maximum_fusion.2.own), channel_id=1, source_target_pairs={{0,1},{1,2},{2,3},{3,0},{4,5},{5,6},{6,7},{7,4},{8,9},{9,10},{10,1... | collective-permute-start | bytes 196616 | tf_op jit(solution)/shard_map/ppermute | solution.py:264
  (4 other events, 32.4 us)

commit v3 on v2

--- a/solution.py
+++ b/solution.py
@@ -18,7 +18,7 @@
 NCT = 64
 CAP = 384
 MIB = 1 << 20
-PZ, PX, PC, P1, P2, PY, PY1, PY2, PY3 = range(9)
+PZ, PX, PC, P1, P2, PY, PY1, PY2, PY3, PX1, PX3 = range(11)
 RING = ("z", "x", "core")
 
 
@@ -69,7 +69,7 @@
     )(pos, in_vmem(dense), *rest)
 
 
-def dense_block(tv, rows, cols, count, dense, done, sem):
+def dense_block(tv, rows, cols, count, dense, sem):
     def copy(s):
         return pltpu.make_async_copy(
             tv.at[s],
@@ -91,7 +91,6 @@
 
     lax.fori_loop(0, count[0], start, 0)
     lax.fori_loop(0, count[0], wait, 0)
-    done[...] = jnp.zeros_like(done)
 
 
 def column_tile(pos, core, e, d):
@@ -100,38 +99,51 @@
     return 2 * (z * 8 + x * 2 + core)
 
 
-def forward_own(pos, dense, near, far, done, acc):
-    del done
-    for d in range(4):
-        lhs = []
-        for e in range(4):
-            c = column_tile(pos, pos[PC], e, d)
-            lhs += [dense[c], dense[c + 1]]
-        rhs = near[...] if d == 0 else far[(d - 1) * ROWS : d * ROWS]
-        term = jnp.dot(jnp.concatenate(lhs, axis=1), rhs, preferred_element_type=F32)
-        if d == 0:
-            acc[...] = term
-        else:
-            acc[...] += term
-
-
-def forward_other(blocks, pos, dense, near, far, given, *outs):
+def tiles_of(dense, pos, core, d, rows):
+    tiles = []
+    for e in range(4):
+        c = column_tile(pos, core, e, d)
+        tiles += [jnp.concatenate([dense[c + i, r, :] for r in rows], axis=0) for i in range(2)]
+    return jnp.concatenate(tiles, axis=1)
+
+
+WHOLE = (slice(None),)
+
+
+def forward_near(pos, dense, near, near_other, acc):
+    core = pos[PC]
+    acc[...] = jnp.dot(
+        tiles_of(dense, pos, core, 0, WHOLE), near[...], preferred_element_type=F32
+    ) + jnp.dot(
+        tiles_of(dense, pos, 1 - core, 0, WHOLE), near_other[...], preferred_element_type=F32
+    )
+
+
+def far_sum(total, dense, pos, core, far, rows):
+    for d in range(1, 4):
+        rhs = far[(d - 1) * ROWS : d * ROWS]
+        total += jnp.dot(tiles_of(dense, pos, core, d, rows), rhs, preferred_element_type=F32)
+    return total
+
+
+def forward_own(pos, dense, far, given, acc):
+    acc[...] = far_sum(given[...], dense, pos, pos[PC], far, WHOLE)
+
+
+def forward_other(blocks, pos, dense, far, given, *outs):
     rows = [pl.ds(pl.multiple_of(pos[b] * NODE, NODE), NODE) for b in blocks]
     total = jnp.concatenate([given[r, :] for r in rows], axis=0)
-    for d in range(4):
-        lhs = []
-        for e in range(4):
-            c = column_tile(pos, 1 - pos[PC], e, d)
-            lhs += [jnp.concatenate([dense[c + i, r, :] for r in rows], axis=0) for i in range(2)]
-        rhs = near[...] if d == 0 else far[(d - 1) * ROWS : d * ROWS]
-        total += jnp.dot(jnp.concatenate(lhs, axis=1), rhs, preferred_element_type=F32)
-    n = total.shape[0] // len(outs)
+    total = far_sum(total, dense, pos, 1 - pos[PC], far, rows)
     for i, out in enumerate(outs):
-        out[...] = total[i * n : (i + 1) * n].astype(out.dtype)
-
-
-def middle(pos, own, r1, r2, r3, w, cot, act, bt, q, m1, m2, m3, lg):
-    agg = (own[...] + r1[...].astype(F32) + r2[...].astype(F32) + r3[...].astype(F32)).astype(BF16)
+        out[...] = total[i * NODE : (i + 1) * NODE].astype(out.dtype)
+
+
+def add_two(own, r1, r2, out):
+    out[...] = own[...] + r1[...].astype(F32) + r2[...].astype(F32)
+
+
+def middle(pos, own, r3, w, cot, act, bt, q, m1, m2, m3, lg):
+    agg = (own[...] + r3[...].astype(F32)).astype(BF16)
     pre = jnp.dot(agg, w[...], preferred_element_type=F32)
     sg = jax.nn.sigmoid(pre)
     act[...] = (pre * sg).astype(BF16)
@@ -150,7 +162,7 @@
             out[NODE:] = piece.astype(BF16)
 
 
-FIRST, LAST = (2, 1), (3, 0)
+FIRST, LAST = (1, 3), (2, 0)
 
 
 def back_all(bt):
@@ -203,15 +215,15 @@
             out[4 * NODE + 32 :] = lo
 
 
-def backward_own_first(pos, dense, bt, got, qown, x2, x1, qs):
+def backward_own_first(pos, dense, bt, got, qown, x1, x3, qs):
     hi, lo = two_parts(qown[...] + got[8 * NODE :].astype(F32))
     qs[...] = hi.astype(F32) + lo.astype(F32)
-    backward_own(FIRST, dense, back_all(bt), pos, got, (x2, x1), hi, lo)
-
-
-def backward_own_last(pos, dense, bt, got, qs, x3, x0):
+    backward_own(FIRST, dense, back_all(bt), pos, got, (x1, x3), hi, lo)
+
+
+def backward_own_last(pos, dense, bt, got, qs, x2, x0):
     hi, lo = two_parts(qs[...])
-    backward_own(LAST, dense, back_all(bt), pos, got, (x3, x0), hi, lo)
+    backward_own(LAST, dense, back_all(bt), pos, got, (x2, x0), hi, lo)
 
 
 def ring_sum(place, own, received, held):
@@ -225,20 +237,20 @@
     return [(d, (r[at : at + 32], r[at + 32 :])) for d, r in enumerate(received, 1)]
 
 
+def add_pair(own, r1, r3, out):
+    n = 4 * NODE
+    out[...] = own[...] + r1[:n].astype(F32) + r3[:n].astype(F32)
+
+
 def first_sum(pos, x0, r1, r2, r3, qs, t0, t1, t2, t3, qt, held):
     hi, lo = two_parts(ring_sum(pos[P1], qs[...], weight_parts((r1, r2, r3), 4 * NODE), held))
     qt[...] = hi.astype(F32) + lo.astype(F32)
     for d, out in enumerate((t0, t1, t2, t3)):
         at = slice(d * NODE, (d + 1) * NODE)
-        s = x0[at]
-        for r in (r1, r2, r3):
-            s += r[at].astype(F32)
+        out[:NODE] = (x0[at] + r2[at].astype(F32)).astype(out.dtype)
         if d:
-            out[:NODE] = s.astype(BF16)
             out[NODE : NODE + 32] = hi
             out[NODE + 32 :] = lo
-        else:
-            out[...] = s
 
 
 def weight_sum(pos, r1, r2, r3, qt, qu, held):
@@ -282,7 +294,7 @@
     z, x, core, y = (lax.axis_index(a) for a in ("z", "x", "core", "y"))
     zero = core == 0
     places = [z, x, core, jnp.where(zero, x, z), jnp.where(zero, z, x)]
-    places += [lax.rem(y + d, 4) for d in range(4)]
+    places += [lax.rem(y + d, 4) for d in range(4)] + [y ^ 1, y ^ 3]
     pos = jnp.stack(places).astype(jnp.int32)
     tv = pltpu.with_memory_space_constraint(tv, pltpu.HBM)
 
@@ -291,38 +303,40 @@
     near, count, pos = lax.optimization_barrier((near, count, pos))
     far = {d: send_by_core(near, 1, -d) for d in (2, 1, 3)}
     near_other = send(near, "core", 1, 2)
-    dense, done = call(
+    dense = call(
         dense_block,
-        [DENSE, shape((8, 128), F32)],
+        DENSE,
         [ASPEC, SSPEC, SSPEC, SSPEC],
         [pltpu.SemaphoreType.DMA],
         nbytes=24 * MIB,
     )(tv, rows, cols, count)
+    sums = shape((ROWS, FEAT), F32)
+    dense, acc = dense_call(forward_near, [sums], dense, pos, near, near_other, cost=16 * MIB)
+    far, acc = lax.optimization_barrier((far, acc))
     far = jnp.concatenate([far[d] for d in (1, 2, 3)], axis=0)
-    far, done = lax.optimization_barrier((far, done))
     far_other = send(far, "core", 1, 2)
-
-    dense, acc = dense_call(forward_own, [shape((ROWS, FEAT), F32)], dense, pos, near, far, done)
+    dense, acc = dense_call(forward_own, [sums], dense, pos, far, acc)
     block, blockf = shape((NODE, FEAT), BF16), shape((NODE, FEAT), F32)
 
     def other_columns(dense, blocks, outs):
         kernel = functools.partial(forward_other, blocks)
-        return dense_call(kernel, outs, dense, pos, near_other, far_other, acc)
+        return dense_call(kernel, outs, dense, pos, far_other, acc)
 
     dense, s2, s1 = other_columns(dense, (PY2, PY1), [block, block])
     r2, r1 = send(s2, "y", 2), send(s1, "y", 1)
     dense, s3, own = other_columns(dense, (PY3, PY), [block, blockf])
+    own = call(add_two, blockf, [VSPEC] * 3, nbytes=MIB // 2)(own, r1, r2)
     r3 = send(s3, "y", 3)
 
     packed = shape((NODE + 64, FEAT), BF16)
     activated, bt, q, m1, m2, m3 = call(
         middle,
         [block, block, shape((64, FEAT), F32), packed, packed, packed],
-        [SSPEC] + [VSPEC] * 6,
+        [SSPEC] + [VSPEC] * 4,
         [pltpu.VMEM((FEAT, FEAT), F32)],
         flops=6 * FEAT**3,
         nbytes=MIB,
-    )(pos, own, r1, r2, r3, weight, cotangent)
+    )(pos, own, r3, weight, cotangent)
     r = {d: send(m, "y", d) for d, m in ((2, m2), (1, m1), (3, m3))}
 
     piece = shape((32, FEAT), F32)
@@ -334,37 +348,29 @@
     )
     got_first = send(other, "core", 1, 2)
     dense, other = dense_call(
-        backward_other_last, [shape((8 * NODE, FEAT), BF16)], dense, pos, bt,
+        backward_other_last, [shape((8 * NODE, FEAT), BF16)], dense, pos, bt
     )
     got_last = send(other, "core", 1, 2)
-    long = shape((4 * NODE + 64, FEAT), BF16)
-    dense, x2, x1, qs = dense_call(
-        backward_own_first, [long, long, piece], dense, pos, bt, got_first, qown,
-    )
-    r = {2: send_by_core(x2, 0, 2), 1: send_by_core(x1, 0, 1)}
-    dense, x3, x0 = dense_call(
-        backward_own_last,
-        [long, shape((4 * NODE, FEAT), F32)],
-        dense, pos, bt, got_last, qs,
-    )
-    r[3] = send_by_core(x3, 0, 3)
+    long, longf = shape((4 * NODE + 64, FEAT), BF16), shape((4 * NODE, FEAT), F32)
+    dense, x1, x3, qs = dense_call(
+        backward_own_first, [long, long, piece], dense, pos, bt, got_first, qown
+    )
+    r1, r3 = send_by_core(x1, 0, 1), send_by_core(x3, 0, 3)
+    dense, x2, x0 = dense_call(backward_own_last, [long, longf], dense, pos, bt, got_last, qs)
+    r2 = send_by_core(x2, 0, 2)
+    held = [pltpu.VMEM((4, 32, FEAT), F32)]
+    x0 = call(add_pair, longf, [VSPEC] * 3, nbytes=MIB)(x0, r1, r3)
     t0, t1, t2, t3, qt = call(
         first_sum,
         [blockf, packed, packed, packed, piece],
         [SSPEC] + [VSPEC] * 5,
-        [pltpu.VMEM((4, 32, FEAT), F32)],
-        nbytes=4 * MIB,
-    )(pos, x0, r[1], r[2], r[3], qs)
-    r = {d: send_by_core(v, 1, d) for d, v in ((2, t2), (1, t1), (3, t3))}
-    qu = call(
-        weight_sum,
-        piece,
-        [SSPEC] + [VSPEC] * 4,
-        [pltpu.VMEM((4, 32, FEAT), F32)],
-        nbytes=MIB // 4,
-    )(pos, r[1], r[2], r[3], qt)
+        held,
+        nbytes=MIB,
+    )(pos, x0, r1, r2, r3, qs)
+    r1, r2, r3 = (send_by_core(v, 1, d) for d, v in ((1, t1), (2, t2), (3, t3)))
+    qu = call(weight_sum, piece, [SSPEC] + [VSPEC] * 4, held, nbytes=MIB // 4)(pos, r1, r2, r3, qt)
     pair = jnp.concatenate([qu, send(qu, "core", 1, 2)], axis=0)
-    feature_grad = call(last_sum, block, [VSPEC] * 4, nbytes=MIB)(t0, r[1], r[2], r[3])
+    feature_grad = call(last_sum, block, [VSPEC] * 4, nbytes=MIB)(t0, r1, r2, r3)
     r = {d: send(pair, "y", d) for d in (2, 1, 3)}
     weight_grad = call(
         weight_rows, shape((FEAT, FEAT), F32), [SSPEC] + [VSPEC] * 4, nbytes=MIB // 2

time: 111 us -> 106 us (0.955)
  waiting for transfers between devices: 47.6 us -> 37.3 us
  starting transfers between devices: 33 us -> 36.5 us
    ppermute x14, waiting for transfers between devices: 21.7 us -> 16.3 us  [send(): return lax.ppermute(v, axis, [(i, (i + d) % n) for i in range(n)])]
    ppermute x12, waiting for transfers between devices: 25.9 us -> 21 us  [send_by_core(): return lax.ppermute(v, RING, pairs)]
    ppermute x14, starting transfers between devices: 13.3 us -> 15.9 us  [send(): return lax.ppermute(v, axis, [(i, (i + d) % n) for i in range(n)])]
    pallas_call x7 -> x8, Pallas kernels: 13.8 us -> 14.5 us  [dense_call(): call(wrapped, [DENSE] + outs, [SSPEC] + [VSPEC] * (n - 1), scratch, flops...]
    pallas_call x3 -> x5, Pallas kernels: 8.97 us -> 9.39 us  [the longest x1 7.86 us: body(): call(dense_block, DENSE, [ASPEC, SSPEC, SSPEC, SSPEC], [pltpu.SemaphoreTy...]
  transfers between devices with their start and end apart: 26 -> 26, of which waited for: 20 -> 17; matrix products, arithmetic and copies ran while one was open for 1% -> 1% of each run, Pallas kernels for 13% -> 19%
where the time goes in v3:
time: 106 us; the launch traced here: 105 us
  waiting for transfers between devices  37.3 us (35%)
  starting transfers between devices  36.5 us (34%)
  Pallas kernels  27.3 us (26%)
  other arithmetic  2.34 us (2%)
  between operations  1.48 us (1%)
    ppermute x12, waiting for transfers between devices, send_by_core(): return lax.ppermute(v, RING, pairs)  21 us
    ppermute x12, starting transfers between devices, send_by_core(): return lax.ppermute(v, RING, pairs)  20.6 us
    ppermute x14, waiting for transfers between devices, send(): return lax.ppermute(v, axis, [(i, (i + d) % n) for i in range(n)])  16.3 us
    ppermute x14, starting transfers between devices, send(): return lax.ppermute(v, axis, [(i, (i + d) % n) for i in range(n)])  15.9 us
    pallas_call x8, Pallas kernels, dense_call(): call(wrapped, [DENSE] + outs, [SSPEC] + [VSPEC] * (n - 1), scratch, flops...  14.5 us
    pallas_call x1, Pallas kernels, body(): call(dense_block, DENSE, [ASPEC, SSPEC, SSPEC, SSPEC], [pltpu.SemaphoreTy...  7.86 us
  transfers between devices with their start and end apart: 26, of which 17 were waited for; matrix products, arithmetic and copies ran while one was open for 1% of the time, Pallas kernels for 19%

profile of v3, /device:TPU:0, one launch (start us, length us, event | category | flops | bytes accessed | tf_op | source)
XLA Modules:
  0.0 105.0 jit_solution(12974273238924601056)
XLA Ops:
  0.6 3.2 %collective-permute-start.1 = (bf16[256,256]{1,0:T(8,128)(2,1)}, bf16[256,256]{1,0:T(8,128)(2,1)S(1)}, u32[]{:S(2)}, u32[]{:S(2)}) collective-permute-start(bf16[256,256]{1,0:T(8,128)(2,1)} %param.7), channel_id=1, source_target_pairs={{0,16},{4,68},{8,24},{12,76},{16,0},{20,84},{24,8},{28,92},{32,48}... | collective-permute-start | bytes 393224 | tf_op jit(solution)/shard_map/ppermute | solution.py:289
  9.0 2.4 %collective-permute-done.2 = bf16[256,256]{1,0:T(8,128)(2,1)S(1)} collective-permute-done((bf16[256,256]{1,0:T(8,128)(2,1)}, bf16[256,256]{1,0:T(8,128)(2,1)S(1)}, u32[]{:S(2)}, u32[]{:S(2)}) %collective-permute-start.2) | collective-permute-done | bytes 131104 | tf_op jit(solution)/shard_map/ppermute | solution.py:289
  12.4 2.0 %collective-permute-start.6 = (bf16[1024,256]{1,0:T(8,128)(2,1)S(1)}, bf16[1024,256]{1,0:T(8,128)(2,1)S(1)}, u32[]{:S(2)}, u32[]{:S(2)}) collective-permute-start(bf16[1024,256]{1,0:T(8,128)(2,1)S(1)} %pad_maximum_fusion.refs_2_), channel_id=1, source_target_pairs={{0,32},{4,12},{8,40},{12,20},{16,48},{20,28},{24,56},{28,4},{32,64... | collective-permute-start | bytes 1572872 | tf_op jit(solution)/shard_map/ppermute | solution.py:289
  14.4 3.6 %collective-permute-start.5 = (bf16[1024,256]{1,0:T(8,128)(2,1)S(1)}, bf16[1024,256]{1,0:T(8,128)(2,1)S(1)}, u32[]{:S(2)}, u32[]{:S(2)}) collective-permute-start(bf16[1024,256]{1,0:T(8,128)(2,1)S(1)} %pad_maximum_fusion.refs_2_), channel_id=1, source_target_pairs={{0,64},{4,20},{8,72},{12,28},{16,80},{20,4},{24,88},{28,12},{32,96... | collective-permute-start | bytes 1572872 | tf_op jit(solution)/shard_map/ppermute | solution.py:289
  21.0 7.9 %shard_map.94.refs_1_ = bf16[64,1024,128]{2,1,0:T(8,128)(2,1)S(1)} custom-call(bf16[384,128,128]{2,1,0:T(8,128)(2,1)} %bitcast.14, s32[384]{0:T(512)S(1)} %reduce.rows, s32[384]{0:T(512)S(1)} %reduce.1.cols, s32[1]{0:T(128)} %bitcast.13.count), custom_call_target="tpu_custom_call" | custom-call | bytes 25165824 | tf_op jit(solution)/shard_map/pallas_call | solution.py:306
  28.9 1.8 %shard_map.95 = (bf16[64,1024,128]{2,1,0:T(8,128)(2,1)S(1)}, f32[1024,256]{1,0:T(8,128)S(1)}) custom-call(s32[11]{0:T(128)S(1)} %stack.47.refs_0_.pos, bf16[64,1024,128]{2,1,0:T(8,128)(2,1)S(1)} %shard_map.94.refs_1_, bf16[1024,256]{1,0:T(8,128)(2,1)S(1)} %pad_maximum_fusion.refs_2_, ...), custom_call_target="tpu_custom_call", output_to_operand_aliasing={{0}: (1, {})} | custom-call | flops 16777216 | bytes 16777216 | tf_op jit(solution)/shard_map/pallas_call | solution.py:61
  30.9 2.3 %shard_map.96 = (bf16[64,1024,128]{2,1,0:T(8,128)(2,1)S(1)}, f32[1024,256]{1,0:T(8,128)S(1)}) custom-call(s32[11]{0:T(128)S(1)} %stack.47.refs_0_.pos, bf16[64,1024,128]{2,1,0:T(8,128)(2,1)S(1)} %get-tuple-element.46.refs_1_, bf16[3072,256]{1,0:T(8,128)(2,1)S(1)} %constant_dynamic-update-slice_fusion.refs_2_, ...), custom_call_target="tpu_custom_call", output_to_operand_aliasing={{0}: (1, {})} | custom-call | flops 1000 | bytes 1000 | tf_op jit(solution)/shard_map/pallas_call | solution.py:61
  35.9 1.6 %collective-permute-start.8 = (bf16[256,256]{1,0:T(8,128)(2,1)S(1)}, bf16[256,256]{1,0:T(8,128)(2,1)S(1)}, u32[]{:S(2)}, u32[]{:S(2)}) collective-permute-start(bf16[256,256]{1,0:T(8,128)(2,1)S(1)} %get-tuple-element.56), channel_id=1, source_target_pairs={{0,1},{1,2},{2,3},{3,0},{4,5},{5,6},{6,7},{7,4},{8,9},{9,10},{10,1... | collective-permute-start | bytes 393224 | tf_op jit(solution)/shard_map/ppermute | solution.py:276
  37.5 2.9 %collective-permute-start.9 = (bf16[256,256]{1,0:T(8,128)(2,1)S(1)}, bf16[256,256]{1,0:T(8,128)(2,1)S(1)}, u32[]{:S(2)}, u32[]{:S(2)}) collective-permute-start(bf16[256,256]{1,0:T(8,128)(2,1)S(1)} %get-tuple-element.57), channel_id=1, source_target_pairs={{0,2},{1,3},{2,0},{3,1},{4,6},{5,7},{6,4},{7,5},{8,10},{9,11},{10,... | collective-permute-start | bytes 393224 | tf_op jit(solution)/shard_map/ppermute | solution.py:276
  43.4 3.4 %collective-permute-done.9.r2 = bf16[256,256]{1,0:T(8,128)(2,1)S(1)} collective-permute-done((bf16[256,256]{1,0:T(8,128)(2,1)S(1)}, bf16[256,256]{1,0:T(8,128)(2,1)S(1)}, u32[]{:S(2)}, u32[]{:S(2)}) %collective-permute-start.9) | collective-permute-done | bytes 131104 | tf_op jit(solution)/shard_map/ppermute | solution.py:276
  48.4 1.7 %collective-permute-start.11 = (bf16[320,256]{1,0:T(8,128)(2,1)S(1)}, bf16[320,256]{1,0:T(8,128)(2,1)S(1)}, u32[]{:S(2)}, u32[]{:S(2)}) collective-permute-start(bf16[320,256]{1,0:T(8,128)(2,1)S(1)} %get-tuple-element.62), channel_id=1, source_target_pairs={{0,1},{1,2},{2,3},{3,0},{4,5},{5,6},{6,7},{7,4},{8,9},{9,10},{10,1... | collective-permute-start | bytes 491528 | tf_op jit(solution)/shard_map/ppermute | solution.py:276
  50.1 2.4 %collective-permute-start.12 = (bf16[320,256]{1,0:T(8,128)(2,1)S(1)}, bf16[320,256]{1,0:T(8,128)(2,1)S(1)}, u32[]{:S(2)}, u32[]{:S(2)}) collective-permute-start(bf16[320,256]{1,0:T(8,128)(2,1)S(1)} %get-tuple-element.63), channel_id=1, source_target_pairs={{0,2},{1,3},{2,0},{3,1},{4,6},{5,7},{6,4},{7,5},{8,10},{9,11},{10,... | collective-permute-start | bytes 491528 | tf_op jit(solution)/shard_map/ppermute | solution.py:276
  53.4 3.0 %collective-permute-done.11.refs_3_ = bf16[320,256]{1,0:T(8,128)(2,1)S(1)} collective-permute-done((bf16[320,256]{1,0:T(8,128)(2,1)S(1)}, bf16[320,256]{1,0:T(8,128)(2,1)S(1)}, u32[]{:S(2)}, u32[]{:S(2)}) %collective-permute-start.11) | collective-permute-done | bytes 163872 | tf_op jit(solution)/shard_map/ppermute | solution.py:276
  56.3 2.8 %collective-permute-done.12.refs_4_ = bf16[320,256]{1,0:T(8,128)(2,1)S(1)} collective-permute-done((bf16[320,256]{1,0:T(8,128)(2,1)S(1)}, bf16[320,256]{1,0:T(8,128)(2,1)S(1)}, u32[]{:S(2)}, u32[]{:S(2)}) %collective-permute-start.12) | collective-permute-done | bytes 163872 | tf_op jit(solution)/shard_map/ppermute | solution.py:276
  59.1 1.8 %shard_map.101 = (bf16[64,1024,128]{2,1,0:T(8,128)(2,1)S(1)}, bf16[2080,256]{1,0:T(8,128)(2,1)S(1)}, bf16[4,256,256]{2,1,0:T(8,128)(2,1)S(1)}, f32[32,256]{1,0:T(8,128)S(1)}) custom-call(s32[11]{0:T(128)S(1)} %stack.47.refs_0_.pos, bf16[64,1024,128]{2,1,0:T(8,128)(2,1)S(1)} %get-tuple-element.60.refs_1_, ...), custom_call_target="tpu_custom_call", output_to_operand_aliasing={{0}: (1, {})} | custom-call | flops 1000 | bytes 1000 | tf_op jit(solution)/shard_map/pallas_call | solution.py:61
  61.0 1.8 %shard_map.102 = (bf16[64,1024,128]{2,1,0:T(8,128)(2,1)S(1)}, bf16[2048,256]{1,0:T(8,128)(2,1)S(1)}) custom-call(s32[11]{0:T(128)S(1)} %stack.47.refs_0_.pos, bf16[64,1024,128]{2,1,0:T(8,128)(2,1)S(1)} %get-tuple-element.66.refs_1_, bf16[4,256,256]{2,1,0:T(8,128)(2,1)S(1)} %get-tuple-element.67.refs_2_), custom_call_target="tpu_custom_call", output_to_operand_aliasing={{0}: (1, {})} | custom-call | flops 1000 | bytes 1000 | tf_op jit(solution)/shard_map/pallas_call | solution.py:61
  63.7 1.8 %shard_map.103 = (bf16[64,1024,128]{2,1,0:T(8,128)(2,1)S(1)}, bf16[1088,256]{1,0:T(8,128)(2,1)S(1)}, bf16[1088,256]{1,0:T(8,128)(2,1)S(1)}, f32[32,256]{1,0:T(8,128)S(1)}) custom-call(s32[11]{0:T(128)S(1)} %stack.47.refs_0_.pos, bf16[64,1024,128]{2,1,0:T(8,128)(2,1)S(1)} %get-tuple-element.68.refs_1_, ...), custom_call_target="tpu_custom_call", output_to_operand_aliasing={{0}: (1, {})} | custom-call | flops 1000 | bytes 1000 | tf_op jit(solution)/shard_map/pallas_call | solution.py:61
  65.8 3.2 %collective-permute-start.17 = (bf16[1088,256]{1,0:T(8,128)(2,1)S(1)}, bf16[1088,256]{1,0:T(8,128)(2,1)S(1)}, u32[]{:S(2)}, u32[]{:S(2)}) collective-permute-start(bf16[1088,256]{1,0:T(8,128)(2,1)S(1)} %get-tuple-element.76), channel_id=1, source_target_pairs={{0,24},{4,100},{8,0},{12,108},{16,8},{20,116},{24,16},{28,124},{32... | collective-permute-start | bytes 1671176 | tf_op jit(solution)/shard_map/ppermute | solution.py:289
  69.0 1.8 %shard_map.104 = (bf16[64,1024,128]{2,1,0:T(8,128)(2,1)S(1)}, bf16[1088,256]{1,0:T(8,128)(2,1)S(1)}, f32[1024,256]{1,0:T(8,128)S(1)}) custom-call(s32[11]{0:T(128)S(1)} %stack.47.refs_0_.pos, bf16[64,1024,128]{2,1,0:T(8,128)(2,1)S(1)} %get-tuple-element.71.refs_1_, ...), custom_call_target="tpu_custom_call", output_to_operand_aliasing={{0}: (1, {})} | custom-call | flops 1000 | bytes 1000 | tf_op jit(solution)/shard_map/pallas_call | solution.py:61
  71.0 11.5 %collective-permute-done.16.r1 = bf16[1088,256]{1,0:T(8,128)(2,1)S(1)} collective-permute-done((bf16[1088,256]{1,0:T(8,128)(2,1)S(1)}, bf16[1088,256]{1,0:T(8,128)(2,1)S(1)}, u32[]{:S(2)}, u32[]{:S(2)}) %collective-permute-start.16) | collective-permute-done | bytes 557088 | tf_op jit(solution)/shard_map/ppermute | solution.py:289
  84.9 2.0 %collective-permute-start.20 = (bf16[320,256]{1,0:T(8,128)(2,1)S(1)}, bf16[320,256]{1,0:T(8,128)(2,1)S(1)}, u32[]{:S(2)}, u32[]{:S(2)}) collective-permute-start(bf16[320,256]{1,0:T(8,128)(2,1)S(1)} %get-tuple-element.79), channel_id=1, source_target_pairs={{0,64},{4,20},{8,72},{12,28},{16,80},{20,4},{24,88},{28,12},{32,96... | collective-permute-start | bytes 491528 | tf_op jit(solution)/shard_map/ppermute | solution.py:289
  89.9 2.0 %collective-permute-done.20.r2 = bf16[320,256]{1,0:T(8,128)(2,1)S(1)} collective-permute-done((bf16[320,256]{1,0:T(8,128)(2,1)S(1)}, bf16[320,256]{1,0:T(8,128)(2,1)S(1)}, u32[]{:S(2)}, u32[]{:S(2)}) %collective-permute-start.20) | collective-permute-done | bytes 163872 | tf_op jit(solution)/shard_map/ppermute | solution.py:289
  94.4 2.6 %collective-permute-start.25 = (f32[64,256]{1,0:T(8,128)S(1)}, f32[64,256]{1,0:T(8,128)S(1)}, u32[]{:S(2)}, u32[]{:S(2)}) collective-permute-start(f32[64,256]{1,0:T(8,128)S(1)} %pad_maximum_fusion.1.own), channel_id=1, source_target_pairs={{0,3},{1,0},{2,1},{3,2},{4,7},{5,4},{6,5},{7,6},{8,11},{9,8},{10,9... | collective-permute-start | bytes 196616 | tf_op jit(solution)/shard_map/ppermute | solution.py:276
  100.1 3.0 %collective-permute-done.24.r2 = f32[64,256]{1,0:T(8,128)S(1)} collective-permute-done((f32[64,256]{1,0:T(8,128)S(1)}, f32[64,256]{1,0:T(8,128)S(1)}, u32[]{:S(2)}, u32[]{:S(2)}) %collective-permute-start.24) | collective-permute-done | bytes 65568 | tf_op jit(solution)/shard_map/ppermute | solution.py:276
  (56 shorter events, 31.1 us)
Async XLA Ops:
  0.6 6.8 %collective-permute-start.1 = (bf16[256,256]{1,0:T(8,128)(2,1)}, bf16[256,256]{1,0:T(8,128)(2,1)S(1)}, u32[]{:S(2)}, u32[]{:S(2)}) collective-permute-start(bf16[256,256]{1,0:T(8,128)(2,1)} %param.7), channel_id=1, source_target_pairs={{0,16},{4,68},{8,24},{12,76},{16,0},{20,84},{24,8},{28,92},{32,48}... | collective-permute-start | bytes 393224 | tf_op jit(solution)/shard_map/ppermute | solution.py:289
  3.8 5.2 %collective-permute-start = (bf16[256,256]{1,0:T(8,128)(2,1)}, bf16[256,256]{1,0:T(8,128)(2,1)S(1)}, u32[]{:S(2)}, u32[]{:S(2)}) collective-permute-start(bf16[256,256]{1,0:T(8,128)(2,1)} %param.7), channel_id=1, source_target_pairs={{0,24},{4,100},{8,0},{12,108},{16,8},{20,116},{24,16},{28,124},{32... | collective-permute-start | bytes 393224 | tf_op jit(solution)/shard_map/ppermute | solution.py:289
  5.0 6.4 %collective-permute-start.2 = (bf16[256,256]{1,0:T(8,128)(2,1)}, bf16[256,256]{1,0:T(8,128)(2,1)S(1)}, u32[]{:S(2)}, u32[]{:S(2)}) collective-permute-start(bf16[256,256]{1,0:T(8,128)(2,1)} %param.7), channel_id=1, source_target_pairs={{0,8},{4,36},{8,16},{12,44},{16,24},{20,52},{24,0},{28,60},{32,40}... | collective-permute-start | bytes 393224 | tf_op jit(solution)/shard_map/ppermute | solution.py:289
  12.3 16.6 %collective-permute-start.3 = (bf16[1024,256]{1,0:T(8,128)(2,1)S(1)}, bf16[1024,256]{1,0:T(8,128)(2,1)S(1)}, u32[]{:S(2)}, u32[]{:S(2)}) collective-permute-start(bf16[1024,256]{1,0:T(8,128)(2,1)S(1)} %pad_maximum_fusion.refs_2_), channel_id=1, source_target_pairs={{0,4},{4,0},{1,5},{5,1},{2,6},{6,2},{3,7},{7,3},{8,12},{12,8},{9,1... | collective-permute-start | bytes 1572872 | tf_op jit(solution)/shard_map/ppermute | solution.py:276
  12.4 18.3 %collective-permute-start.6 = (bf16[1024,256]{1,0:T(8,128)(2,1)S(1)}, bf16[1024,256]{1,0:T(8,128)(2,1)S(1)}, u32[]{:S(2)}, u32[]{:S(2)}) collective-permute-start(bf16[1024,256]{1,0:T(8,128)(2,1)S(1)} %pad_maximum_fusion.refs_2_), channel_id=1, source_target_pairs={{0,32},{4,12},{8,40},{12,20},{16,48},{20,28},{24,56},{28,4},{32,64... | collective-permute-start | bytes 1572872 | tf_op jit(solution)/shard_map/ppermute | solution.py:289
  14.4 16.4 %collective-permute-start.5 = (bf16[1024,256]{1,0:T(8,128)(2,1)S(1)}, bf16[1024,256]{1,0:T(8,128)(2,1)S(1)}, u32[]{:S(2)}, u32[]{:S(2)}) collective-permute-start(bf16[1024,256]{1,0:T(8,128)(2,1)S(1)} %pad_maximum_fusion.refs_2_), channel_id=1, source_target_pairs={{0,64},{4,20},{8,72},{12,28},{16,80},{20,4},{24,88},{28,12},{32,96... | collective-permute-start | bytes 1572872 | tf_op jit(solution)/shard_map/ppermute | solution.py:289
  17.9 12.8 %collective-permute-start.4 = (bf16[1024,256]{1,0:T(8,128)(2,1)S(1)}, bf16[1024,256]{1,0:T(8,128)(2,1)S(1)}, u32[]{:S(2)}, u32[]{:S(2)}) collective-permute-start(bf16[1024,256]{1,0:T(8,128)(2,1)S(1)} %pad_maximum_fusion.refs_2_), channel_id=1, source_target_pairs={{0,96},{4,28},{8,104},{12,4},{16,112},{20,12},{24,120},{28,20},{32... | collective-permute-start | bytes 1572872 | tf_op jit(solution)/shard_map/ppermute | solution.py:289
  30.9 3.5 %collective-permute-start.7 = (bf16[3072,256]{1,0:T(8,128)(2,1)S(1)}, bf16[3072,256]{1,0:T(8,128)(2,1)S(1)}, u32[]{:S(2)}, u32[]{:S(2)}) collective-permute-start(bf16[3072,256]{1,0:T(8,128)(2,1)S(1)} %constant_dynamic-update-slice_fusion.refs_2_), channel_id=1, source_target_pairs={{0,4},{4,0},{1,5},{5,1},{2,6},{6,2},{3,7},{7,3},{8,12},{12,8},{9,1... | collective-permute-start | bytes 4718600 | tf_op jit(solution)/shard_map/ppermute | solution.py:276
  35.9 7.5 %collective-permute-start.8 = (bf16[256,256]{1,0:T(8,128)(2,1)S(1)}, bf16[256,256]{1,0:T(8,128)(2,1)S(1)}, u32[]{:S(2)}, u32[]{:S(2)}) collective-permute-start(bf16[256,256]{1,0:T(8,128)(2,1)S(1)} %get-tuple-element.56), channel_id=1, source_target_pairs={{0,1},{1,2},{2,3},{3,0},{4,5},{5,6},{6,7},{7,4},{8,9},{9,10},{10,1... | collective-permute-start | bytes 393224 | tf_op jit(solution)/shard_map/ppermute | solution.py:276
  37.5 9.2 %collective-permute-start.9 = (bf16[256,256]{1,0:T(8,128)(2,1)S(1)}, bf16[256,256]{1,0:T(8,128)(2,1)S(1)}, u32[]{:S(2)}, u32[]{:S(2)}) collective-permute-start(bf16[256,256]{1,0:T(8,128)(2,1)S(1)} %get-tuple-element.57), channel_id=1, source_target_pairs={{0,2},{1,3},{2,0},{3,1},{4,6},{5,7},{6,4},{7,5},{8,10},{9,11},{10,... | collective-permute-start | bytes 393224 | tf_op jit(solution)/shard_map/ppermute | solution.py:276
  41.9 5.0 %collective-permute-start.10 = (bf16[256,256]{1,0:T(8,128)(2,1)S(1)}, bf16[256,256]{1,0:T(8,128)(2,1)S(1)}, u32[]{:S(2)}, u32[]{:S(2)}) collective-permute-start(bf16[256,256]{1,0:T(8,128)(2,1)S(1)} %get-tuple-element.58), channel_id=1, source_target_pairs={{0,3},{1,0},{2,1},{3,2},{4,7},{5,4},{6,5},{7,6},{8,11},{9,8},{10,9... | collective-permute-start | bytes 393224 | tf_op jit(solution)/shard_map/ppermute | solution.py:276
  48.4 7.9 %collective-permute-start.11 = (bf16[320,256]{1,0:T(8,128)(2,1)S(1)}, bf16[320,256]{1,0:T(8,128)(2,1)S(1)}, u32[]{:S(2)}, u32[]{:S(2)}) collective-permute-start(bf16[320,256]{1,0:T(8,128)(2,1)S(1)} %get-tuple-element.62), channel_id=1, source_target_pairs={{0,1},{1,2},{2,3},{3,0},{4,5},{5,6},{6,7},{7,4},{8,9},{9,10},{10,1... | collective-permute-start | bytes 491528 | tf_op jit(solution)/shard_map/ppermute | solution.py:276
  50.1 9.0 %collective-permute-start.12 = (bf16[320,256]{1,0:T(8,128)(2,1)S(1)}, bf16[320,256]{1,0:T(8,128)(2,1)S(1)}, u32[]{:S(2)}, u32[]{:S(2)}) collective-permute-start(bf16[320,256]{1,0:T(8,128)(2,1)S(1)} %get-tuple-element.63), channel_id=1, source_target_pairs={{0,2},{1,3},{2,0},{3,1},{4,6},{5,7},{6,4},{7,5},{8,10},{9,11},{10,... | collective-permute-start | bytes 491528 | tf_op jit(solution)/shard_map/ppermute | solution.py:276
  52.5 6.6 %collective-permute-start.13 = (bf16[320,256]{1,0:T(8,128)(2,1)S(1)}, bf16[320,256]{1,0:T(8,128)(2,1)S(1)}, u32[]{:S(2)}, u32[]{:S(2)}) collective-permute-start(bf16[320,256]{1,0:T(8,128)(2,1)S(1)} %get-tuple-element.64), channel_id=1, source_target_pairs={{0,3},{1,0},{2,1},{3,2},{4,7},{5,4},{6,5},{7,6},{8,11},{9,8},{10,9... | collective-permute-start | bytes 491528 | tf_op jit(solution)/shard_map/ppermute | solution.py:276
  62.9 6.2 %collective-permute-start.15 = (bf16[2048,256]{1,0:T(8,128)(2,1)S(1)}, bf16[2048,256]{1,0:T(8,128)(2,1)S(1)}, u32[]{:S(2)}, u32[]{:S(2)}) collective-permute-start(bf16[2048,256]{1,0:T(8,128)(2,1)S(1)} %get-tuple-element.72), channel_id=1, source_target_pairs={{0,4},{4,0},{1,5},{5,1},{2,6},{6,2},{3,7},{7,3},{8,12},{12,8},{9,1... | collective-permute-start | bytes 3145736 | tf_op jit(solution)/shard_map/ppermute | solution.py:276
  65.5 17.0 %collective-permute-start.16 = (bf16[1088,256]{1,0:T(8,128)(2,1)S(1)}, bf16[1088,256]{1,0:T(8,128)(2,1)S(1)}, u32[]{:S(2)}, u32[]{:S(2)}) collective-permute-start(bf16[1088,256]{1,0:T(8,128)(2,1)S(1)} %get-tuple-element.75), channel_id=1, source_target_pairs={{0,8},{4,36},{8,16},{12,44},{16,24},{20,52},{24,0},{28,60},{32,40}... | collective-permute-start | bytes 1671176 | tf_op jit(solution)/shard_map/ppermute | solution.py:289
  65.8 16.7 %collective-permute-start.17 = (bf16[1088,256]{1,0:T(8,128)(2,1)S(1)}, bf16[1088,256]{1,0:T(8,128)(2,1)S(1)}, u32[]{:S(2)}, u32[]{:S(2)}) collective-permute-start(bf16[1088,256]{1,0:T(8,128)(2,1)S(1)} %get-tuple-element.76), channel_id=1, source_target_pairs={{0,24},{4,100},{8,0},{12,108},{16,8},{20,116},{24,16},{28,124},{32... | collective-permute-start | bytes 1671176 | tf_op jit(solution)/shard_map/ppermute | solution.py:289
  70.9 11.8 %collective-permute-start.18 = (bf16[1088,256]{1,0:T(8,128)(2,1)S(1)}, bf16[1088,256]{1,0:T(8,128)(2,1)S(1)}, u32[]{:S(2)}, u32[]{:S(2)}) collective-permute-start(bf16[1088,256]{1,0:T(8,128)(2,1)S(1)} %get-tuple-element.77), channel_id=1, source_target_pairs={{0,16},{4,68},{8,24},{12,76},{16,0},{20,84},{24,8},{28,92},{32,48}... | collective-permute-start | bytes 1671176 | tf_op jit(solution)/shard_map/ppermute | solution.py:289
  83.3 6.6 %collective-permute-start.19 = (bf16[320,256]{1,0:T(8,128)(2,1)S(1)}, bf16[320,256]{1,0:T(8,128)(2,1)S(1)}, u32[]{:S(2)}, u32[]{:S(2)}) collective-permute-start(bf16[320,256]{1,0:T(8,128)(2,1)S(1)} %get-tuple-element.78), channel_id=1, source_target_pairs={{0,32},{4,12},{8,40},{12,20},{16,48},{20,28},{24,56},{28,4},{32,64... | collective-permute-start | bytes 491528 | tf_op jit(solution)/shard_map/ppermute | solution.py:289
  84.9 7.1 %collective-permute-start.20 = (bf16[320,256]{1,0:T(8,128)(2,1)S(1)}, bf16[320,256]{1,0:T(8,128)(2,1)S(1)}, u32[]{:S(2)}, u32[]{:S(2)}) collective-permute-start(bf16[320,256]{1,0:T(8,128)(2,1)S(1)} %get-tuple-element.79), channel_id=1, source_target_pairs={{0,64},{4,20},{8,72},{12,28},{16,80},{20,4},{24,88},{28,12},{32,96... | collective-permute-start | bytes 491528 | tf_op jit(solution)/shard_map/ppermute | solution.py:289
  86.9 5.6 %collective-permute-start.21 = (bf16[320,256]{1,0:T(8,128)(2,1)S(1)}, bf16[320,256]{1,0:T(8,128)(2,1)S(1)}, u32[]{:S(2)}, u32[]{:S(2)}) collective-permute-start(bf16[320,256]{1,0:T(8,128)(2,1)S(1)} %get-tuple-element.80), channel_id=1, source_target_pairs={{0,96},{4,28},{8,104},{12,4},{16,112},{20,12},{24,120},{28,20},{32... | collective-permute-start | bytes 491528 | tf_op jit(solution)/shard_map/ppermute | solution.py:289
  94.4 5.7 %collective-permute-start.25 = (f32[64,256]{1,0:T(8,128)S(1)}, f32[64,256]{1,0:T(8,128)S(1)}, u32[]{:S(2)}, u32[]{:S(2)}) collective-permute-start(f32[64,256]{1,0:T(8,128)S(1)} %pad_maximum_fusion.1.own), channel_id=1, source_target_pairs={{0,3},{1,0},{2,1},{3,2},{4,7},{5,4},{6,5},{7,6},{8,11},{9,8},{10,9... | collective-permute-start | bytes 196616 | tf_op jit(solution)/shard_map/ppermute | solution.py:276
  97.0 6.1 %collective-permute-start.24 = (f32[64,256]{1,0:T(8,128)S(1)}, f32[64,256]{1,0:T(8,128)S(1)}, u32[]{:S(2)}, u32[]{:S(2)}) collective-permute-start(f32[64,256]{1,0:T(8,128)S(1)} %pad_maximum_fusion.1.own), channel_id=1, source_target_pairs={{0,2},{1,3},{2,0},{3,1},{4,6},{5,7},{6,4},{7,5},{8,10},{9,11},{10,... | collective-permute-start | bytes 196616 | tf_op jit(solution)/shard_map/ppermute | solution.py:276
  98.2 5.6 %collective-permute-start.23 = (f32[64,256]{1,0:T(8,128)S(1)}, f32[64,256]{1,0:T(8,128)S(1)}, u32[]{:S(2)}, u32[]{:S(2)}) collective-permute-start(f32[64,256]{1,0:T(8,128)S(1)} %pad_maximum_fusion.1.own), channel_id=1, source_target_pairs={{0,1},{1,2},{2,3},{3,0},{4,5},{5,6},{6,7},{7,4},{8,9},{9,10},{10,1... | collective-permute-start | bytes 196616 | tf_op jit(solution)/shard_map/ppermute | solution.py:276
  (4 other events, 17.2 us)

commit v4 on v3

--- a/solution.py
+++ b/solution.py
@@ -18,7 +18,7 @@
 NCT = 64
 CAP = 384
 MIB = 1 << 20
-PZ, PX, PC, P1, P2, PY, PY1, PY2, PY3, PX1, PX3 = range(11)
+PZ, PX, PC, PY, PY1, PY2, PY3, PX1, PX3 = range(9)
 RING = ("z", "x", "core")
 
 
@@ -73,7 +73,7 @@
     def copy(s):
         return pltpu.make_async_copy(
             tv.at[s],
-            dense.at[cols[s], pl.ds(pl.multiple_of(rows[s] * TILE, TILE), TILE), :],
+            dense.at[cols[0, 0, s], pl.ds(pl.multiple_of(rows[0, 0, s] * TILE, TILE), TILE), :],
             sem,
         )
 
@@ -175,11 +175,6 @@
     return jnp.dot(lhs, rhs, preferred_element_type=F32)
 
 
-def two_parts(v):
-    hi = v.astype(BF16)
-    return hi, (v - hi.astype(F32)).astype(BF16)
-
-
 def backward_other(distances, dense, lhs, pos, out):
     for k, e in enumerate(distances):
         for d in range(4):
@@ -187,16 +182,22 @@
             out[i : i + NODE] = backward_block(dense, lhs, pos, 1 - pos[PC], e, d).astype(BF16)
 
 
-def backward_other_first(pos, dense, own, r1, r2, r3, q, out, bt, qown, qsum):
-    core, y = pos[PC], pos[PY]
+def two_parts(v):
+    hi = v.astype(BF16)
+    return hi, (v - hi.astype(F32)).astype(BF16)
+
+
+def backward_other_first(pos, dense, own, r1, r2, r3, q, out, bt, qown):
+    y = pos[PY]
     bt[y] = own[...]
     total = q[...]
     for d, r in ((1, r1), (2, r2), (3, r3)):
         bt[lax.rem(y + 4 - d, 4)] = r[:NODE]
         total += r[NODE:].astype(F32)
-    qsum[...] = total
-    qown[...] = qsum[pl.ds(pl.multiple_of(core * 32, 32), 32), :]
-    out[8 * NODE :] = qsum[pl.ds(pl.multiple_of((1 - core) * 32, 32), 32), :].astype(BF16)
+    hi, lo = two_parts(total)
+    qown[...] = hi.astype(F32) + lo.astype(F32)
+    out[8 * NODE : 8 * NODE + 64] = hi
+    out[8 * NODE + 64 :] = lo
     backward_other(FIRST, dense, back_all(bt), pos, out)
 
 
@@ -204,76 +205,58 @@
     backward_other(LAST, dense, back_all(bt), pos, out)
 
 
-def backward_own(distances, dense, lhs, pos, got, outs, hi, lo):
+def backward_own(distances, dense, bt, pos, got, outs):
+    lhs = back_all(bt)
     for k, (e, out) in enumerate(zip(distances, outs, strict=True)):
         for d in range(4):
             i = (k * 4 + d) * NODE
             g = backward_block(dense, lhs, pos, pos[PC], e, d) + got[i : i + NODE].astype(F32)
             out[d * NODE : (d + 1) * NODE] = g.astype(out.dtype)
-        if e:
-            out[4 * NODE : 4 * NODE + 32] = hi
-            out[4 * NODE + 32 :] = lo
-
-
-def backward_own_first(pos, dense, bt, got, qown, x1, x3, qs):
-    hi, lo = two_parts(qown[...] + got[8 * NODE :].astype(F32))
-    qs[...] = hi.astype(F32) + lo.astype(F32)
-    backward_own(FIRST, dense, back_all(bt), pos, got, (x1, x3), hi, lo)
-
-
-def backward_own_last(pos, dense, bt, got, qs, x2, x0):
-    hi, lo = two_parts(qs[...])
-    backward_own(LAST, dense, back_all(bt), pos, got, (x2, x0), hi, lo)
-
-
-def ring_sum(place, own, received, held):
-    held[place] = own
-    for d, (hi, lo) in received:
-        held[lax.rem(place + 4 - d, 4)] = hi.astype(F32) + lo.astype(F32)
-    return (held[0] + held[1]) + (held[2] + held[3])
-
-
-def weight_parts(received, at):
-    return [(d, (r[at : at + 32], r[at + 32 :])) for d, r in enumerate(received, 1)]
-
-
-def add_pair(own, r1, r3, out):
-    n = 4 * NODE
-    out[...] = own[...] + r1[:n].astype(F32) + r3[:n].astype(F32)
-
-
-def first_sum(pos, x0, r1, r2, r3, qs, t0, t1, t2, t3, qt, held):
-    hi, lo = two_parts(ring_sum(pos[P1], qs[...], weight_parts((r1, r2, r3), 4 * NODE), held))
-    qt[...] = hi.astype(F32) + lo.astype(F32)
+
+
+def ring_sum(place, terms, out, held):
+    for d, term in enumerate(terms):
+        held[lax.rem(place + 4 - d, 4)] = term[...]
+    out[...] = (held[0] + held[1]) + (held[2] + held[3])
+
+
+def backward_own_first(pos, dense, bt, got, qown, qsum, x1, x3):
+    hi, lo = got[8 * NODE : 8 * NODE + 64], got[8 * NODE + 64 :]
+    qsum[...] = qown[...] + (hi.astype(F32) + lo.astype(F32))
+    backward_own(FIRST, dense, bt, pos, got, (x1, x3))
+
+
+def backward_own_last(pos, dense, bt, got, q, q1, q2, q3, qsum, x2, x0, held):
+    ring_sum(pos[PX], (q, q1, q2, q3), qsum, held)
+    backward_own(LAST, dense, bt, pos, got, (x2, x0))
+
+
+def first_sum(pos, x0, r2, q, q1, q2, q3, t0, t1, t2, t3, qsum, held):
+    ring_sum(pos[PZ], (q, q1, q2, q3), qsum, held)
     for d, out in enumerate((t0, t1, t2, t3)):
         at = slice(d * NODE, (d + 1) * NODE)
-        out[:NODE] = (x0[at] + r2[at].astype(F32)).astype(out.dtype)
-        if d:
-            out[NODE : NODE + 32] = hi
-            out[NODE + 32 :] = lo
-
-
-def weight_sum(pos, r1, r2, r3, qt, qu, held):
-    qu[...] = ring_sum(pos[P2], qt[...], weight_parts((r1, r2, r3), NODE), held)
+        out[...] = (x0[at] + r2[at].astype(F32)).astype(out.dtype)
 
 
 def last_sum(t0, r1, r2, r3, out):
     s = t0[...]
     for r in (r1, r2, r3):
-        s += r[:NODE].astype(F32)
+        s += r[...].astype(F32)
     out[...] = s.T.astype(BF16)
 
 
-def weight_rows(pos, own, r1, r2, r3, out):
-    core = pos[PC]
-    for p, r in ((PY, own), (PY3, r1), (PY2, r2), (PY1, r3)):
-        for c, at in ((core, 0), (1 - core, 32)):
-            row = pl.multiple_of(pos[p] * 64 + c * 32, 32)
-            out[pl.ds(row, 32), :] = r[at : at + 32] * (1.0 / NODE)
+def weight_rows(pos, first, second, out):
+    for r, i, p in ((first, 0, PY), (first, 64, PX1), (second, 0, PX3), (second, 64, PY2)):
+        row = pl.multiple_of(pos[p] * 64, 64)
+        out[pl.ds(row, 64), :] = r[i : i + 64] * (1.0 / NODE)
 
 
 def send(v, axis, d, n=4):
     return lax.ppermute(v, axis, [(i, (i + d) % n) for i in range(n)])
+
+
+def swap(v, axis, step):
+    return lax.ppermute(v, axis, [(i, i ^ step) for i in range(4)])
 
 
 def send_by_core(v, stage, d):
@@ -290,11 +273,9 @@
 
 
 def body(features, cotangent, weight, tile_values, tile_rows, tile_cols, tile_count):
-    tv, rows, cols, count = tile_values[0, 0], tile_rows[0, 0], tile_cols[0, 0], tile_count[0]
+    tv, rows, cols, count = tile_values[0, 0], tile_rows, tile_cols, tile_count[0]
     z, x, core, y = (lax.axis_index(a) for a in ("z", "x", "core", "y"))
-    zero = core == 0
-    places = [z, x, core, jnp.where(zero, x, z), jnp.where(zero, z, x)]
-    places += [lax.rem(y + d, 4) for d in range(4)] + [y ^ 1, y ^ 3]
+    places = [z, x, core] + [lax.rem(y + d, 4) for d in range(4)] + [y ^ 1, y ^ 3]
     pos = jnp.stack(places).astype(jnp.int32)
     tv = pltpu.with_memory_space_constraint(tv, pltpu.HBM)
 
@@ -339,42 +320,46 @@
     )(pos, own, r3, weight, cotangent)
     r = {d: send(m, "y", d) for d, m in ((2, m2), (1, m1), (3, m3))}
 
-    piece = shape((32, FEAT), F32)
-    dense, other, bt, qown = dense_call(
+    piece = shape((64, FEAT), F32)
+    dense, other, bt, q = dense_call(
         backward_other_first,
-        [shape((8 * NODE + 32, FEAT), BF16), shape((4, FEAT, NODE), BF16), piece],
+        [shape((8 * NODE + 128, FEAT), BF16), shape((4, FEAT, NODE), BF16), piece],
         dense, pos, bt, r[1], r[2], r[3], q,
-        scratch=[pltpu.VMEM((64, FEAT), F32)],
     )
     got_first = send(other, "core", 1, 2)
     dense, other = dense_call(
         backward_other_last, [shape((8 * NODE, FEAT), BF16)], dense, pos, bt
     )
     got_last = send(other, "core", 1, 2)
-    long, longf = shape((4 * NODE + 64, FEAT), BF16), shape((4 * NODE, FEAT), F32)
-    dense, x1, x3, qs = dense_call(
-        backward_own_first, [long, long, piece], dense, pos, bt, got_first, qown
-    )
+    long, longf = shape((4 * NODE, FEAT), BF16), shape((4 * NODE, FEAT), F32)
+
+    held = [pltpu.VMEM((4, 64, FEAT), F32)]
+    dense, q, x1, x3 = dense_call(
+        backward_own_first, [piece, long, long], dense, pos, bt, got_first, q
+    )
+    along_x = [send(q, "x", d) for d in (1, 2, 3)]
     r1, r3 = send_by_core(x1, 0, 1), send_by_core(x3, 0, 3)
-    dense, x2, x0 = dense_call(backward_own_last, [long, longf], dense, pos, bt, got_last, qs)
+    dense, q, x2, x0 = dense_call(
+        backward_own_last,
+        [piece, long, longf],
+        dense, pos, bt, got_last, q, *along_x,
+        scratch=held,
+    )
     r2 = send_by_core(x2, 0, 2)
-    held = [pltpu.VMEM((4, 32, FEAT), F32)]
-    x0 = call(add_pair, longf, [VSPEC] * 3, nbytes=MIB)(x0, r1, r3)
-    t0, t1, t2, t3, qt = call(
+    x0 = call(add_two, longf, [VSPEC] * 3, nbytes=MIB)(x0, r1, r3)
+    t0, t1, t2, t3, q = call(
         first_sum,
-        [blockf, packed, packed, packed, piece],
-        [SSPEC] + [VSPEC] * 5,
+        [blockf, block, block, block, piece],
+        [SSPEC] + [VSPEC] * 6,
         held,
         nbytes=MIB,
-    )(pos, x0, r1, r2, r3, qs)
-    r1, r2, r3 = (send_by_core(v, 1, d) for d, v in ((1, t1), (2, t2), (3, t3)))
-    qu = call(weight_sum, piece, [SSPEC] + [VSPEC] * 4, held, nbytes=MIB // 4)(pos, r1, r2, r3, qt)
-    pair = jnp.concatenate([qu, send(qu, "core", 1, 2)], axis=0)
-    feature_grad = call(last_sum, block, [VSPEC] * 4, nbytes=MIB)(t0, r1, r2, r3)
-    r = {d: send(pair, "y", d) for d in (2, 1, 3)}
+    )(pos, x0, r2, q, *[send(q, "z", d) for d in (1, 2, 3)])
+    r = {d: send_by_core(v, 1, d) for d, v in ((2, t2), (1, t1), (3, t3))}
+    feature_grad = call(last_sum, block, [VSPEC] * 4, nbytes=MIB)(t0, r[1], r[2], r[3])
+    first = jnp.concatenate([q, swap(q, "y", 1)], axis=0)
     weight_grad = call(
-        weight_rows, shape((FEAT, FEAT), F32), [SSPEC] + [VSPEC] * 4, nbytes=MIB // 2
-    )(pos, pair, r[1], r[2], r[3])
+        weight_rows, shape((FEAT, FEAT), F32), [SSPEC, VSPEC, VSPEC], nbytes=MIB // 2
+    )(pos, first, swap(first, "y", 3))
     return activated, weight_grad, feature_grad
 
 

time: 106 us -> 102 us (0.962); the launches traced: 105 us -> 102 us
  waiting for transfers between devices: 37.3 us -> 29.8 us
  starting transfers between devices: 36.5 us -> 43.9 us
  Pallas kernels: 27.3 us -> 24.4 us
  other arithmetic: 2.34 us -> 0.94 us
  local copies, waits for them, and re-layouts: 0.2 us -> 1.57 us
    ppermute x12, waiting for transfers between devices: 21 us -> 9.87 us  [send_by_core(): return lax.ppermute(v, RING, pairs)]
    ppermute x0 -> x2, starting transfers between devices: none -> 3.44 us  [swap(): return lax.ppermute(v, axis, [(i, i ^ step) for i in range(4)])]
    ppermute x14 -> x16, starting transfers between devices: 15.9 us -> 18.5 us  [send(): return lax.ppermute(v, axis, [(i, (i + d) % n) for i in range(n)])]
    pallas_call x1, Pallas kernels: 7.86 us -> 5.44 us  [body(): call(dense_block, DENSE, [ASPEC, SSPEC, SSPEC, SSPEC], [pltpu.SemaphoreTy...]
    ppermute x0 -> x2, waiting for transfers between devices: none -> 1.87 us  [swap(): return lax.ppermute(v, axis, [(i, i ^ step) for i in range(4)])]
    ppermute x14 -> x16, waiting for transfers between devices: 16.3 us -> 18.1 us  [send(): return lax.ppermute(v, axis, [(i, (i + d) % n) for i in range(n)])]
    unnamed x2 -> x0, other arithmetic: 1.4 us -> none
    ppermute x12, starting transfers between devices: 20.6 us -> 21.9 us  [send_by_core(): return lax.ppermute(v, RING, pairs)]
  transfers between devices with their start and end apart: 26 -> 30, of which waited for: 17 -> 18; matrix products, arithmetic and copies ran while one was open for 1% -> 0% of each run, Pallas kernels for 19% -> 17%
where the time goes in v4:
time: 102 us
  starting transfers between devices  43.9 us (43%)
  waiting for transfers between devices  29.8 us (29%)
  Pallas kernels  24.4 us (24%)
  local copies, waits for them, and re-layouts  1.57 us (2%)
  between operations  1.47 us (1%)
    ppermute x12, starting transfers between devices, send_by_core(): return lax.ppermute(v, RING, pairs)  21.9 us
    ppermute x16, starting transfers between devices, send(): return lax.ppermute(v, axis, [(i, (i + d) % n) for i in range(n)])  18.5 us
    ppermute x16, waiting for transfers between devices, send(): return lax.ppermute(v, axis, [(i, (i + d) % n) for i in range(n)])  18.1 us
    pallas_call x8, Pallas kernels, dense_call(): call(wrapped, [DENSE] + outs, [SSPEC] + [VSPEC] * (n - 1), scratch, flops...  14.6 us
    ppermute x12, waiting for transfers between devices, send_by_core(): return lax.ppermute(v, RING, pairs)  9.87 us
    pallas_call x1, Pallas kernels, body(): call(dense_block, DENSE, [ASPEC, SSPEC, SSPEC, SSPEC], [pltpu.SemaphoreTy...  5.44 us
    ppermute x2, starting transfers between devices, swap(): return lax.ppermute(v, axis, [(i, i ^ step) for i in range(4)])  3.44 us
  transfers between devices with their start and end apart: 30, of which 18 were waited for; matrix products, arithmetic and copies ran while one was open for 0% of the time, Pallas kernels for 17%

profile of v4, /device:TPU:0, one launch (start us, length us, event | category | flops | bytes accessed | tf_op | source)
XLA Modules:
  0.0 102.1 jit_solution(12074617881036630983)
XLA Ops:
  0.6 3.2 %collective-permute-start.1 = (bf16[256,256]{1,0:T(8,128)(2,1)}, bf16[256,256]{1,0:T(8,128)(2,1)S(1)}, u32[]{:S(2)}, u32[]{:S(2)}) collective-permute-start(bf16[256,256]{1,0:T(8,128)(2,1)} %param.7), channel_id=1, source_target_pairs={{0,16},{4,68},{8,24},{12,76},{16,0},{20,84},{24,8},{28,92},{32,48}... | collective-permute-start | bytes 393224 | tf_op jit(solution)/shard_map/ppermute | solution.py:272
  9.0 2.4 %collective-permute-done.2 = bf16[256,256]{1,0:T(8,128)(2,1)S(1)} collective-permute-done((bf16[256,256]{1,0:T(8,128)(2,1)}, bf16[256,256]{1,0:T(8,128)(2,1)S(1)}, u32[]{:S(2)}, u32[]{:S(2)}) %collective-permute-start.2) | collective-permute-done | bytes 131104 | tf_op jit(solution)/shard_map/ppermute | solution.py:272
  12.4 2.0 %collective-permute-start.6 = (bf16[1024,256]{1,0:T(8,128)(2,1)S(1)}, bf16[1024,256]{1,0:T(8,128)(2,1)S(1)}, u32[]{:S(2)}, u32[]{:S(2)}) collective-permute-start(bf16[1024,256]{1,0:T(8,128)(2,1)S(1)} %pad_maximum_fusion.refs_2_), channel_id=1, source_target_pairs={{0,32},{4,12},{8,40},{12,20},{16,48},{20,28},{24,56},{28,4},{32,64... | collective-permute-start | bytes 1572872 | tf_op jit(solution)/shard_map/ppermute | solution.py:272
  14.4 3.6 %collective-permute-start.5 = (bf16[1024,256]{1,0:T(8,128)(2,1)S(1)}, bf16[1024,256]{1,0:T(8,128)(2,1)S(1)}, u32[]{:S(2)}, u32[]{:S(2)}) collective-permute-start(bf16[1024,256]{1,0:T(8,128)(2,1)S(1)} %pad_maximum_fusion.refs_2_), channel_id=1, source_target_pairs={{0,64},{4,20},{8,72},{12,28},{16,80},{20,4},{24,88},{28,12},{32,96... | collective-permute-start | bytes 1572872 | tf_op jit(solution)/shard_map/ppermute | solution.py:272
  21.0 5.4 %shard_map.94.refs_1_ = bf16[64,1024,128]{2,1,0:T(8,128)(2,1)S(1)} custom-call(bf16[384,128,128]{2,1,0:T(8,128)(2,1)} %bitcast.12, s32[1,1,384]{2,1,0:T(1,128)S(1)} %copy-done.2, s32[1,1,384]{2,1,0:T(1,128)S(1)} %copy-done.3, s32[1]{0:T(128)} %bitcast.11.count), custom_call_target="tpu_custom_call" | custom-call | bytes 25165824 | tf_op jit(solution)/shard_map/pallas_call | solution.py:287
  26.4 1.8 %shard_map.95 = (bf16[64,1024,128]{2,1,0:T(8,128)(2,1)S(1)}, f32[1024,256]{1,0:T(8,128)S(1)}) custom-call(s32[9]{0:T(128)S(1)} %stack.39.refs_0_.pos, bf16[64,1024,128]{2,1,0:T(8,128)(2,1)S(1)} %shard_map.94.refs_1_, bf16[1024,256]{1,0:T(8,128)(2,1)S(1)} %pad_maximum_fusion.refs_2_, ...), custom_call_target="tpu_custom_call", output_to_operand_aliasing={{0}: (1, {})} | custom-call | flops 16777216 | bytes 16777216 | tf_op jit(solution)/shard_map/pallas_call | solution.py:61
  28.2 2.5 %collective-permute-done.5 = bf16[1024,256]{1,0:T(8,128)(2,1)S(1)} collective-permute-done((bf16[1024,256]{1,0:T(8,128)(2,1)S(1)}, bf16[1024,256]{1,0:T(8,128)(2,1)S(1)}, u32[]{:S(2)}, u32[]{:S(2)}) %collective-permute-start.5) | collective-permute-done | bytes 524320 | tf_op jit(solution)/shard_map/ppermute | solution.py:272
  30.9 2.3 %shard_map.96 = (bf16[64,1024,128]{2,1,0:T(8,128)(2,1)S(1)}, f32[1024,256]{1,0:T(8,128)S(1)}) custom-call(s32[9]{0:T(128)S(1)} %stack.39.refs_0_.pos, bf16[64,1024,128]{2,1,0:T(8,128)(2,1)S(1)} %get-tuple-element.47.refs_1_, bf16[3072,256]{1,0:T(8,128)(2,1)S(1)} %constant_dynamic-update-slice_fusion.refs_2_, ...), custom_call_target="tpu_custom_call", output_to_operand_aliasing={{0}: (1, {})} | custom-call | flops 1000 | bytes 1000 | tf_op jit(solution)/shard_map/pallas_call | solution.py:61
  37.5 2.9 %collective-permute-start.9 = (bf16[256,256]{1,0:T(8,128)(2,1)S(1)}, bf16[256,256]{1,0:T(8,128)(2,1)S(1)}, u32[]{:S(2)}, u32[]{:S(2)}) collective-permute-start(bf16[256,256]{1,0:T(8,128)(2,1)S(1)} %get-tuple-element.58), channel_id=1, source_target_pairs={{0,2},{1,3},{2,0},{3,1},{4,6},{5,7},{6,4},{7,5},{8,10},{9,11},{10,... | collective-permute-start | bytes 393224 | tf_op jit(solution)/shard_map/ppermute | solution.py:255
  43.4 3.4 %collective-permute-done.9.r2 = bf16[256,256]{1,0:T(8,128)(2,1)S(1)} collective-permute-done((bf16[256,256]{1,0:T(8,128)(2,1)S(1)}, bf16[256,256]{1,0:T(8,128)(2,1)S(1)}, u32[]{:S(2)}, u32[]{:S(2)}) %collective-permute-start.9) | collective-permute-done | bytes 131104 | tf_op jit(solution)/shard_map/ppermute | solution.py:255
  48.4 1.7 %collective-permute-start.11 = (bf16[320,256]{1,0:T(8,128)(2,1)S(1)}, bf16[320,256]{1,0:T(8,128)(2,1)S(1)}, u32[]{:S(2)}, u32[]{:S(2)}) collective-permute-start(bf16[320,256]{1,0:T(8,128)(2,1)S(1)} %get-tuple-element.63), channel_id=1, source_target_pairs={{0,1},{1,2},{2,3},{3,0},{4,5},{5,6},{6,7},{7,4},{8,9},{9,10},{10,1... | collective-permute-start | bytes 491528 | tf_op jit(solution)/shard_map/ppermute | solution.py:255
  50.1 2.4 %collective-permute-start.12 = (bf16[320,256]{1,0:T(8,128)(2,1)S(1)}, bf16[320,256]{1,0:T(8,128)(2,1)S(1)}, u32[]{:S(2)}, u32[]{:S(2)}) collective-permute-start(bf16[320,256]{1,0:T(8,128)(2,1)S(1)} %get-tuple-element.64), channel_id=1, source_target_pairs={{0,2},{1,3},{2,0},{3,1},{4,6},{5,7},{6,4},{7,5},{8,10},{9,11},{10,... | collective-permute-start | bytes 491528 | tf_op jit(solution)/shard_map/ppermute | solution.py:255
  53.4 3.0 %collective-permute-done.11.refs_3_ = bf16[320,256]{1,0:T(8,128)(2,1)S(1)} collective-permute-done((bf16[320,256]{1,0:T(8,128)(2,1)S(1)}, bf16[320,256]{1,0:T(8,128)(2,1)S(1)}, u32[]{:S(2)}, u32[]{:S(2)}) %collective-permute-start.11) | collective-permute-done | bytes 163872 | tf_op jit(solution)/shard_map/ppermute | solution.py:255
  56.3 2.8 %collective-permute-done.12.refs_4_ = bf16[320,256]{1,0:T(8,128)(2,1)S(1)} collective-permute-done((bf16[320,256]{1,0:T(8,128)(2,1)S(1)}, bf16[320,256]{1,0:T(8,128)(2,1)S(1)}, u32[]{:S(2)}, u32[]{:S(2)}) %collective-permute-start.12) | collective-permute-done | bytes 163872 | tf_op jit(solution)/shard_map/ppermute | solution.py:255
  59.1 1.9 %shard_map.101 = (bf16[64,1024,128]{2,1,0:T(8,128)(2,1)S(1)}, bf16[2176,256]{1,0:T(8,128)(2,1)S(1)}, bf16[4,256,256]{2,1,0:T(8,128)(2,1)S(1)}, f32[64,256]{1,0:T(8,128)S(1)}) custom-call(s32[9]{0:T(128)S(1)} %stack.39.refs_0_.pos, bf16[64,1024,128]{2,1,0:T(8,128)(2,1)S(1)} %get-tuple-element.61.refs_1_, ...), custom_call_target="tpu_custom_call", output_to_operand_aliasing={{0}: (1, {})} | custom-call | flops 1000 | bytes 1000 | tf_op jit(solution)/shard_map/pallas_call | solution.py:61
  61.1 1.8 %shard_map.102 = (bf16[64,1024,128]{2,1,0:T(8,128)(2,1)S(1)}, bf16[2048,256]{1,0:T(8,128)(2,1)S(1)}) custom-call(s32[9]{0:T(128)S(1)} %stack.39.refs_0_.pos, bf16[64,1024,128]{2,1,0:T(8,128)(2,1)S(1)} %get-tuple-element.67.refs_1_, bf16[4,256,256]{2,1,0:T(8,128)(2,1)S(1)} %get-tuple-element.68.refs_2_), custom_call_target="tpu_custom_call", output_to_operand_aliasing={{0}: (1, {})} | custom-call | flops 1000 | bytes 1000 | tf_op jit(solution)/shard_map/pallas_call | solution.py:61
  63.8 1.9 %shard_map.103 = (bf16[64,1024,128]{2,1,0:T(8,128)(2,1)S(1)}, f32[64,256]{1,0:T(8,128)S(1)}, bf16[1024,256]{1,0:T(8,128)(2,1)S(1)}, bf16[1024,256]{1,0:T(8,128)(2,1)S(1)}) custom-call(s32[9]{0:T(128)S(1)} %stack.39.refs_0_.pos, bf16[64,1024,128]{2,1,0:T(8,128)(2,1)S(1)} %get-tuple-element.69.refs_1_, ...), custom_call_target="tpu_custom_call", output_to_operand_aliasing={{0}: (1, {})} | custom-call | flops 1000 | bytes 1000 | tf_op jit(solution)/shard_map/pallas_call | solution.py:61
  67.8 1.7 %collective-permute-start.19 = (bf16[1024,256]{1,0:T(8,128)(2,1)S(1)}, bf16[1024,256]{1,0:T(8,128)(2,1)S(1)}, u32[]{:S(2)}, u32[]{:S(2)}) collective-permute-start(bf16[1024,256]{1,0:T(8,128)(2,1)S(1)} %get-tuple-element.76), channel_id=1, source_target_pairs={{0,8},{4,36},{8,16},{12,44},{16,24},{20,52},{24,0},{28,60},{32,40}... | collective-permute-start | bytes 1572872 | tf_op jit(solution)/shard_map/ppermute | solution.py:272
  73.0 1.9 %shard_map.104 = (bf16[64,1024,128]{2,1,0:T(8,128)(2,1)S(1)}, f32[64,256]{1,0:T(8,128)S(1)}, bf16[1024,256]{1,0:T(8,128)(2,1)S(1)}, f32[1024,256]{1,0:T(8,128)S(1)}) custom-call(s32[9]{0:T(128)S(1)} %stack.39.refs_0_.pos, bf16[64,1024,128]{2,1,0:T(8,128)(2,1)S(1)} %get-tuple-element.72.refs_1_, ...), custom_call_target="tpu_custom_call", output_to_operand_aliasing={{0}: (1, {})} | custom-call | flops 1000 | bytes 1000 | tf_op jit(solution)/shard_map/pallas_call | solution.py:61
  76.2 3.3 %collective-permute-start.24 = (f32[64,256]{1,0:T(8,128)S(1)}, f32[64,256]{1,0:T(8,128)S(1)}, u32[]{:S(2)}, u32[]{:S(2)}) collective-permute-start(f32[64,256]{1,0:T(8,128)S(1)} %get-tuple-element.79.q), channel_id=1, source_target_pairs={{0,96},{32,0},{64,32},{96,64},{1,97},{33,1},{65,33},{97,65},{2,98}... | collective-permute-start | bytes 196616 | tf_op jit(solution)/shard_map/ppermute | solution.py:255
  80.9 4.6 %collective-permute-done.24.q3 = f32[64,256]{1,0:T(8,128)S(1)} collective-permute-done((f32[64,256]{1,0:T(8,128)S(1)}, f32[64,256]{1,0:T(8,128)S(1)}, u32[]{:S(2)}, u32[]{:S(2)}) %collective-permute-start.24) | collective-permute-done | bytes 65568 | tf_op jit(solution)/shard_map/ppermute | solution.py:255
  87.2 1.8 %collective-permute-start.25 = (f32[64,256]{1,0:T(8,128)S(1)}, f32[64,256]{1,0:T(8,128)S(1)}, u32[]{:S(2)}, u32[]{:S(2)}) collective-permute-start(f32[64,256]{1,0:T(8,128)S(1)} %get-tuple-element.80), channel_id=1, source_target_pairs={{0,1},{1,0},{2,3},{3,2},{4,5},{5,4},{6,7},{7,6},{8,9},{9,8},{10,11... | collective-permute-start | bytes 196616 | tf_op jit(solution)/shard_map/ppermute | solution.py:259
  89.9 3.4 %collective-permute-start.28 = (bf16[256,256]{1,0:T(8,128)(2,1)S(1)}, bf16[256,256]{1,0:T(8,128)(2,1)S(1)}, u32[]{:S(2)}, u32[]{:S(2)}) collective-permute-start(bf16[256,256]{1,0:T(8,128)(2,1)S(1)} %get-tuple-element.83), channel_id=1, source_target_pairs={{0,64},{4,20},{8,72},{12,28},{16,80},{20,4},{24,88},{28,12},{32,96... | collective-permute-start | bytes 393224 | tf_op jit(solution)/shard_map/ppermute | solution.py:272
  99.0 1.9 %collective-permute-done.26.second = f32[128,256]{1,0:T(8,128)S(1)} collective-permute-done((f32[128,256]{1,0:T(8,128)S(1)}, f32[128,256]{1,0:T(8,128)S(1)}, u32[]{:S(2)}, u32[]{:S(2)}) %collective-permute-start.26) | collective-permute-done | bytes 131104 | tf_op jit(solution)/shard_map/ppermute | solution.py:259
  (66 shorter events, 37.4 us)
Async XLA Ops:
  0.6 6.8 %collective-permute-start.1 = (bf16[256,256]{1,0:T(8,128)(2,1)}, bf16[256,256]{1,0:T(8,128)(2,1)S(1)}, u32[]{:S(2)}, u32[]{:S(2)}) collective-permute-start(bf16[256,256]{1,0:T(8,128)(2,1)} %param.7), channel_id=1, source_target_pairs={{0,16},{4,68},{8,24},{12,76},{16,0},{20,84},{24,8},{28,92},{32,48}... | collective-permute-start | bytes 393224 | tf_op jit(solution)/shard_map/ppermute | solution.py:272
  5.0 6.4 %collective-permute-start.2 = (bf16[256,256]{1,0:T(8,128)(2,1)}, bf16[256,256]{1,0:T(8,128)(2,1)S(1)}, u32[]{:S(2)}, u32[]{:S(2)}) collective-permute-start(bf16[256,256]{1,0:T(8,128)(2,1)} %param.7), channel_id=1, source_target_pairs={{0,8},{4,36},{8,16},{12,44},{16,24},{20,52},{24,0},{28,60},{32,40}... | collective-permute-start | bytes 393224 | tf_op jit(solution)/shard_map/ppermute | solution.py:272
  12.3 14.1 %collective-permute-start.3 = (bf16[1024,256]{1,0:T(8,128)(2,1)S(1)}, bf16[1024,256]{1,0:T(8,128)(2,1)S(1)}, u32[]{:S(2)}, u32[]{:S(2)}) collective-permute-start(bf16[1024,256]{1,0:T(8,128)(2,1)S(1)} %pad_maximum_fusion.refs_2_), channel_id=1, source_target_pairs={{0,4},{4,0},{1,5},{5,1},{2,6},{6,2},{3,7},{7,3},{8,12},{12,8},{9,1... | collective-permute-start | bytes 1572872 | tf_op jit(solution)/shard_map/ppermute | solution.py:255
  12.4 15.8 %collective-permute-start.6 = (bf16[1024,256]{1,0:T(8,128)(2,1)S(1)}, bf16[1024,256]{1,0:T(8,128)(2,1)S(1)}, u32[]{:S(2)}, u32[]{:S(2)}) collective-permute-start(bf16[1024,256]{1,0:T(8,128)(2,1)S(1)} %pad_maximum_fusion.refs_2_), channel_id=1, source_target_pairs={{0,32},{4,12},{8,40},{12,20},{16,48},{20,28},{24,56},{28,4},{32,64... | collective-permute-start | bytes 1572872 | tf_op jit(solution)/shard_map/ppermute | solution.py:272
  14.4 16.4 %collective-permute-start.5 = (bf16[1024,256]{1,0:T(8,128)(2,1)S(1)}, bf16[1024,256]{1,0:T(8,128)(2,1)S(1)}, u32[]{:S(2)}, u32[]{:S(2)}) collective-permute-start(bf16[1024,256]{1,0:T(8,128)(2,1)S(1)} %pad_maximum_fusion.refs_2_), channel_id=1, source_target_pairs={{0,64},{4,20},{8,72},{12,28},{16,80},{20,4},{24,88},{28,12},{32,96... | collective-permute-start | bytes 1572872 | tf_op jit(solution)/shard_map/ppermute | solution.py:272
  17.9 12.8 %collective-permute-start.4 = (bf16[1024,256]{1,0:T(8,128)(2,1)S(1)}, bf16[1024,256]{1,0:T(8,128)(2,1)S(1)}, u32[]{:S(2)}, u32[]{:S(2)}) collective-permute-start(bf16[1024,256]{1,0:T(8,128)(2,1)S(1)} %pad_maximum_fusion.refs_2_), channel_id=1, source_target_pairs={{0,96},{4,28},{8,104},{12,4},{16,112},{20,12},{24,120},{28,20},{32... | collective-permute-start | bytes 1572872 | tf_op jit(solution)/shard_map/ppermute | solution.py:272
  35.9 7.5 %collective-permute-start.8 = (bf16[256,256]{1,0:T(8,128)(2,1)S(1)}, bf16[256,256]{1,0:T(8,128)(2,1)S(1)}, u32[]{:S(2)}, u32[]{:S(2)}) collective-permute-start(bf16[256,256]{1,0:T(8,128)(2,1)S(1)} %get-tuple-element.57), channel_id=1, source_target_pairs={{0,1},{1,2},{2,3},{3,0},{4,5},{5,6},{6,7},{7,4},{8,9},{9,10},{10,1... | collective-permute-start | bytes 393224 | tf_op jit(solution)/shard_map/ppermute | solution.py:255
  37.5 9.2 %collective-permute-start.9 = (bf16[256,256]{1,0:T(8,128)(2,1)S(1)}, bf16[256,256]{1,0:T(8,128)(2,1)S(1)}, u32[]{:S(2)}, u32[]{:S(2)}) collective-permute-start(bf16[256,256]{1,0:T(8,128)(2,1)S(1)} %get-tuple-element.58), channel_id=1, source_target_pairs={{0,2},{1,3},{2,0},{3,1},{4,6},{5,7},{6,4},{7,5},{8,10},{9,11},{10,... | collective-permute-start | bytes 393224 | tf_op jit(solution)/shard_map/ppermute | solution.py:255
  48.4 7.9 %collective-permute-start.11 = (bf16[320,256]{1,0:T(8,128)(2,1)S(1)}, bf16[320,256]{1,0:T(8,128)(2,1)S(1)}, u32[]{:S(2)}, u32[]{:S(2)}) collective-permute-start(bf16[320,256]{1,0:T(8,128)(2,1)S(1)} %get-tuple-element.63), channel_id=1, source_target_pairs={{0,1},{1,2},{2,3},{3,0},{4,5},{5,6},{6,7},{7,4},{8,9},{9,10},{10,1... | collective-permute-start | bytes 491528 | tf_op jit(solution)/shard_map/ppermute | solution.py:255
  50.1 9.0 %collective-permute-start.12 = (bf16[320,256]{1,0:T(8,128)(2,1)S(1)}, bf16[320,256]{1,0:T(8,128)(2,1)S(1)}, u32[]{:S(2)}, u32[]{:S(2)}) collective-permute-start(bf16[320,256]{1,0:T(8,128)(2,1)S(1)} %get-tuple-element.64), channel_id=1, source_target_pairs={{0,2},{1,3},{2,0},{3,1},{4,6},{5,7},{6,4},{7,5},{8,10},{9,11},{10,... | collective-permute-start | bytes 491528 | tf_op jit(solution)/shard_map/ppermute | solution.py:255
  52.5 6.6 %collective-permute-start.13 = (bf16[320,256]{1,0:T(8,128)(2,1)S(1)}, bf16[320,256]{1,0:T(8,128)(2,1)S(1)}, u32[]{:S(2)}, u32[]{:S(2)}) collective-permute-start(bf16[320,256]{1,0:T(8,128)(2,1)S(1)} %get-tuple-element.65), channel_id=1, source_target_pairs={{0,3},{1,0},{2,1},{3,2},{4,7},{5,4},{6,5},{7,6},{8,11},{9,8},{10,9... | collective-permute-start | bytes 491528 | tf_op jit(solution)/shard_map/ppermute | solution.py:255
  62.9 6.6 %collective-permute-start.15 = (bf16[2048,256]{1,0:T(8,128)(2,1)S(1)}, bf16[2048,256]{1,0:T(8,128)(2,1)S(1)}, u32[]{:S(2)}, u32[]{:S(2)}) collective-permute-start(bf16[2048,256]{1,0:T(8,128)(2,1)S(1)} %get-tuple-element.73), channel_id=1, source_target_pairs={{0,4},{4,0},{1,5},{5,1},{2,6},{6,2},{3,7},{7,3},{8,12},{12,8},{9,1... | collective-permute-start | bytes 3145736 | tf_op jit(solution)/shard_map/ppermute | solution.py:255
  66.0 5.9 %collective-permute-start.17 = (f32[64,256]{1,0:T(8,128)S(1)}, f32[64,256]{1,0:T(8,128)S(1)}, u32[]{:S(2)}, u32[]{:S(2)}) collective-permute-start(f32[64,256]{1,0:T(8,128)S(1)} %get-tuple-element.74.refs_4_), channel_id=1, source_target_pairs={{0,16},{8,24},{16,0},{24,8},{1,17},{9,25},{17,1},{25,9},{2,18},{10... | collective-permute-start | bytes 196616 | tf_op jit(solution)/shard_map/ppermute | solution.py:255
  67.5 5.5 %collective-permute-start.16 = (f32[64,256]{1,0:T(8,128)S(1)}, f32[64,256]{1,0:T(8,128)S(1)}, u32[]{:S(2)}, u32[]{:S(2)}) collective-permute-start(f32[64,256]{1,0:T(8,128)S(1)} %get-tuple-element.74.refs_4_), channel_id=1, source_target_pairs={{0,8},{8,16},{16,24},{24,0},{1,9},{9,17},{17,25},{25,1},{2,10},{10... | collective-permute-start | bytes 196616 | tf_op jit(solution)/shard_map/ppermute | solution.py:255
  67.8 12.0 %collective-permute-start.19 = (bf16[1024,256]{1,0:T(8,128)(2,1)S(1)}, bf16[1024,256]{1,0:T(8,128)(2,1)S(1)}, u32[]{:S(2)}, u32[]{:S(2)}) collective-permute-start(bf16[1024,256]{1,0:T(8,128)(2,1)S(1)} %get-tuple-element.76), channel_id=1, source_target_pairs={{0,8},{4,36},{8,16},{12,44},{16,24},{20,52},{24,0},{28,60},{32,40}... | collective-permute-start | bytes 1572872 | tf_op jit(solution)/shard_map/ppermute | solution.py:272
  69.5 11.2 %collective-permute-start.20 = (bf16[1024,256]{1,0:T(8,128)(2,1)S(1)}, bf16[1024,256]{1,0:T(8,128)(2,1)S(1)}, u32[]{:S(2)}, u32[]{:S(2)}) collective-permute-start(bf16[1024,256]{1,0:T(8,128)(2,1)S(1)} %get-tuple-element.77), channel_id=1, source_target_pairs={{0,24},{4,100},{8,0},{12,108},{16,8},{20,116},{24,16},{28,124},{32... | collective-permute-start | bytes 1572872 | tf_op jit(solution)/shard_map/ppermute | solution.py:272
  74.8 11.7 %collective-permute-start.21 = (bf16[1024,256]{1,0:T(8,128)(2,1)S(1)}, bf16[1024,256]{1,0:T(8,128)(2,1)S(1)}, u32[]{:S(2)}, u32[]{:S(2)}) collective-permute-start(bf16[1024,256]{1,0:T(8,128)(2,1)S(1)} %get-tuple-element.78), channel_id=1, source_target_pairs={{0,16},{4,68},{8,24},{12,76},{16,0},{20,84},{24,8},{28,92},{32,48}... | collective-permute-start | bytes 1572872 | tf_op jit(solution)/shard_map/ppermute | solution.py:272
  76.2 9.4 %collective-permute-start.24 = (f32[64,256]{1,0:T(8,128)S(1)}, f32[64,256]{1,0:T(8,128)S(1)}, u32[]{:S(2)}, u32[]{:S(2)}) collective-permute-start(f32[64,256]{1,0:T(8,128)S(1)} %get-tuple-element.79.q), channel_id=1, source_target_pairs={{0,96},{32,0},{64,32},{96,64},{1,97},{33,1},{65,33},{97,65},{2,98}... | collective-permute-start | bytes 196616 | tf_op jit(solution)/shard_map/ppermute | solution.py:255
  79.5 6.4 %collective-permute-start.23 = (f32[64,256]{1,0:T(8,128)S(1)}, f32[64,256]{1,0:T(8,128)S(1)}, u32[]{:S(2)}, u32[]{:S(2)}) collective-permute-start(f32[64,256]{1,0:T(8,128)S(1)} %get-tuple-element.79.q), channel_id=1, source_target_pairs={{0,64},{32,96},{64,0},{96,32},{1,65},{33,97},{65,1},{97,33},{2,66}... | collective-permute-start | bytes 196616 | tf_op jit(solution)/shard_map/ppermute | solution.py:255
  79.8 6.8 %collective-permute-start.22 = (f32[64,256]{1,0:T(8,128)S(1)}, f32[64,256]{1,0:T(8,128)S(1)}, u32[]{:S(2)}, u32[]{:S(2)}) collective-permute-start(f32[64,256]{1,0:T(8,128)S(1)} %get-tuple-element.79.q), channel_id=1, source_target_pairs={{0,32},{32,64},{64,96},{96,0},{1,33},{33,65},{65,97},{97,1},{2,34}... | collective-permute-start | bytes 196616 | tf_op jit(solution)/shard_map/ppermute | solution.py:255
  87.2 7.4 %collective-permute-start.25 = (f32[64,256]{1,0:T(8,128)S(1)}, f32[64,256]{1,0:T(8,128)S(1)}, u32[]{:S(2)}, u32[]{:S(2)}) collective-permute-start(f32[64,256]{1,0:T(8,128)S(1)} %get-tuple-element.80), channel_id=1, source_target_pairs={{0,1},{1,0},{2,3},{3,2},{4,5},{5,4},{6,7},{7,6},{8,9},{9,8},{10,11... | collective-permute-start | bytes 196616 | tf_op jit(solution)/shard_map/ppermute | solution.py:259
  89.0 7.2 %collective-permute-start.27 = (bf16[256,256]{1,0:T(8,128)(2,1)S(1)}, bf16[256,256]{1,0:T(8,128)(2,1)S(1)}, u32[]{:S(2)}, u32[]{:S(2)}) collective-permute-start(bf16[256,256]{1,0:T(8,128)(2,1)S(1)} %get-tuple-element.82), channel_id=1, source_target_pairs={{0,32},{4,12},{8,40},{12,20},{16,48},{20,28},{24,56},{28,4},{32,64... | collective-permute-start | bytes 393224 | tf_op jit(solution)/shard_map/ppermute | solution.py:272
  89.9 7.7 %collective-permute-start.28 = (bf16[256,256]{1,0:T(8,128)(2,1)S(1)}, bf16[256,256]{1,0:T(8,128)(2,1)S(1)}, u32[]{:S(2)}, u32[]{:S(2)}) collective-permute-start(bf16[256,256]{1,0:T(8,128)(2,1)S(1)} %get-tuple-element.83), channel_id=1, source_target_pairs={{0,64},{4,20},{8,72},{12,28},{16,80},{20,4},{24,88},{28,12},{32,96... | collective-permute-start | bytes 393224 | tf_op jit(solution)/shard_map/ppermute | solution.py:272
  94.6 6.3 %collective-permute-start.26 = (f32[128,256]{1,0:T(8,128)S(1)}, f32[128,256]{1,0:T(8,128)S(1)}, u32[]{:S(2)}, u32[]{:S(2)}) collective-permute-start(f32[128,256]{1,0:T(8,128)S(1)} %constant_dynamic-update-slice_fusion.3.first), channel_id=1, source_target_pairs={{0,3},{1,2},{2,1},{3,0},{4,7},{5,6},{6,5},{7,4},{8,11},{9,10},{10,... | collective-permute-start | bytes 393224 | tf_op jit(solution)/shard_map/ppermute | solution.py:259
  (10 other events, 41.4 us)

commit v5 on v4

--- a/solution.py
+++ b/solution.py
@@ -69,8 +69,26 @@
     )(pos, in_vmem(dense), *rest)
 
 
-def dense_block(tv, rows, cols, count, dense, sem):
-    def copy(s):
+def dense_zeros(pos, dense):
+    del pos
+
+    @pl.loop(0, NCT)
+    def _(c):
+        dense[c] = jnp.zeros((ROWS, TILE), BF16)
+
+
+def dense_block(tv, rows_in, cols_in, count, given, dense, rows, cols, sem, sem_rows, sem_cols):
+    del given
+    index_copies = (
+        pltpu.make_async_copy(rows_in, rows, sem_rows),
+        pltpu.make_async_copy(cols_in, cols, sem_cols),
+    )
+    for copy in index_copies:
+        copy.start()
+    for copy in index_copies:
+        copy.wait()
+
+    def tile(s):
         return pltpu.make_async_copy(
             tv.at[s],
             dense.at[cols[0, 0, s], pl.ds(pl.multiple_of(rows[0, 0, s] * TILE, TILE), TILE), :],
@@ -78,16 +96,12 @@
         )
 
     def start(s, _):
-        copy(s).start()
+        tile(s).start()
         return 0
 
     def wait(s, _):
-        copy(s).wait()
+        tile(s).wait()
         return 0
-
-    @pl.loop(0, NCT)
-    def _(c):
-        dense[c] = jnp.zeros((ROWS, TILE), BF16)
 
     lax.fori_loop(0, count[0], start, 0)
     lax.fori_loop(0, count[0], wait, 0)
@@ -119,9 +133,12 @@
     )
 
 
+FAR = (1, 3, 2)
+
+
 def far_sum(total, dense, pos, core, far, rows):
-    for d in range(1, 4):
-        rhs = far[(d - 1) * ROWS : d * ROWS]
+    for i, d in enumerate(FAR):
+        rhs = far[i * ROWS : (i + 1) * ROWS]
         total += jnp.dot(tiles_of(dense, pos, core, d, rows), rhs, preferred_element_type=F32)
     return total
 
@@ -277,24 +294,26 @@
     z, x, core, y = (lax.axis_index(a) for a in ("z", "x", "core", "y"))
     places = [z, x, core] + [lax.rem(y + d, 4) for d in range(4)] + [y ^ 1, y ^ 3]
     pos = jnp.stack(places).astype(jnp.int32)
-    tv = pltpu.with_memory_space_constraint(tv, pltpu.HBM)
+    tv, rows, cols = (pltpu.with_memory_space_constraint(v, pltpu.HBM) for v in (tv, rows, cols))
 
     near = {d: send_by_core(features, 0, -d) for d in (2, 1, 3)}
     near = jnp.concatenate([features] + [near[d] for d in (1, 2, 3)], axis=0)
-    near, count, pos = lax.optimization_barrier((near, count, pos))
-    far = {d: send_by_core(near, 1, -d) for d in (2, 1, 3)}
+    dense = call(dense_zeros, DENSE, [SSPEC], nbytes=16 * MIB)(pos)
+    near, count, pos, dense = lax.optimization_barrier((near, count, pos, dense))
+    far = [send_by_core(near, 1, -d) for d in FAR]
     near_other = send(near, "core", 1, 2)
     dense = call(
         dense_block,
         DENSE,
-        [ASPEC, SSPEC, SSPEC, SSPEC],
-        [pltpu.SemaphoreType.DMA],
+        [ASPEC, ASPEC, ASPEC, SSPEC, VSPEC],
+        [pltpu.SMEM((1, 1, CAP), jnp.int32)] * 2 + [pltpu.SemaphoreType.DMA] * 3,
         nbytes=24 * MIB,
-    )(tv, rows, cols, count)
+        aliases={4: 0},
+    )(tv, rows, cols, count, in_vmem(dense))
     sums = shape((ROWS, FEAT), F32)
     dense, acc = dense_call(forward_near, [sums], dense, pos, near, near_other, cost=16 * MIB)
     far, acc = lax.optimization_barrier((far, acc))
-    far = jnp.concatenate([far[d] for d in (1, 2, 3)], axis=0)
+    far = jnp.concatenate(far, axis=0)
     far_other = send(far, "core", 1, 2)
     dense, acc = dense_call(forward_own, [sums], dense, pos, far, acc)
     block, blockf = shape((NODE, FEAT), BF16), shape((NODE, FEAT), F32)

time: 102 us -> 101 us (level)
  starting transfers between devices: 43.9 us -> 42.5 us
  local copies, waits for them, and re-layouts: 1.57 us -> 0.22 us
  Pallas kernels: 24.4 us -> 25.7 us
    pallas_call x1 -> x2, Pallas kernels: 5.44 us -> 6.96 us  [the longest x1 4.19 us: body(): call(dense_block, DENSE, [ASPEC, ASPEC, ASPEC, SSPEC, VSPEC], [pltpu.SMEM...]
    unnamed x11 -> x9, local copies, waits for them, and re-layouts: 1.44 us -> 0.09 us
    ppermute x12, waiting for transfers between devices: 9.87 us -> 8.71 us  [send_by_core(): return lax.ppermute(v, RING, pairs)]
    ppermute x16, waiting for transfers between devices: 18.1 us -> 19.3 us  [send(): return lax.ppermute(v, axis, [(i, (i + d) % n) for i in range(n)])]
    ppermute x16, starting transfers between devices: 18.5 us -> 17.5 us  [send(): return lax.ppermute(v, axis, [(i, (i + d) % n) for i in range(n)])]
  transfers between devices with their start and end apart: 30 -> 30, of which waited for: 18 -> 18; matrix products, arithmetic and copies ran while one was open for 0% -> 0% of each run, Pallas kernels for 17% -> 19%
where the time goes in v5:
time: 101 us; the launch traced here: 100 us
  starting transfers between devices  42.5 us (42%)
  waiting for transfers between devices  30.4 us (30%)
  Pallas kernels  25.7 us (25%)
  between operations  1.48 us (1%)
    ppermute x12, starting transfers between devices, send_by_core(): return lax.ppermute(v, RING, pairs)  21.7 us
    ppermute x16, waiting for transfers between devices, send(): return lax.ppermute(v, axis, [(i, (i + d) % n) for i in range(n)])  19.3 us
    ppermute x16, starting transfers between devices, send(): return lax.ppermute(v, axis, [(i, (i + d) % n) for i in range(n)])  17.5 us
    pallas_call x8, Pallas kernels, dense_call(): call(wrapped, [DENSE] + outs, [SSPEC] + [VSPEC] * (n - 1), scratch, flops...  14.4 us
    ppermute x12, waiting for transfers between devices, send_by_core(): return lax.ppermute(v, RING, pairs)  8.71 us
    pallas_call x1, Pallas kernels, body(): call(dense_block, DENSE, [ASPEC, ASPEC, ASPEC, SSPEC, VSPEC], [pltpu.SMEM...  4.19 us
    ppermute x2, starting transfers between devices, swap(): return lax.ppermute(v, axis, [(i, i ^ step) for i in range(4)])  3.41 us
    pallas_call x1, Pallas kernels, body(): dense = call(dense_zeros, DENSE, [SSPEC], nbytes=16 * MIB)(pos)  2.77 us
  transfers between devices with their start and end apart: 30, of which 18 were waited for; matrix products, arithmetic and copies ran while one was open for 0% of the time, Pallas kernels for 19%

profile of v5, /device:TPU:0, one launch (start us, length us, event | category | flops | bytes accessed | tf_op | source)
XLA Modules:
  0.0 100.4 jit_solution(18147290993238000025)
XLA Ops:
  0.6 3.2 %collective-permute-start.1 = (bf16[256,256]{1,0:T(8,128)(2,1)}, bf16[256,256]{1,0:T(8,128)(2,1)S(1)}, u32[]{:S(2)}, u32[]{:S(2)}) collective-permute-start(bf16[256,256]{1,0:T(8,128)(2,1)} %param.7), channel_id=1, source_target_pairs={{0,16},{4,68},{8,24},{12,76},{16,0},{20,84},{24,8},{28,92},{32,48}... | collective-permute-start | bytes 393224 | tf_op jit(solution)/shard_map/ppermute | solution.py:289
  5.9 2.8 %shard_map.94.given = bf16[64,1024,128]{2,1,0:T(8,128)(2,1)S(1)} custom-call(s32[9]{0:T(128)S(1)} %stack.39.pos.refs_0_), custom_call_target="tpu_custom_call" | custom-call | bytes 16777216 | tf_op jit(solution)/shard_map/pallas_call | solution.py:301
  9.0 2.4 %collective-permute-done.2 = bf16[256,256]{1,0:T(8,128)(2,1)S(1)} collective-permute-done((bf16[256,256]{1,0:T(8,128)(2,1)}, bf16[256,256]{1,0:T(8,128)(2,1)S(1)}, u32[]{:S(2)}, u32[]{:S(2)}) %collective-permute-start.2) | collective-permute-done | bytes 131104 | tf_op jit(solution)/shard_map/ppermute | solution.py:289
  11.5 4.0 %collective-permute-start.6 = (bf16[1024,256]{1,0:T(8,128)(2,1)S(1)}, bf16[1024,256]{1,0:T(8,128)(2,1)S(1)}, u32[]{:S(2)}, u32[]{:S(2)}) collective-permute-start(bf16[1024,256]{1,0:T(8,128)(2,1)S(1)} %pad_maximum_fusion.refs_2_), channel_id=1, source_target_pairs={{0,64},{4,20},{8,72},{12,28},{16,80},{20,4},{24,88},{28,12},{32,96... | collective-permute-start | bytes 1572872 | tf_op jit(solution)/shard_map/ppermute | solution.py:289
  16.5 2.2 %collective-permute-start.4 = (bf16[1024,256]{1,0:T(8,128)(2,1)S(1)}, bf16[1024,256]{1,0:T(8,128)(2,1)S(1)}, u32[]{:S(2)}, u32[]{:S(2)}) collective-permute-start(bf16[1024,256]{1,0:T(8,128)(2,1)S(1)} %pad_maximum_fusion.refs_2_), channel_id=1, source_target_pairs={{0,96},{4,28},{8,104},{12,4},{16,112},{20,12},{24,120},{28,20},{32... | collective-permute-start | bytes 1572872 | tf_op jit(solution)/shard_map/ppermute | solution.py:289
  19.3 4.2 %shard_map.95.refs_1_ = bf16[64,1024,128]{2,1,0:T(8,128)(2,1)S(1)} custom-call(bf16[384,128,128]{2,1,0:T(8,128)(2,1)} %bitcast.12, s32[1,1,384]{2,1,0:T(1,128)} %rows_in.1, s32[1,1,384]{2,1,0:T(1,128)} %cols_in.1, s32[1]{0:T(128)} %bitcast.11.count, bf16[64,1024,128]{2,1,0:T(8,128)(2,1)S(1)} %shard_map.94.given), custom_call_target="tpu_custom_call", output_to_operand_aliasing={{}: (4, {})} | custom-call | bytes 25165824 | tf_op jit(solution)/shard_map/pallas_call | solution.py:305
  23.5 1.8 %shard_map.96 = (bf16[64,1024,128]{2,1,0:T(8,128)(2,1)S(1)}, f32[1024,256]{1,0:T(8,128)S(1)}) custom-call(s32[9]{0:T(128)S(1)} %stack.39.pos.refs_0_, bf16[64,1024,128]{2,1,0:T(8,128)(2,1)S(1)} %shard_map.95.refs_1_, bf16[1024,256]{1,0:T(8,128)(2,1)S(1)} %pad_maximum_fusion.refs_2_, ...), custom_call_target="tpu_custom_call", output_to_operand_aliasing={{0}: (1, {})} | custom-call | flops 16777216 | bytes 16777216 | tf_op jit(solution)/shard_map/pallas_call | solution.py:61
  25.3 2.9 %collective-permute-done.5 = bf16[1024,256]{1,0:T(8,128)(2,1)S(1)} collective-permute-done((bf16[1024,256]{1,0:T(8,128)(2,1)S(1)}, bf16[1024,256]{1,0:T(8,128)(2,1)S(1)}, u32[]{:S(2)}, u32[]{:S(2)}) %collective-permute-start.5) | collective-permute-done | bytes 524320 | tf_op jit(solution)/shard_map/ppermute | solution.py:289
  29.5 2.3 %shard_map.97 = (bf16[64,1024,128]{2,1,0:T(8,128)(2,1)S(1)}, f32[1024,256]{1,0:T(8,128)S(1)}) custom-call(s32[9]{0:T(128)S(1)} %stack.39.pos.refs_0_, bf16[64,1024,128]{2,1,0:T(8,128)(2,1)S(1)} %get-tuple-element.49.refs_1_, bf16[3072,256]{1,0:T(8,128)(2,1)S(1)} %constant_dynamic-update-slice_fusion.refs_2_, ...), custom_call_target="tpu_custom_call", output_to_operand_aliasing={{0}: (1, {})} | custom-call | flops 1000 | bytes 1000 | tf_op jit(solution)/shard_map/pallas_call | solution.py:61
  36.1 2.9 %collective-permute-start.9 = (bf16[256,256]{1,0:T(8,128)(2,1)S(1)}, bf16[256,256]{1,0:T(8,128)(2,1)S(1)}, u32[]{:S(2)}, u32[]{:S(2)}) collective-permute-start(bf16[256,256]{1,0:T(8,128)(2,1)S(1)} %get-tuple-element.60), channel_id=1, source_target_pairs={{0,2},{1,3},{2,0},{3,1},{4,6},{5,7},{6,4},{7,5},{8,10},{9,11},{10,... | collective-permute-start | bytes 393224 | tf_op jit(solution)/shard_map/ppermute | solution.py:272
  41.9 3.4 %collective-permute-done.9.r2 = bf16[256,256]{1,0:T(8,128)(2,1)S(1)} collective-permute-done((bf16[256,256]{1,0:T(8,128)(2,1)S(1)}, bf16[256,256]{1,0:T(8,128)(2,1)S(1)}, u32[]{:S(2)}, u32[]{:S(2)}) %collective-permute-start.9) | collective-permute-done | bytes 131104 | tf_op jit(solution)/shard_map/ppermute | solution.py:272
  48.7 2.3 %collective-permute-start.12 = (bf16[320,256]{1,0:T(8,128)(2,1)S(1)}, bf16[320,256]{1,0:T(8,128)(2,1)S(1)}, u32[]{:S(2)}, u32[]{:S(2)}) collective-permute-start(bf16[320,256]{1,0:T(8,128)(2,1)S(1)} %get-tuple-element.66), channel_id=1, source_target_pairs={{0,2},{1,3},{2,0},{3,1},{4,6},{5,7},{6,4},{7,5},{8,10},{9,11},{10,... | collective-permute-start | bytes 491528 | tf_op jit(solution)/shard_map/ppermute | solution.py:272
  51.9 2.9 %collective-permute-done.11.refs_3_ = bf16[320,256]{1,0:T(8,128)(2,1)S(1)} collective-permute-done((bf16[320,256]{1,0:T(8,128)(2,1)S(1)}, bf16[320,256]{1,0:T(8,128)(2,1)S(1)}, u32[]{:S(2)}, u32[]{:S(2)}) %collective-permute-start.11) | collective-permute-done | bytes 163872 | tf_op jit(solution)/shard_map/ppermute | solution.py:272
  54.8 2.8 %collective-permute-done.12.refs_4_ = bf16[320,256]{1,0:T(8,128)(2,1)S(1)} collective-permute-done((bf16[320,256]{1,0:T(8,128)(2,1)S(1)}, bf16[320,256]{1,0:T(8,128)(2,1)S(1)}, u32[]{:S(2)}, u32[]{:S(2)}) %collective-permute-start.12) | collective-permute-done | bytes 163872 | tf_op jit(solution)/shard_map/ppermute | solution.py:272
  57.6 1.8 %shard_map.102 = (bf16[64,1024,128]{2,1,0:T(8,128)(2,1)S(1)}, bf16[2176,256]{1,0:T(8,128)(2,1)S(1)}, bf16[4,256,256]{2,1,0:T(8,128)(2,1)S(1)}, f32[64,256]{1,0:T(8,128)S(1)}) custom-call(s32[9]{0:T(128)S(1)} %stack.39.pos.refs_0_, bf16[64,1024,128]{2,1,0:T(8,128)(2,1)S(1)} %get-tuple-element.63.refs_1_, ...), custom_call_target="tpu_custom_call", output_to_operand_aliasing={{0}: (1, {})} | custom-call | flops 1000 | bytes 1000 | tf_op jit(solution)/shard_map/pallas_call | solution.py:61
  59.6 1.8 %shard_map.103 = (bf16[64,1024,128]{2,1,0:T(8,128)(2,1)S(1)}, bf16[2048,256]{1,0:T(8,128)(2,1)S(1)}) custom-call(s32[9]{0:T(128)S(1)} %stack.39.pos.refs_0_, bf16[64,1024,128]{2,1,0:T(8,128)(2,1)S(1)} %get-tuple-element.69.refs_1_, bf16[4,256,256]{2,1,0:T(8,128)(2,1)S(1)} %get-tuple-element.70.refs_2_), custom_call_target="tpu_custom_call", output_to_operand_aliasing={{0}: (1, {})} | custom-call | flops 1000 | bytes 1000 | tf_op jit(solution)/shard_map/pallas_call | solution.py:61
  62.3 1.8 %shard_map.104 = (bf16[64,1024,128]{2,1,0:T(8,128)(2,1)S(1)}, f32[64,256]{1,0:T(8,128)S(1)}, bf16[1024,256]{1,0:T(8,128)(2,1)S(1)}, bf16[1024,256]{1,0:T(8,128)(2,1)S(1)}) custom-call(s32[9]{0:T(128)S(1)} %stack.39.pos.refs_0_, bf16[64,1024,128]{2,1,0:T(8,128)(2,1)S(1)} %get-tuple-element.71.refs_1_, ...), custom_call_target="tpu_custom_call", output_to_operand_aliasing={{0}: (1, {})} | custom-call | flops 1000 | bytes 1000 | tf_op jit(solution)/shard_map/pallas_call | solution.py:61
  66.2 1.7 %collective-permute-start.19 = (bf16[1024,256]{1,0:T(8,128)(2,1)S(1)}, bf16[1024,256]{1,0:T(8,128)(2,1)S(1)}, u32[]{:S(2)}, u32[]{:S(2)}) collective-permute-start(bf16[1024,256]{1,0:T(8,128)(2,1)S(1)} %get-tuple-element.78), channel_id=1, source_target_pairs={{0,8},{4,36},{8,16},{12,44},{16,24},{20,52},{24,0},{28,60},{32,40}... | collective-permute-start | bytes 1572872 | tf_op jit(solution)/shard_map/ppermute | solution.py:289
  71.4 1.8 %shard_map.105 = (bf16[64,1024,128]{2,1,0:T(8,128)(2,1)S(1)}, f32[64,256]{1,0:T(8,128)S(1)}, bf16[1024,256]{1,0:T(8,128)(2,1)S(1)}, f32[1024,256]{1,0:T(8,128)S(1)}) custom-call(s32[9]{0:T(128)S(1)} %stack.39.pos.refs_0_, bf16[64,1024,128]{2,1,0:T(8,128)(2,1)S(1)} %get-tuple-element.74.refs_1_, ...), custom_call_target="tpu_custom_call", output_to_operand_aliasing={{0}: (1, {})} | custom-call | flops 1000 | bytes 1000 | tf_op jit(solution)/shard_map/pallas_call | solution.py:61
  74.6 2.6 %collective-permute-start.24 = (f32[64,256]{1,0:T(8,128)S(1)}, f32[64,256]{1,0:T(8,128)S(1)}, u32[]{:S(2)}, u32[]{:S(2)}) collective-permute-start(f32[64,256]{1,0:T(8,128)S(1)} %get-tuple-element.81.q), channel_id=1, source_target_pairs={{0,96},{32,0},{64,32},{96,64},{1,97},{33,1},{65,33},{97,65},{2,98}... | collective-permute-start | bytes 196616 | tf_op jit(solution)/shard_map/ppermute | solution.py:272
  78.2 5.0 %collective-permute-done.24.q3 = f32[64,256]{1,0:T(8,128)S(1)} collective-permute-done((f32[64,256]{1,0:T(8,128)S(1)}, f32[64,256]{1,0:T(8,128)S(1)}, u32[]{:S(2)}, u32[]{:S(2)}) %collective-permute-start.24) | collective-permute-done | bytes 65568 | tf_op jit(solution)/shard_map/ppermute | solution.py:272
  85.7 1.8 %collective-permute-start.25 = (f32[64,256]{1,0:T(8,128)S(1)}, f32[64,256]{1,0:T(8,128)S(1)}, u32[]{:S(2)}, u32[]{:S(2)}) collective-permute-start(f32[64,256]{1,0:T(8,128)S(1)} %get-tuple-element.82), channel_id=1, source_target_pairs={{0,1},{1,0},{2,3},{3,2},{4,5},{5,4},{6,7},{7,6},{8,9},{9,8},{10,11... | collective-permute-start | bytes 196616 | tf_op jit(solution)/shard_map/ppermute | solution.py:276
  87.8 3.1 %collective-permute-start.28 = (bf16[256,256]{1,0:T(8,128)(2,1)S(1)}, bf16[256,256]{1,0:T(8,128)(2,1)S(1)}, u32[]{:S(2)}, u32[]{:S(2)}) collective-permute-start(bf16[256,256]{1,0:T(8,128)(2,1)S(1)} %get-tuple-element.85), channel_id=1, source_target_pairs={{0,64},{4,20},{8,72},{12,28},{16,80},{20,4},{24,88},{28,12},{32,96... | collective-permute-start | bytes 393224 | tf_op jit(solution)/shard_map/ppermute | solution.py:289
  96.7 2.4 %collective-permute-done.26.second = f32[128,256]{1,0:T(8,128)S(1)} collective-permute-done((f32[128,256]{1,0:T(8,128)S(1)}, f32[128,256]{1,0:T(8,128)S(1)}, u32[]{:S(2)}, u32[]{:S(2)}) %collective-permute-start.26) | collective-permute-done | bytes 131104 | tf_op jit(solution)/shard_map/ppermute | solution.py:276
  (65 shorter events, 35.0 us)
Async XLA Ops:
  0.6 8.1 %collective-permute-start.1 = (bf16[256,256]{1,0:T(8,128)(2,1)}, bf16[256,256]{1,0:T(8,128)(2,1)S(1)}, u32[]{:S(2)}, u32[]{:S(2)}) collective-permute-start(bf16[256,256]{1,0:T(8,128)(2,1)} %param.7), channel_id=1, source_target_pairs={{0,16},{4,68},{8,24},{12,76},{16,0},{20,84},{24,8},{28,92},{32,48}... | collective-permute-start | bytes 393224 | tf_op jit(solution)/shard_map/ppermute | solution.py:289
  5.0 6.4 %collective-permute-start.2 = (bf16[256,256]{1,0:T(8,128)(2,1)}, bf16[256,256]{1,0:T(8,128)(2,1)S(1)}, u32[]{:S(2)}, u32[]{:S(2)}) collective-permute-start(bf16[256,256]{1,0:T(8,128)(2,1)} %param.7), channel_id=1, source_target_pairs={{0,8},{4,36},{8,16},{12,44},{16,24},{20,52},{24,0},{28,60},{32,40}... | collective-permute-start | bytes 393224 | tf_op jit(solution)/shard_map/ppermute | solution.py:289
  11.4 12.1 %collective-permute-start.3 = (bf16[1024,256]{1,0:T(8,128)(2,1)S(1)}, bf16[1024,256]{1,0:T(8,128)(2,1)S(1)}, u32[]{:S(2)}, u32[]{:S(2)}) collective-permute-start(bf16[1024,256]{1,0:T(8,128)(2,1)S(1)} %pad_maximum_fusion.refs_2_), channel_id=1, source_target_pairs={{0,4},{4,0},{1,5},{5,1},{2,6},{6,2},{3,7},{7,3},{8,12},{12,8},{9,1... | collective-permute-start | bytes 1572872 | tf_op jit(solution)/shard_map/ppermute | solution.py:272
  11.5 13.9 %collective-permute-start.6 = (bf16[1024,256]{1,0:T(8,128)(2,1)S(1)}, bf16[1024,256]{1,0:T(8,128)(2,1)S(1)}, u32[]{:S(2)}, u32[]{:S(2)}) collective-permute-start(bf16[1024,256]{1,0:T(8,128)(2,1)S(1)} %pad_maximum_fusion.refs_2_), channel_id=1, source_target_pairs={{0,64},{4,20},{8,72},{12,28},{16,80},{20,4},{24,88},{28,12},{32,96... | collective-permute-start | bytes 1572872 | tf_op jit(solution)/shard_map/ppermute | solution.py:289
  15.4 12.8 %collective-permute-start.5 = (bf16[1024,256]{1,0:T(8,128)(2,1)S(1)}, bf16[1024,256]{1,0:T(8,128)(2,1)S(1)}, u32[]{:S(2)}, u32[]{:S(2)}) collective-permute-start(bf16[1024,256]{1,0:T(8,128)(2,1)S(1)} %pad_maximum_fusion.refs_2_), channel_id=1, source_target_pairs={{0,32},{4,12},{8,40},{12,20},{16,48},{20,28},{24,56},{28,4},{32,64... | collective-permute-start | bytes 1572872 | tf_op jit(solution)/shard_map/ppermute | solution.py:289
  16.5 12.8 %collective-permute-start.4 = (bf16[1024,256]{1,0:T(8,128)(2,1)S(1)}, bf16[1024,256]{1,0:T(8,128)(2,1)S(1)}, u32[]{:S(2)}, u32[]{:S(2)}) collective-permute-start(bf16[1024,256]{1,0:T(8,128)(2,1)S(1)} %pad_maximum_fusion.refs_2_), channel_id=1, source_target_pairs={{0,96},{4,28},{8,104},{12,4},{16,112},{20,12},{24,120},{28,20},{32... | collective-permute-start | bytes 1572872 | tf_op jit(solution)/shard_map/ppermute | solution.py:289
  34.4 7.5 %collective-permute-start.8 = (bf16[256,256]{1,0:T(8,128)(2,1)S(1)}, bf16[256,256]{1,0:T(8,128)(2,1)S(1)}, u32[]{:S(2)}, u32[]{:S(2)}) collective-permute-start(bf16[256,256]{1,0:T(8,128)(2,1)S(1)} %get-tuple-element.59), channel_id=1, source_target_pairs={{0,1},{1,2},{2,3},{3,0},{4,5},{5,6},{6,7},{7,4},{8,9},{9,10},{10,1... | collective-permute-start | bytes 393224 | tf_op jit(solution)/shard_map/ppermute | solution.py:272
  36.1 9.2 %collective-permute-start.9 = (bf16[256,256]{1,0:T(8,128)(2,1)S(1)}, bf16[256,256]{1,0:T(8,128)(2,1)S(1)}, u32[]{:S(2)}, u32[]{:S(2)}) collective-permute-start(bf16[256,256]{1,0:T(8,128)(2,1)S(1)} %get-tuple-element.60), channel_id=1, source_target_pairs={{0,2},{1,3},{2,0},{3,1},{4,6},{5,7},{6,4},{7,5},{8,10},{9,11},{10,... | collective-permute-start | bytes 393224 | tf_op jit(solution)/shard_map/ppermute | solution.py:272
  47.0 7.9 %collective-permute-start.11 = (bf16[320,256]{1,0:T(8,128)(2,1)S(1)}, bf16[320,256]{1,0:T(8,128)(2,1)S(1)}, u32[]{:S(2)}, u32[]{:S(2)}) collective-permute-start(bf16[320,256]{1,0:T(8,128)(2,1)S(1)} %get-tuple-element.65), channel_id=1, source_target_pairs={{0,1},{1,2},{2,3},{3,0},{4,5},{5,6},{6,7},{7,4},{8,9},{9,10},{10,1... | collective-permute-start | bytes 491528 | tf_op jit(solution)/shard_map/ppermute | solution.py:272
  48.7 9.0 %collective-permute-start.12 = (bf16[320,256]{1,0:T(8,128)(2,1)S(1)}, bf16[320,256]{1,0:T(8,128)(2,1)S(1)}, u32[]{:S(2)}, u32[]{:S(2)}) collective-permute-start(bf16[320,256]{1,0:T(8,128)(2,1)S(1)} %get-tuple-element.66), channel_id=1, source_target_pairs={{0,2},{1,3},{2,0},{3,1},{4,6},{5,7},{6,4},{7,5},{8,10},{9,11},{10,... | collective-permute-start | bytes 491528 | tf_op jit(solution)/shard_map/ppermute | solution.py:272
  51.0 6.6 %collective-permute-start.13 = (bf16[320,256]{1,0:T(8,128)(2,1)S(1)}, bf16[320,256]{1,0:T(8,128)(2,1)S(1)}, u32[]{:S(2)}, u32[]{:S(2)}) collective-permute-start(bf16[320,256]{1,0:T(8,128)(2,1)S(1)} %get-tuple-element.67), channel_id=1, source_target_pairs={{0,3},{1,0},{2,1},{3,2},{4,7},{5,4},{6,5},{7,6},{8,11},{9,8},{10,9... | collective-permute-start | bytes 491528 | tf_op jit(solution)/shard_map/ppermute | solution.py:272
  61.4 6.6 %collective-permute-start.15 = (bf16[2048,256]{1,0:T(8,128)(2,1)S(1)}, bf16[2048,256]{1,0:T(8,128)(2,1)S(1)}, u32[]{:S(2)}, u32[]{:S(2)}) collective-permute-start(bf16[2048,256]{1,0:T(8,128)(2,1)S(1)} %get-tuple-element.75), channel_id=1, source_target_pairs={{0,4},{4,0},{1,5},{5,1},{2,6},{6,2},{3,7},{7,3},{8,12},{12,8},{9,1... | collective-permute-start | bytes 3145736 | tf_op jit(solution)/shard_map/ppermute | solution.py:272
  64.5 5.9 %collective-permute-start.17 = (f32[64,256]{1,0:T(8,128)S(1)}, f32[64,256]{1,0:T(8,128)S(1)}, u32[]{:S(2)}, u32[]{:S(2)}) collective-permute-start(f32[64,256]{1,0:T(8,128)S(1)} %get-tuple-element.76.refs_4_), channel_id=1, source_target_pairs={{0,16},{8,24},{16,0},{24,8},{1,17},{9,25},{17,1},{25,9},{2,18},{10... | collective-permute-start | bytes 196616 | tf_op jit(solution)/shard_map/ppermute | solution.py:272
  65.9 5.5 %collective-permute-start.16 = (f32[64,256]{1,0:T(8,128)S(1)}, f32[64,256]{1,0:T(8,128)S(1)}, u32[]{:S(2)}, u32[]{:S(2)}) collective-permute-start(f32[64,256]{1,0:T(8,128)S(1)} %get-tuple-element.76.refs_4_), channel_id=1, source_target_pairs={{0,8},{8,16},{16,24},{24,0},{1,9},{9,17},{17,25},{25,1},{2,10},{10... | collective-permute-start | bytes 196616 | tf_op jit(solution)/shard_map/ppermute | solution.py:272
  66.2 11.5 %collective-permute-start.19 = (bf16[1024,256]{1,0:T(8,128)(2,1)S(1)}, bf16[1024,256]{1,0:T(8,128)(2,1)S(1)}, u32[]{:S(2)}, u32[]{:S(2)}) collective-permute-start(bf16[1024,256]{1,0:T(8,128)(2,1)S(1)} %get-tuple-element.78), channel_id=1, source_target_pairs={{0,8},{4,36},{8,16},{12,44},{16,24},{20,52},{24,0},{28,60},{32,40}... | collective-permute-start | bytes 1572872 | tf_op jit(solution)/shard_map/ppermute | solution.py:289
  68.0 10.1 %collective-permute-start.20 = (bf16[1024,256]{1,0:T(8,128)(2,1)S(1)}, bf16[1024,256]{1,0:T(8,128)(2,1)S(1)}, u32[]{:S(2)}, u32[]{:S(2)}) collective-permute-start(bf16[1024,256]{1,0:T(8,128)(2,1)S(1)} %get-tuple-element.79), channel_id=1, source_target_pairs={{0,24},{4,100},{8,0},{12,108},{16,8},{20,116},{24,16},{28,124},{32... | collective-permute-start | bytes 1572872 | tf_op jit(solution)/shard_map/ppermute | solution.py:289
  73.3 11.7 %collective-permute-start.21 = (bf16[1024,256]{1,0:T(8,128)(2,1)S(1)}, bf16[1024,256]{1,0:T(8,128)(2,1)S(1)}, u32[]{:S(2)}, u32[]{:S(2)}) collective-permute-start(bf16[1024,256]{1,0:T(8,128)(2,1)S(1)} %get-tuple-element.80), channel_id=1, source_target_pairs={{0,16},{4,68},{8,24},{12,76},{16,0},{20,84},{24,8},{28,92},{32,48}... | collective-permute-start | bytes 1572872 | tf_op jit(solution)/shard_map/ppermute | solution.py:289
  74.6 8.6 %collective-permute-start.24 = (f32[64,256]{1,0:T(8,128)S(1)}, f32[64,256]{1,0:T(8,128)S(1)}, u32[]{:S(2)}, u32[]{:S(2)}) collective-permute-start(f32[64,256]{1,0:T(8,128)S(1)} %get-tuple-element.81.q), channel_id=1, source_target_pairs={{0,96},{32,0},{64,32},{96,64},{1,97},{33,1},{65,33},{97,65},{2,98}... | collective-permute-start | bytes 196616 | tf_op jit(solution)/shard_map/ppermute | solution.py:272
  77.2 6.6 %collective-permute-start.23 = (f32[64,256]{1,0:T(8,128)S(1)}, f32[64,256]{1,0:T(8,128)S(1)}, u32[]{:S(2)}, u32[]{:S(2)}) collective-permute-start(f32[64,256]{1,0:T(8,128)S(1)} %get-tuple-element.81.q), channel_id=1, source_target_pairs={{0,64},{32,96},{64,0},{96,32},{1,65},{33,97},{65,1},{97,33},{2,66}... | collective-permute-start | bytes 196616 | tf_op jit(solution)/shard_map/ppermute | solution.py:272
  77.7 7.3 %collective-permute-start.22 = (f32[64,256]{1,0:T(8,128)S(1)}, f32[64,256]{1,0:T(8,128)S(1)}, u32[]{:S(2)}, u32[]{:S(2)}) collective-permute-start(f32[64,256]{1,0:T(8,128)S(1)} %get-tuple-element.81.q), channel_id=1, source_target_pairs={{0,32},{32,64},{64,96},{96,0},{1,33},{33,65},{65,97},{97,1},{2,34}... | collective-permute-start | bytes 196616 | tf_op jit(solution)/shard_map/ppermute | solution.py:272
  85.7 6.5 %collective-permute-start.25 = (f32[64,256]{1,0:T(8,128)S(1)}, f32[64,256]{1,0:T(8,128)S(1)}, u32[]{:S(2)}, u32[]{:S(2)}) collective-permute-start(f32[64,256]{1,0:T(8,128)S(1)} %get-tuple-element.82), channel_id=1, source_target_pairs={{0,1},{1,0},{2,3},{3,2},{4,5},{5,4},{6,7},{7,6},{8,9},{9,8},{10,11... | collective-permute-start | bytes 196616 | tf_op jit(solution)/shard_map/ppermute | solution.py:276
  87.5 6.3 %collective-permute-start.27 = (bf16[256,256]{1,0:T(8,128)(2,1)S(1)}, bf16[256,256]{1,0:T(8,128)(2,1)S(1)}, u32[]{:S(2)}, u32[]{:S(2)}) collective-permute-start(bf16[256,256]{1,0:T(8,128)(2,1)S(1)} %get-tuple-element.84), channel_id=1, source_target_pairs={{0,32},{4,12},{8,40},{12,20},{16,48},{20,28},{24,56},{28,4},{32,64... | collective-permute-start | bytes 393224 | tf_op jit(solution)/shard_map/ppermute | solution.py:289
  87.8 7.4 %collective-permute-start.28 = (bf16[256,256]{1,0:T(8,128)(2,1)S(1)}, bf16[256,256]{1,0:T(8,128)(2,1)S(1)}, u32[]{:S(2)}, u32[]{:S(2)}) collective-permute-start(bf16[256,256]{1,0:T(8,128)(2,1)S(1)} %get-tuple-element.85), channel_id=1, source_target_pairs={{0,64},{4,20},{8,72},{12,28},{16,80},{20,4},{24,88},{28,12},{32,96... | collective-permute-start | bytes 393224 | tf_op jit(solution)/shard_map/ppermute | solution.py:289
  92.2 6.9 %collective-permute-start.26 = (f32[128,256]{1,0:T(8,128)S(1)}, f32[128,256]{1,0:T(8,128)S(1)}, u32[]{:S(2)}, u32[]{:S(2)}) collective-permute-start(f32[128,256]{1,0:T(8,128)S(1)} %constant_dynamic-update-slice_fusion.3.first), channel_id=1, source_target_pairs={{0,3},{1,2},{2,1},{3,0},{4,7},{5,6},{6,5},{7,4},{8,11},{9,10},{10,... | collective-permute-start | bytes 393224 | tf_op jit(solution)/shard_map/ppermute | solution.py:276
  (9 other events, 45.5 us)

commit v6 on v5

--- a/solution.py
+++ b/solution.py
@@ -155,6 +155,10 @@
         out[...] = total[i * NODE : (i + 1) * NODE].astype(out.dtype)
 
 
+def add_one(own, r, out):
+    out[...] = own[...] + r[...].astype(F32)
+
+
 def add_two(own, r1, r2, out):
     out[...] = own[...] + r1[...].astype(F32) + r2[...].astype(F32)
 
@@ -179,7 +183,7 @@
             out[NODE:] = piece.astype(BF16)
 
 
-FIRST, LAST = (1, 3), (2, 0)
+FIRST, LAST = (2, 0), (1, 3)
 
 
 def back_all(bt):
@@ -233,39 +237,36 @@
 
 def ring_sum(place, terms, out, held):
     for d, term in enumerate(terms):
-        held[lax.rem(place + 4 - d, 4)] = term[...]
-    out[...] = (held[0] + held[1]) + (held[2] + held[3])
-
-
-def backward_own_first(pos, dense, bt, got, qown, qsum, x1, x3):
+        held[lax.rem(place + 4 - d, 4)] = term[...].astype(F32)
+    out[...] = ((held[0] + held[1]) + (held[2] + held[3])).astype(out.dtype)
+
+
+def backward_own_first(pos, dense, bt, got, qown, qsum, x2, x0):
     hi, lo = got[8 * NODE : 8 * NODE + 64], got[8 * NODE + 64 :]
-    qsum[...] = qown[...] + (hi.astype(F32) + lo.astype(F32))
-    backward_own(FIRST, dense, bt, pos, got, (x1, x3))
-
-
-def backward_own_last(pos, dense, bt, got, q, q1, q2, q3, qsum, x2, x0, held):
+    qsum[...] = (qown[...] + (hi.astype(F32) + lo.astype(F32))).astype(BF16)
+    backward_own(FIRST, dense, bt, pos, got, (x2, x0))
+
+
+def backward_own_last(pos, dense, bt, got, q, q1, q2, q3, qsum, x1, x3, held):
     ring_sum(pos[PX], (q, q1, q2, q3), qsum, held)
-    backward_own(LAST, dense, bt, pos, got, (x2, x0))
-
-
-def first_sum(pos, x0, r2, q, q1, q2, q3, t0, t1, t2, t3, qsum, held):
+    backward_own(LAST, dense, bt, pos, got, (x1, x3))
+
+
+def first_sum(pos, x0, r1, r3, q, q1, q2, q3, t0, t1, t2, t3, qsum, held):
     ring_sum(pos[PZ], (q, q1, q2, q3), qsum, held)
     for d, out in enumerate((t0, t1, t2, t3)):
         at = slice(d * NODE, (d + 1) * NODE)
-        out[...] = (x0[at] + r2[at].astype(F32)).astype(out.dtype)
-
-
-def last_sum(t0, r1, r2, r3, out):
+        out[...] = (x0[at] + r1[at].astype(F32) + r3[at].astype(F32)).astype(out.dtype)
+
+
+def last_sum(pos, t0, r1, r2, r3, first, second, out, grad):
     s = t0[...]
     for r in (r1, r2, r3):
         s += r[...].astype(F32)
     out[...] = s.T.astype(BF16)
-
-
-def weight_rows(pos, first, second, out):
     for r, i, p in ((first, 0, PY), (first, 64, PX1), (second, 0, PX3), (second, 64, PY2)):
         row = pl.multiple_of(pos[p] * 64, 64)
-        out[pl.ds(row, 64), :] = r[i : i + 64] * (1.0 / NODE)
+        grad[pl.ds(row, 64), :] = r[i : i + 64] * (1.0 / NODE)
 
 
 def send(v, axis, d, n=4):
@@ -353,32 +354,32 @@
     long, longf = shape((4 * NODE, FEAT), BF16), shape((4 * NODE, FEAT), F32)
 
     held = [pltpu.VMEM((4, 64, FEAT), F32)]
+    rounded = shape((64, FEAT), BF16)
+    dense, q, x2, x0 = dense_call(
+        backward_own_first, [rounded, long, longf], dense, pos, bt, got_first, q
+    )
+    along_x = [send(q, "x", d) for d in (1, 2, 3)]
+    r2 = send_by_core(x2, 0, 2)
     dense, q, x1, x3 = dense_call(
-        backward_own_first, [piece, long, long], dense, pos, bt, got_first, q
-    )
-    along_x = [send(q, "x", d) for d in (1, 2, 3)]
-    r1, r3 = send_by_core(x1, 0, 1), send_by_core(x3, 0, 3)
-    dense, q, x2, x0 = dense_call(
         backward_own_last,
-        [piece, long, longf],
+        [rounded, long, long],
         dense, pos, bt, got_last, q, *along_x,
         scratch=held,
     )
-    r2 = send_by_core(x2, 0, 2)
-    x0 = call(add_two, longf, [VSPEC] * 3, nbytes=MIB)(x0, r1, r3)
+    r1, r3 = send_by_core(x1, 0, 1), send_by_core(x3, 0, 3)
+    x0 = call(add_one, longf, [VSPEC] * 2, nbytes=MIB)(x0, r2)
     t0, t1, t2, t3, q = call(
         first_sum,
         [blockf, block, block, block, piece],
-        [SSPEC] + [VSPEC] * 6,
+        [SSPEC] + [VSPEC] * 7,
         held,
         nbytes=MIB,
-    )(pos, x0, r2, q, *[send(q, "z", d) for d in (1, 2, 3)])
+    )(pos, x0, r1, r3, q, *[send(q, "z", d) for d in (1, 2, 3)])
     r = {d: send_by_core(v, 1, d) for d, v in ((2, t2), (1, t1), (3, t3))}
-    feature_grad = call(last_sum, block, [VSPEC] * 4, nbytes=MIB)(t0, r[1], r[2], r[3])
     first = jnp.concatenate([q, swap(q, "y", 1)], axis=0)
-    weight_grad = call(
-        weight_rows, shape((FEAT, FEAT), F32), [SSPEC, VSPEC, VSPEC], nbytes=MIB // 2
-    )(pos, first, swap(first, "y", 3))
+    feature_grad, weight_grad = call(
+        last_sum, [block, shape((FEAT, FEAT), F32)], [SSPEC] + [VSPEC] * 6, nbytes=MIB
+    )(pos, t0, r[1], r[2], r[3], first, swap(first, "y", 3))
     return activated, weight_grad, feature_grad
 
 

time: 101 us -> 99.4 us (0.984)
  waiting for transfers between devices: 30.4 us -> 25.8 us
  starting transfers between devices: 42.5 us -> 45 us
    ppermute x16, waiting for transfers between devices: 19.3 us -> 16.1 us  [send(): return lax.ppermute(v, axis, [(i, (i + d) % n) for i in range(n)])]
    ppermute x12, starting transfers between devices: 21.7 us -> 24.2 us  [send_by_core(): return lax.ppermute(v, RING, pairs)]
    pallas_call x1, Pallas kernels: 4.19 us -> 5.66 us  [body(): call(dense_block, DENSE, [ASPEC, ASPEC, ASPEC, SSPEC, VSPEC], [pltpu.SMEM...]
    ppermute x12, waiting for transfers between devices: 8.71 us -> 7.59 us  [send_by_core(): return lax.ppermute(v, RING, pairs)]
    pallas_call x3 -> x2, Pallas kernels: 2.19 us -> 1.44 us  [the longest x1 1.36 us: body(): call(last_sum, [block, shape((FEAT, FEAT), F32)], [SSPEC] + [VSPEC] * 6,...]
  transfers between devices with their start and end apart: 30 -> 30, of which waited for: 18 -> 17; matrix products, arithmetic and copies ran while one was open for 0% -> 0% of each run, Pallas kernels for 19% -> 20%
where the time goes in v6:
time: 99.4 us; the launch traced here: 99.1 us
  starting transfers between devices  45 us (45%)
  Pallas kernels  26.5 us (27%)
  waiting for transfers between devices  25.8 us (26%)
  between operations  1.48 us (1%)
    ppermute x12, starting transfers between devices, send_by_core(): return lax.ppermute(v, RING, pairs)  24.2 us
    ppermute x16, starting transfers between devices, send(): return lax.ppermute(v, axis, [(i, (i + d) % n) for i in range(n)])  17.5 us
    ppermute x16, waiting for transfers between devices, send(): return lax.ppermute(v, axis, [(i, (i + d) % n) for i in range(n)])  16.1 us
    pallas_call x8, Pallas kernels, dense_call(): call(wrapped, [DENSE] + outs, [SSPEC] + [VSPEC] * (n - 1), scratch, flops...  14.4 us
    ppermute x12, waiting for transfers between devices, send_by_core(): return lax.ppermute(v, RING, pairs)  7.59 us
    pallas_call x1, Pallas kernels, body(): call(dense_block, DENSE, [ASPEC, ASPEC, ASPEC, SSPEC, VSPEC], [pltpu.SMEM...  5.66 us
    ppermute x2, starting transfers between devices, swap(): return lax.ppermute(v, axis, [(i, i ^ step) for i in range(4)])  3.41 us
    pallas_call x1, Pallas kernels, body(): dense = call(dense_zeros, DENSE, [SSPEC], nbytes=16 * MIB)(pos)  2.77 us
  transfers between devices with their start and end apart: 30, of which 17 were waited for; matrix products, arithmetic and copies ran while one was open for 0% of the time, Pallas kernels for 20%

profile of v6, /device:TPU:0, one launch (start us, length us, event | category | flops | bytes accessed | tf_op | source)
XLA Modules:
  0.0 99.1 jit_solution(4541077626363005278)
XLA Ops:
  0.6 3.2 %collective-permute-start.1 = (bf16[256,256]{1,0:T(8,128)(2,1)}, bf16[256,256]{1,0:T(8,128)(2,1)S(1)}, u32[]{:S(2)}, u32[]{:S(2)}) collective-permute-start(bf16[256,256]{1,0:T(8,128)(2,1)} %param.7), channel_id=1, source_target_pairs={{0,16},{4,68},{8,24},{12,76},{16,0},{20,84},{24,8},{28,92},{32,48}... | collective-permute-start | bytes 393224 | tf_op jit(solution)/shard_map/ppermute | solution.py:290
  5.9 2.8 %shard_map.94.given = bf16[64,1024,128]{2,1,0:T(8,128)(2,1)S(1)} custom-call(s32[9]{0:T(128)S(1)} %stack.39.pos.refs_0_), custom_call_target="tpu_custom_call" | custom-call | bytes 16777216 | tf_op jit(solution)/shard_map/pallas_call | solution.py:302
  9.0 2.4 %collective-permute-done.2 = bf16[256,256]{1,0:T(8,128)(2,1)S(1)} collective-permute-done((bf16[256,256]{1,0:T(8,128)(2,1)}, bf16[256,256]{1,0:T(8,128)(2,1)S(1)}, u32[]{:S(2)}, u32[]{:S(2)}) %collective-permute-start.2) | collective-permute-done | bytes 131104 | tf_op jit(solution)/shard_map/ppermute | solution.py:290
  11.5 4.0 %collective-permute-start.6 = (bf16[1024,256]{1,0:T(8,128)(2,1)S(1)}, bf16[1024,256]{1,0:T(8,128)(2,1)S(1)}, u32[]{:S(2)}, u32[]{:S(2)}) collective-permute-start(bf16[1024,256]{1,0:T(8,128)(2,1)S(1)} %pad_maximum_fusion.refs_2_), channel_id=1, source_target_pairs={{0,64},{4,20},{8,72},{12,28},{16,80},{20,4},{24,88},{28,12},{32,96... | collective-permute-start | bytes 1572872 | tf_op jit(solution)/shard_map/ppermute | solution.py:290
  16.5 2.2 %collective-permute-start.4 = (bf16[1024,256]{1,0:T(8,128)(2,1)S(1)}, bf16[1024,256]{1,0:T(8,128)(2,1)S(1)}, u32[]{:S(2)}, u32[]{:S(2)}) collective-permute-start(bf16[1024,256]{1,0:T(8,128)(2,1)S(1)} %pad_maximum_fusion.refs_2_), channel_id=1, source_target_pairs={{0,96},{4,28},{8,104},{12,4},{16,112},{20,12},{24,120},{28,20},{32... | collective-permute-start | bytes 1572872 | tf_op jit(solution)/shard_map/ppermute | solution.py:290
  19.3 5.7 %shard_map.95.refs_1_ = bf16[64,1024,128]{2,1,0:T(8,128)(2,1)S(1)} custom-call(bf16[384,128,128]{2,1,0:T(8,128)(2,1)} %bitcast.12, s32[1,1,384]{2,1,0:T(1,128)} %rows_in.1, s32[1,1,384]{2,1,0:T(1,128)} %cols_in.1, s32[1]{0:T(128)} %bitcast.11.count, bf16[64,1024,128]{2,1,0:T(8,128)(2,1)S(1)} %shard_map.94.given), custom_call_target="tpu_custom_call", output_to_operand_aliasing={{}: (4, {})} | custom-call | bytes 25165824 | tf_op jit(solution)/shard_map/pallas_call | solution.py:306
  25.0 1.8 %shard_map.96 = (bf16[64,1024,128]{2,1,0:T(8,128)(2,1)S(1)}, f32[1024,256]{1,0:T(8,128)S(1)}) custom-call(s32[9]{0:T(128)S(1)} %stack.39.pos.refs_0_, bf16[64,1024,128]{2,1,0:T(8,128)(2,1)S(1)} %shard_map.95.refs_1_, bf16[1024,256]{1,0:T(8,128)(2,1)S(1)} %pad_maximum_fusion.refs_2_, ...), custom_call_target="tpu_custom_call", output_to_operand_aliasing={{0}: (1, {})} | custom-call | flops 16777216 | bytes 16777216 | tf_op jit(solution)/shard_map/pallas_call | solution.py:61
  29.5 2.3 %shard_map.97 = (bf16[64,1024,128]{2,1,0:T(8,128)(2,1)S(1)}, f32[1024,256]{1,0:T(8,128)S(1)}) custom-call(s32[9]{0:T(128)S(1)} %stack.39.pos.refs_0_, bf16[64,1024,128]{2,1,0:T(8,128)(2,1)S(1)} %get-tuple-element.51.refs_1_, bf16[3072,256]{1,0:T(8,128)(2,1)S(1)} %constant_dynamic-update-slice_fusion.refs_2_, ...), custom_call_target="tpu_custom_call", output_to_operand_aliasing={{0}: (1, {})} | custom-call | flops 1000 | bytes 1000 | tf_op jit(solution)/shard_map/pallas_call | solution.py:61
  36.1 2.9 %collective-permute-start.9 = (bf16[256,256]{1,0:T(8,128)(2,1)S(1)}, bf16[256,256]{1,0:T(8,128)(2,1)S(1)}, u32[]{:S(2)}, u32[]{:S(2)}) collective-permute-start(bf16[256,256]{1,0:T(8,128)(2,1)S(1)} %get-tuple-element.62), channel_id=1, source_target_pairs={{0,2},{1,3},{2,0},{3,1},{4,6},{5,7},{6,4},{7,5},{8,10},{9,11},{10,... | collective-permute-start | bytes 393224 | tf_op jit(solution)/shard_map/ppermute | solution.py:273
  41.9 3.4 %collective-permute-done.9.r2 = bf16[256,256]{1,0:T(8,128)(2,1)S(1)} collective-permute-done((bf16[256,256]{1,0:T(8,128)(2,1)S(1)}, bf16[256,256]{1,0:T(8,128)(2,1)S(1)}, u32[]{:S(2)}, u32[]{:S(2)}) %collective-permute-start.9) | collective-permute-done | bytes 131104 | tf_op jit(solution)/shard_map/ppermute | solution.py:273
  48.7 2.3 %collective-permute-start.12 = (bf16[320,256]{1,0:T(8,128)(2,1)S(1)}, bf16[320,256]{1,0:T(8,128)(2,1)S(1)}, u32[]{:S(2)}, u32[]{:S(2)}) collective-permute-start(bf16[320,256]{1,0:T(8,128)(2,1)S(1)} %get-tuple-element.68), channel_id=1, source_target_pairs={{0,2},{1,3},{2,0},{3,1},{4,6},{5,7},{6,4},{7,5},{8,10},{9,11},{10,... | collective-permute-start | bytes 491528 | tf_op jit(solution)/shard_map/ppermute | solution.py:273
  51.9 2.9 %collective-permute-done.11.refs_3_ = bf16[320,256]{1,0:T(8,128)(2,1)S(1)} collective-permute-done((bf16[320,256]{1,0:T(8,128)(2,1)S(1)}, bf16[320,256]{1,0:T(8,128)(2,1)S(1)}, u32[]{:S(2)}, u32[]{:S(2)}) %collective-permute-start.11) | collective-permute-done | bytes 163872 | tf_op jit(solution)/shard_map/ppermute | solution.py:273
  54.8 2.8 %collective-permute-done.12.refs_4_ = bf16[320,256]{1,0:T(8,128)(2,1)S(1)} collective-permute-done((bf16[320,256]{1,0:T(8,128)(2,1)S(1)}, bf16[320,256]{1,0:T(8,128)(2,1)S(1)}, u32[]{:S(2)}, u32[]{:S(2)}) %collective-permute-start.12) | collective-permute-done | bytes 163872 | tf_op jit(solution)/shard_map/ppermute | solution.py:273
  57.6 1.8 %shard_map.102 = (bf16[64,1024,128]{2,1,0:T(8,128)(2,1)S(1)}, bf16[2176,256]{1,0:T(8,128)(2,1)S(1)}, bf16[4,256,256]{2,1,0:T(8,128)(2,1)S(1)}, f32[64,256]{1,0:T(8,128)S(1)}) custom-call(s32[9]{0:T(128)S(1)} %stack.39.pos.refs_0_, bf16[64,1024,128]{2,1,0:T(8,128)(2,1)S(1)} %get-tuple-element.65.refs_1_, ...), custom_call_target="tpu_custom_call", output_to_operand_aliasing={{0}: (1, {})} | custom-call | flops 1000 | bytes 1000 | tf_op jit(solution)/shard_map/pallas_call | solution.py:61
  59.6 1.8 %shard_map.103 = (bf16[64,1024,128]{2,1,0:T(8,128)(2,1)S(1)}, bf16[2048,256]{1,0:T(8,128)(2,1)S(1)}) custom-call(s32[9]{0:T(128)S(1)} %stack.39.pos.refs_0_, bf16[64,1024,128]{2,1,0:T(8,128)(2,1)S(1)} %get-tuple-element.71.refs_1_, bf16[4,256,256]{2,1,0:T(8,128)(2,1)S(1)} %get-tuple-element.72.refs_2_), custom_call_target="tpu_custom_call", output_to_operand_aliasing={{0}: (1, {})} | custom-call | flops 1000 | bytes 1000 | tf_op jit(solution)/shard_map/pallas_call | solution.py:61
  62.3 1.8 %shard_map.104 = (bf16[64,1024,128]{2,1,0:T(8,128)(2,1)S(1)}, bf16[64,256]{1,0:T(8,128)(2,1)S(1)}, bf16[1024,256]{1,0:T(8,128)(2,1)S(1)}, f32[1024,256]{1,0:T(8,128)S(1)}) custom-call(s32[9]{0:T(128)S(1)} %stack.39.pos.refs_0_, bf16[64,1024,128]{2,1,0:T(8,128)(2,1)S(1)} %get-tuple-element.73.refs_1_, ...), custom_call_target="tpu_custom_call", output_to_operand_aliasing={{0}: (1, {})} | custom-call | flops 1000 | bytes 1000 | tf_op jit(solution)/shard_map/pallas_call | solution.py:61
  66.2 4.1 %collective-permute-start.15 = (bf16[1024,256]{1,0:T(8,128)(2,1)S(1)}, bf16[1024,256]{1,0:T(8,128)(2,1)S(1)}, u32[]{:S(2)}, u32[]{:S(2)}) collective-permute-start(bf16[1024,256]{1,0:T(8,128)(2,1)S(1)} %get-tuple-element.77), channel_id=1, source_target_pairs={{0,16},{4,68},{8,24},{12,76},{16,0},{20,84},{24,8},{28,92},{32,48}... | collective-permute-start | bytes 1572872 | tf_op jit(solution)/shard_map/ppermute | solution.py:290
  71.0 1.8 %shard_map.106 = (bf16[64,1024,128]{2,1,0:T(8,128)(2,1)S(1)}, bf16[64,256]{1,0:T(8,128)(2,1)S(1)}, bf16[1024,256]{1,0:T(8,128)(2,1)S(1)}, bf16[1024,256]{1,0:T(8,128)(2,1)S(1)}) custom-call(s32[9]{0:T(128)S(1)} %stack.39.pos.refs_0_, bf16[64,1024,128]{2,1,0:T(8,128)(2,1)S(1)} %get-tuple-element.78.refs_1_, ...), custom_call_target="tpu_custom_call", output_to_operand_aliasing={{0}: (1, {})} | custom-call | flops 1000 | bytes 1000 | tf_op jit(solution)/shard_map/pallas_call | solution.py:61
  73.5 2.6 %collective-permute-start.21 = (bf16[1024,256]{1,0:T(8,128)(2,1)S(1)}, bf16[1024,256]{1,0:T(8,128)(2,1)S(1)}, u32[]{:S(2)}, u32[]{:S(2)}) collective-permute-start(bf16[1024,256]{1,0:T(8,128)(2,1)S(1)} %get-tuple-element.82), channel_id=1, source_target_pairs={{0,24},{4,100},{8,0},{12,108},{16,8},{20,116},{24,16},{28,124},{32... | collective-permute-start | bytes 1572872 | tf_op jit(solution)/shard_map/ppermute | solution.py:290
  76.2 2.6 %collective-permute-start.24 = (bf16[64,256]{1,0:T(8,128)(2,1)S(1)}, bf16[64,256]{1,0:T(8,128)(2,1)S(1)}, u32[]{:S(2)}, u32[]{:S(2)}) collective-permute-start(bf16[64,256]{1,0:T(8,128)(2,1)S(1)} %get-tuple-element.83.q), channel_id=1, source_target_pairs={{0,96},{32,0},{64,32},{96,64},{1,97},{33,1},{65,33},{97,65},{2,98}... | collective-permute-start | bytes 98312 | tf_op jit(solution)/shard_map/ppermute | solution.py:273
  80.6 3.7 %collective-permute-done.23.q2 = bf16[64,256]{1,0:T(8,128)(2,1)S(1)} collective-permute-done((bf16[64,256]{1,0:T(8,128)(2,1)S(1)}, bf16[64,256]{1,0:T(8,128)(2,1)S(1)}, u32[]{:S(2)}, u32[]{:S(2)}) %collective-permute-start.23) | collective-permute-done | bytes 32800 | tf_op jit(solution)/shard_map/ppermute | solution.py:273
  85.4 1.8 %collective-permute-start.28 = (f32[64,256]{1,0:T(8,128)S(1)}, f32[64,256]{1,0:T(8,128)S(1)}, u32[]{:S(2)}, u32[]{:S(2)}) collective-permute-start(f32[64,256]{1,0:T(8,128)S(1)} %get-tuple-element.88), channel_id=1, source_target_pairs={{0,1},{1,0},{2,3},{3,2},{4,5},{5,4},{6,7},{7,6},{8,9},{9,8},{10,11... | collective-permute-start | bytes 196616 | tf_op jit(solution)/shard_map/ppermute | solution.py:277
  87.2 3.0 %collective-permute-start.26 = (bf16[256,256]{1,0:T(8,128)(2,1)S(1)}, bf16[256,256]{1,0:T(8,128)(2,1)S(1)}, u32[]{:S(2)}, u32[]{:S(2)}) collective-permute-start(bf16[256,256]{1,0:T(8,128)(2,1)S(1)} %get-tuple-element.86), channel_id=1, source_target_pairs={{0,64},{4,20},{8,72},{12,28},{16,80},{20,4},{24,88},{28,12},{32,96... | collective-permute-start | bytes 393224 | tf_op jit(solution)/shard_map/ppermute | solution.py:290
  95.6 2.2 %collective-permute-done.29.second = f32[128,256]{1,0:T(8,128)S(1)} collective-permute-done((f32[128,256]{1,0:T(8,128)S(1)}, f32[128,256]{1,0:T(8,128)S(1)}, u32[]{:S(2)}, u32[]{:S(2)}) %collective-permute-start.29) | collective-permute-done | bytes 131104 | tf_op jit(solution)/shard_map/ppermute | solution.py:277
  (64 shorter events, 31.7 us)
Async XLA Ops:
  0.6 8.1 %collective-permute-start.1 = (bf16[256,256]{1,0:T(8,128)(2,1)}, bf16[256,256]{1,0:T(8,128)(2,1)S(1)}, u32[]{:S(2)}, u32[]{:S(2)}) collective-permute-start(bf16[256,256]{1,0:T(8,128)(2,1)} %param.7), channel_id=1, source_target_pairs={{0,16},{4,68},{8,24},{12,76},{16,0},{20,84},{24,8},{28,92},{32,48}... | collective-permute-start | bytes 393224 | tf_op jit(solution)/shard_map/ppermute | solution.py:290
  5.0 6.4 %collective-permute-start.2 = (bf16[256,256]{1,0:T(8,128)(2,1)}, bf16[256,256]{1,0:T(8,128)(2,1)S(1)}, u32[]{:S(2)}, u32[]{:S(2)}) collective-permute-start(bf16[256,256]{1,0:T(8,128)(2,1)} %param.7), channel_id=1, source_target_pairs={{0,8},{4,36},{8,16},{12,44},{16,24},{20,52},{24,0},{28,60},{32,40}... | collective-permute-start | bytes 393224 | tf_op jit(solution)/shard_map/ppermute | solution.py:290
  11.4 13.6 %collective-permute-start.3 = (bf16[1024,256]{1,0:T(8,128)(2,1)S(1)}, bf16[1024,256]{1,0:T(8,128)(2,1)S(1)}, u32[]{:S(2)}, u32[]{:S(2)}) collective-permute-start(bf16[1024,256]{1,0:T(8,128)(2,1)S(1)} %pad_maximum_fusion.refs_2_), channel_id=1, source_target_pairs={{0,4},{4,0},{1,5},{5,1},{2,6},{6,2},{3,7},{7,3},{8,12},{12,8},{9,1... | collective-permute-start | bytes 1572872 | tf_op jit(solution)/shard_map/ppermute | solution.py:273
  11.5 15.3 %collective-permute-start.6 = (bf16[1024,256]{1,0:T(8,128)(2,1)S(1)}, bf16[1024,256]{1,0:T(8,128)(2,1)S(1)}, u32[]{:S(2)}, u32[]{:S(2)}) collective-permute-start(bf16[1024,256]{1,0:T(8,128)(2,1)S(1)} %pad_maximum_fusion.refs_2_), channel_id=1, source_target_pairs={{0,64},{4,20},{8,72},{12,28},{16,80},{20,4},{24,88},{28,12},{32,96... | collective-permute-start | bytes 1572872 | tf_op jit(solution)/shard_map/ppermute | solution.py:290
  15.4 12.8 %collective-permute-start.5 = (bf16[1024,256]{1,0:T(8,128)(2,1)S(1)}, bf16[1024,256]{1,0:T(8,128)(2,1)S(1)}, u32[]{:S(2)}, u32[]{:S(2)}) collective-permute-start(bf16[1024,256]{1,0:T(8,128)(2,1)S(1)} %pad_maximum_fusion.refs_2_), channel_id=1, source_target_pairs={{0,32},{4,12},{8,40},{12,20},{16,48},{20,28},{24,56},{28,4},{32,64... | collective-permute-start | bytes 1572872 | tf_op jit(solution)/shard_map/ppermute | solution.py:290
  16.5 12.8 %collective-permute-start.4 = (bf16[1024,256]{1,0:T(8,128)(2,1)S(1)}, bf16[1024,256]{1,0:T(8,128)(2,1)S(1)}, u32[]{:S(2)}, u32[]{:S(2)}) collective-permute-start(bf16[1024,256]{1,0:T(8,128)(2,1)S(1)} %pad_maximum_fusion.refs_2_), channel_id=1, source_target_pairs={{0,96},{4,28},{8,104},{12,4},{16,112},{20,12},{24,120},{28,20},{32... | collective-permute-start | bytes 1572872 | tf_op jit(solution)/shard_map/ppermute | solution.py:290
  34.4 7.5 %collective-permute-start.8 = (bf16[256,256]{1,0:T(8,128)(2,1)S(1)}, bf16[256,256]{1,0:T(8,128)(2,1)S(1)}, u32[]{:S(2)}, u32[]{:S(2)}) collective-permute-start(bf16[256,256]{1,0:T(8,128)(2,1)S(1)} %get-tuple-element.61), channel_id=1, source_target_pairs={{0,1},{1,2},{2,3},{3,0},{4,5},{5,6},{6,7},{7,4},{8,9},{9,10},{10,1... | collective-permute-start | bytes 393224 | tf_op jit(solution)/shard_map/ppermute | solution.py:273
  36.1 9.2 %collective-permute-start.9 = (bf16[256,256]{1,0:T(8,128)(2,1)S(1)}, bf16[256,256]{1,0:T(8,128)(2,1)S(1)}, u32[]{:S(2)}, u32[]{:S(2)}) collective-permute-start(bf16[256,256]{1,0:T(8,128)(2,1)S(1)} %get-tuple-element.62), channel_id=1, source_target_pairs={{0,2},{1,3},{2,0},{3,1},{4,6},{5,7},{6,4},{7,5},{8,10},{9,11},{10,... | collective-permute-start | bytes 393224 | tf_op jit(solution)/shard_map/ppermute | solution.py:273
  47.0 7.9 %collective-permute-start.11 = (bf16[320,256]{1,0:T(8,128)(2,1)S(1)}, bf16[320,256]{1,0:T(8,128)(2,1)S(1)}, u32[]{:S(2)}, u32[]{:S(2)}) collective-permute-start(bf16[320,256]{1,0:T(8,128)(2,1)S(1)} %get-tuple-element.67), channel_id=1, source_target_pairs={{0,1},{1,2},{2,3},{3,0},{4,5},{5,6},{6,7},{7,4},{8,9},{9,10},{10,1... | collective-permute-start | bytes 491528 | tf_op jit(solution)/shard_map/ppermute | solution.py:273
  48.7 9.0 %collective-permute-start.12 = (bf16[320,256]{1,0:T(8,128)(2,1)S(1)}, bf16[320,256]{1,0:T(8,128)(2,1)S(1)}, u32[]{:S(2)}, u32[]{:S(2)}) collective-permute-start(bf16[320,256]{1,0:T(8,128)(2,1)S(1)} %get-tuple-element.68), channel_id=1, source_target_pairs={{0,2},{1,3},{2,0},{3,1},{4,6},{5,7},{6,4},{7,5},{8,10},{9,11},{10,... | collective-permute-start | bytes 491528 | tf_op jit(solution)/shard_map/ppermute | solution.py:273
  51.0 6.6 %collective-permute-start.13 = (bf16[320,256]{1,0:T(8,128)(2,1)S(1)}, bf16[320,256]{1,0:T(8,128)(2,1)S(1)}, u32[]{:S(2)}, u32[]{:S(2)}) collective-permute-start(bf16[320,256]{1,0:T(8,128)(2,1)S(1)} %get-tuple-element.69), channel_id=1, source_target_pairs={{0,3},{1,0},{2,1},{3,2},{4,7},{5,4},{6,5},{7,6},{8,11},{9,8},{10,9... | collective-permute-start | bytes 491528 | tf_op jit(solution)/shard_map/ppermute | solution.py:273
  61.4 9.0 %collective-permute-start.16 = (bf16[2048,256]{1,0:T(8,128)(2,1)S(1)}, bf16[2048,256]{1,0:T(8,128)(2,1)S(1)}, u32[]{:S(2)}, u32[]{:S(2)}) collective-permute-start(bf16[2048,256]{1,0:T(8,128)(2,1)S(1)} %get-tuple-element.79), channel_id=1, source_target_pairs={{0,4},{4,0},{1,5},{5,1},{2,6},{6,2},{3,7},{7,3},{8,12},{12,8},{9,1... | collective-permute-start | bytes 3145736 | tf_op jit(solution)/shard_map/ppermute | solution.py:273
  64.1 6.2 %collective-permute-start.19 = (bf16[64,256]{1,0:T(8,128)(2,1)S(1)}, bf16[64,256]{1,0:T(8,128)(2,1)S(1)}, u32[]{:S(2)}, u32[]{:S(2)}) collective-permute-start(bf16[64,256]{1,0:T(8,128)(2,1)S(1)} %get-tuple-element.80.refs_4_), channel_id=1, source_target_pairs={{0,24},{8,0},{16,8},{24,16},{1,25},{9,1},{17,9},{25,17},{2,26},{10... | collective-permute-start | bytes 98312 | tf_op jit(solution)/shard_map/ppermute | solution.py:273
  64.5 5.9 %collective-permute-start.18 = (bf16[64,256]{1,0:T(8,128)(2,1)S(1)}, bf16[64,256]{1,0:T(8,128)(2,1)S(1)}, u32[]{:S(2)}, u32[]{:S(2)}) collective-permute-start(bf16[64,256]{1,0:T(8,128)(2,1)S(1)} %get-tuple-element.80.refs_4_), channel_id=1, source_target_pairs={{0,16},{8,24},{16,0},{24,8},{1,17},{9,25},{17,1},{25,9},{2,18},{10... | collective-permute-start | bytes 98312 | tf_op jit(solution)/shard_map/ppermute | solution.py:273
  66.2 13.1 %collective-permute-start.15 = (bf16[1024,256]{1,0:T(8,128)(2,1)S(1)}, bf16[1024,256]{1,0:T(8,128)(2,1)S(1)}, u32[]{:S(2)}, u32[]{:S(2)}) collective-permute-start(bf16[1024,256]{1,0:T(8,128)(2,1)S(1)} %get-tuple-element.77), channel_id=1, source_target_pairs={{0,16},{4,68},{8,24},{12,76},{16,0},{20,84},{24,8},{28,92},{32,48}... | collective-permute-start | bytes 1572872 | tf_op jit(solution)/shard_map/ppermute | solution.py:290
  72.9 11.7 %collective-permute-start.20 = (bf16[1024,256]{1,0:T(8,128)(2,1)S(1)}, bf16[1024,256]{1,0:T(8,128)(2,1)S(1)}, u32[]{:S(2)}, u32[]{:S(2)}) collective-permute-start(bf16[1024,256]{1,0:T(8,128)(2,1)S(1)} %get-tuple-element.81), channel_id=1, source_target_pairs={{0,8},{4,36},{8,16},{12,44},{16,24},{20,52},{24,0},{28,60},{32,40}... | collective-permute-start | bytes 1572872 | tf_op jit(solution)/shard_map/ppermute | solution.py:290
  73.5 11.0 %collective-permute-start.21 = (bf16[1024,256]{1,0:T(8,128)(2,1)S(1)}, bf16[1024,256]{1,0:T(8,128)(2,1)S(1)}, u32[]{:S(2)}, u32[]{:S(2)}) collective-permute-start(bf16[1024,256]{1,0:T(8,128)(2,1)S(1)} %get-tuple-element.82), channel_id=1, source_target_pairs={{0,24},{4,100},{8,0},{12,108},{16,8},{20,116},{24,16},{28,124},{32... | collective-permute-start | bytes 1572872 | tf_op jit(solution)/shard_map/ppermute | solution.py:290
  78.8 5.4 %collective-permute-start.23 = (bf16[64,256]{1,0:T(8,128)(2,1)S(1)}, bf16[64,256]{1,0:T(8,128)(2,1)S(1)}, u32[]{:S(2)}, u32[]{:S(2)}) collective-permute-start(bf16[64,256]{1,0:T(8,128)(2,1)S(1)} %get-tuple-element.83.q), channel_id=1, source_target_pairs={{0,64},{32,96},{64,0},{96,32},{1,65},{33,97},{65,1},{97,33},{2,66}... | collective-permute-start | bytes 98312 | tf_op jit(solution)/shard_map/ppermute | solution.py:273
  79.3 5.3 %collective-permute-start.22 = (bf16[64,256]{1,0:T(8,128)(2,1)S(1)}, bf16[64,256]{1,0:T(8,128)(2,1)S(1)}, u32[]{:S(2)}, u32[]{:S(2)}) collective-permute-start(bf16[64,256]{1,0:T(8,128)(2,1)S(1)} %get-tuple-element.83.q), channel_id=1, source_target_pairs={{0,32},{32,64},{64,96},{96,0},{1,33},{33,65},{65,97},{97,1},{2,34}... | collective-permute-start | bytes 98312 | tf_op jit(solution)/shard_map/ppermute | solution.py:273
  85.4 6.1 %collective-permute-start.28 = (f32[64,256]{1,0:T(8,128)S(1)}, f32[64,256]{1,0:T(8,128)S(1)}, u32[]{:S(2)}, u32[]{:S(2)}) collective-permute-start(f32[64,256]{1,0:T(8,128)S(1)} %get-tuple-element.88), channel_id=1, source_target_pairs={{0,1},{1,0},{2,3},{3,2},{4,5},{5,4},{6,7},{7,6},{8,9},{9,8},{10,11... | collective-permute-start | bytes 196616 | tf_op jit(solution)/shard_map/ppermute | solution.py:277
  87.2 7.6 %collective-permute-start.25 = (bf16[256,256]{1,0:T(8,128)(2,1)S(1)}, bf16[256,256]{1,0:T(8,128)(2,1)S(1)}, u32[]{:S(2)}, u32[]{:S(2)}) collective-permute-start(bf16[256,256]{1,0:T(8,128)(2,1)S(1)} %get-tuple-element.85), channel_id=1, source_target_pairs={{0,32},{4,12},{8,40},{12,20},{16,48},{20,28},{24,56},{28,4},{32,64... | collective-permute-start | bytes 393224 | tf_op jit(solution)/shard_map/ppermute | solution.py:290
  87.2 7.6 %collective-permute-start.26 = (bf16[256,256]{1,0:T(8,128)(2,1)S(1)}, bf16[256,256]{1,0:T(8,128)(2,1)S(1)}, u32[]{:S(2)}, u32[]{:S(2)}) collective-permute-start(bf16[256,256]{1,0:T(8,128)(2,1)S(1)} %get-tuple-element.86), channel_id=1, source_target_pairs={{0,64},{4,20},{8,72},{12,28},{16,80},{20,4},{24,88},{28,12},{32,96... | collective-permute-start | bytes 393224 | tf_op jit(solution)/shard_map/ppermute | solution.py:290
  90.1 5.5 %collective-permute-start.27 = (bf16[256,256]{1,0:T(8,128)(2,1)S(1)}, bf16[256,256]{1,0:T(8,128)(2,1)S(1)}, u32[]{:S(2)}, u32[]{:S(2)}) collective-permute-start(bf16[256,256]{1,0:T(8,128)(2,1)S(1)} %get-tuple-element.87), channel_id=1, source_target_pairs={{0,96},{4,28},{8,104},{12,4},{16,112},{20,12},{24,120},{28,20},{32... | collective-permute-start | bytes 393224 | tf_op jit(solution)/shard_map/ppermute | solution.py:290
  91.5 6.3 %collective-permute-start.29 = (f32[128,256]{1,0:T(8,128)S(1)}, f32[128,256]{1,0:T(8,128)S(1)}, u32[]{:S(2)}, u32[]{:S(2)}) collective-permute-start(f32[128,256]{1,0:T(8,128)S(1)} %constant_dynamic-update-slice_fusion.3.first), channel_id=1, source_target_pairs={{0,3},{1,2},{2,1},{3,0},{4,7},{5,6},{6,5},{7,4},{8,11},{9,10},{10,... | collective-permute-start | bytes 393224 | tf_op jit(solution)/shard_map/ppermute | solution.py:277
  (9 other events, 44.6 us)

commit v7 on v6

--- a/solution.py
+++ b/solution.py
@@ -124,13 +124,12 @@
 WHOLE = (slice(None),)
 
 
-def forward_near(pos, dense, near, near_other, acc):
-    core = pos[PC]
-    acc[...] = jnp.dot(
-        tiles_of(dense, pos, core, 0, WHOLE), near[...], preferred_element_type=F32
-    ) + jnp.dot(
-        tiles_of(dense, pos, 1 - core, 0, WHOLE), near_other[...], preferred_element_type=F32
-    )
+def near_sum(dense, pos, core, near):
+    return jnp.dot(tiles_of(dense, pos, core, 0, WHOLE), near[...], preferred_element_type=F32)
+
+
+def forward_near(pos, dense, near, acc):
+    acc[...] = near_sum(dense, pos, pos[PC], near)
 
 
 FAR = (1, 3, 2)
@@ -143,8 +142,9 @@
     return total
 
 
-def forward_own(pos, dense, far, given, acc):
-    acc[...] = far_sum(given[...], dense, pos, pos[PC], far, WHOLE)
+def forward_own(pos, dense, far, near_other, given, acc):
+    total = given[...] + near_sum(dense, pos, 1 - pos[PC], near_other)
+    acc[...] = far_sum(total, dense, pos, pos[PC], far, WHOLE)
 
 
 def forward_other(blocks, pos, dense, far, given, *outs):
@@ -312,11 +312,11 @@
         aliases={4: 0},
     )(tv, rows, cols, count, in_vmem(dense))
     sums = shape((ROWS, FEAT), F32)
-    dense, acc = dense_call(forward_near, [sums], dense, pos, near, near_other, cost=16 * MIB)
-    far, acc = lax.optimization_barrier((far, acc))
+    dense, acc = dense_call(forward_near, [sums], dense, pos, near, cost=16 * MIB)
+    far, acc, near_other = lax.optimization_barrier((far, acc, near_other))
     far = jnp.concatenate(far, axis=0)
     far_other = send(far, "core", 1, 2)
-    dense, acc = dense_call(forward_own, [sums], dense, pos, far, acc)
+    dense, acc = dense_call(forward_own, [sums], dense, pos, far, near_other, acc)
     block, blockf = shape((NODE, FEAT), BF16), shape((NODE, FEAT), F32)
 
     def other_columns(dense, blocks, outs):

time: 99.4 us -> 99.4 us (level)
    ppermute x12, waiting for transfers between devices: 7.59 us -> 8.76 us  [send_by_core(): return lax.ppermute(v, RING, pairs)]
  transfers between devices with their start and end apart: 30 -> 30, of which waited for: 17 -> 17; matrix products, arithmetic and copies ran while one was open for 0% -> 0% of each run, Pallas kernels for 20% -> 19%
where the time goes in v7:
time: 99.4 us; the launch traced here: 99.1 us
  starting transfers between devices  45 us (45%)
  waiting for transfers between devices  26.5 us (27%)
  Pallas kernels  25.9 us (26%)
  between operations  1.48 us (1%)
    ppermute x12, starting transfers between devices, send_by_core(): return lax.ppermute(v, RING, pairs)  24.2 us
    ppermute x16, starting transfers between devices, send(): return lax.ppermute(v, axis, [(i, (i + d) % n) for i in range(n)])  17.5 us
    ppermute x16, waiting for transfers between devices, send(): return lax.ppermute(v, axis, [(i, (i + d) % n) for i in range(n)])  15.5 us
    pallas_call x8, Pallas kernels, dense_call(): call(wrapped, [DENSE] + outs, [SSPEC] + [VSPEC] * (n - 1), scratch, flops...  14.4 us
    ppermute x12, waiting for transfers between devices, send_by_core(): return lax.ppermute(v, RING, pairs)  8.76 us
    pallas_call x1, Pallas kernels, body(): call(dense_block, DENSE, [ASPEC, ASPEC, ASPEC, SSPEC, VSPEC], [pltpu.SMEM...  5.03 us
    ppermute x2, starting transfers between devices, swap(): return lax.ppermute(v, axis, [(i, i ^ step) for i in range(4)])  3.41 us
    pallas_call x1, Pallas kernels, body(): dense = call(dense_zeros, DENSE, [SSPEC], nbytes=16 * MIB)(pos)  2.77 us
  transfers between devices with their start and end apart: 30, of which 17 were waited for; matrix products, arithmetic and copies ran while one was open for 0% of the time, Pallas kernels for 19%

profile of v7, /device:TPU:0, one launch (start us, length us, event | category | flops | bytes accessed | tf_op | source)
XLA Modules:
  0.0 99.1 jit_solution(15071074034042817997)
XLA Ops:
  0.6 3.2 %collective-permute-start.1 = (bf16[256,256]{1,0:T(8,128)(2,1)}, bf16[256,256]{1,0:T(8,128)(2,1)S(1)}, u32[]{:S(2)}, u32[]{:S(2)}) collective-permute-start(bf16[256,256]{1,0:T(8,128)(2,1)} %param.7), channel_id=1, source_target_pairs={{0,16},{4,68},{8,24},{12,76},{16,0},{20,84},{24,8},{28,92},{32,48}... | collective-permute-start | bytes 393224 | tf_op jit(solution)/shard_map/ppermute | solution.py:290
  5.9 2.8 %shard_map.94.given = bf16[64,1024,128]{2,1,0:T(8,128)(2,1)S(1)} custom-call(s32[9]{0:T(128)S(1)} %stack.39.pos.refs_0_), custom_call_target="tpu_custom_call" | custom-call | bytes 16777216 | tf_op jit(solution)/shard_map/pallas_call | solution.py:302
  9.0 2.4 %collective-permute-done.2 = bf16[256,256]{1,0:T(8,128)(2,1)S(1)} collective-permute-done((bf16[256,256]{1,0:T(8,128)(2,1)}, bf16[256,256]{1,0:T(8,128)(2,1)S(1)}, u32[]{:S(2)}, u32[]{:S(2)}) %collective-permute-start.2) | collective-permute-done | bytes 131104 | tf_op jit(solution)/shard_map/ppermute | solution.py:290
  11.5 4.0 %collective-permute-start.5 = (bf16[1024,256]{1,0:T(8,128)(2,1)S(1)}, bf16[1024,256]{1,0:T(8,128)(2,1)S(1)}, u32[]{:S(2)}, u32[]{:S(2)}) collective-permute-start(bf16[1024,256]{1,0:T(8,128)(2,1)S(1)} %pad_maximum_fusion.refs_2_), channel_id=1, source_target_pairs={{0,64},{4,20},{8,72},{12,28},{16,80},{20,4},{24,88},{28,12},{32,96... | collective-permute-start | bytes 1572872 | tf_op jit(solution)/shard_map/ppermute | solution.py:290
  16.5 2.2 %collective-permute-start.3 = (bf16[1024,256]{1,0:T(8,128)(2,1)S(1)}, bf16[1024,256]{1,0:T(8,128)(2,1)S(1)}, u32[]{:S(2)}, u32[]{:S(2)}) collective-permute-start(bf16[1024,256]{1,0:T(8,128)(2,1)S(1)} %pad_maximum_fusion.refs_2_), channel_id=1, source_target_pairs={{0,96},{4,28},{8,104},{12,4},{16,112},{20,12},{24,120},{28,20},{32... | collective-permute-start | bytes 1572872 | tf_op jit(solution)/shard_map/ppermute | solution.py:290
  19.3 5.0 %shard_map.95.refs_1_ = bf16[64,1024,128]{2,1,0:T(8,128)(2,1)S(1)} custom-call(bf16[384,128,128]{2,1,0:T(8,128)(2,1)} %bitcast.12, s32[1,1,384]{2,1,0:T(1,128)} %rows_in.1, s32[1,1,384]{2,1,0:T(1,128)} %cols_in.1, s32[1]{0:T(128)} %bitcast.11.count, bf16[64,1024,128]{2,1,0:T(8,128)(2,1)S(1)} %shard_map.94.given), custom_call_target="tpu_custom_call", output_to_operand_aliasing={{}: (4, {})} | custom-call | bytes 25165824 | tf_op jit(solution)/shard_map/pallas_call | solution.py:306
  25.6 2.6 %collective-permute-done.4 = bf16[1024,256]{1,0:T(8,128)(2,1)S(1)} collective-permute-done((bf16[1024,256]{1,0:T(8,128)(2,1)S(1)}, bf16[1024,256]{1,0:T(8,128)(2,1)S(1)}, u32[]{:S(2)}, u32[]{:S(2)}) %collective-permute-start.4) | collective-permute-done | bytes 524320 | tf_op jit(solution)/shard_map/ppermute | solution.py:290
  29.5 2.9 %shard_map.97 = (bf16[64,1024,128]{2,1,0:T(8,128)(2,1)S(1)}, f32[1024,256]{1,0:T(8,128)S(1)}) custom-call(s32[9]{0:T(128)S(1)} %stack.39.pos.refs_0_, bf16[64,1024,128]{2,1,0:T(8,128)(2,1)S(1)} %get-tuple-element.52.refs_1_, bf16[3072,256]{1,0:T(8,128)(2,1)S(1)} %constant_dynamic-update-slice_fusion.refs_2_, ...), custom_call_target="tpu_custom_call", output_to_operand_aliasing={{0}: (1, {})} | custom-call | flops 1000 | bytes 1000 | tf_op jit(solution)/shard_map/pallas_call | solution.py:61
  36.1 2.9 %collective-permute-start.9 = (bf16[256,256]{1,0:T(8,128)(2,1)S(1)}, bf16[256,256]{1,0:T(8,128)(2,1)S(1)}, u32[]{:S(2)}, u32[]{:S(2)}) collective-permute-start(bf16[256,256]{1,0:T(8,128)(2,1)S(1)} %get-tuple-element.64), channel_id=1, source_target_pairs={{0,2},{1,3},{2,0},{3,1},{4,6},{5,7},{6,4},{7,5},{8,10},{9,11},{10,... | collective-permute-start | bytes 393224 | tf_op jit(solution)/shard_map/ppermute | solution.py:273
  41.9 3.4 %collective-permute-done.9.r2 = bf16[256,256]{1,0:T(8,128)(2,1)S(1)} collective-permute-done((bf16[256,256]{1,0:T(8,128)(2,1)S(1)}, bf16[256,256]{1,0:T(8,128)(2,1)S(1)}, u32[]{:S(2)}, u32[]{:S(2)}) %collective-permute-start.9) | collective-permute-done | bytes 131104 | tf_op jit(solution)/shard_map/ppermute | solution.py:273
  48.7 2.3 %collective-permute-start.12 = (bf16[320,256]{1,0:T(8,128)(2,1)S(1)}, bf16[320,256]{1,0:T(8,128)(2,1)S(1)}, u32[]{:S(2)}, u32[]{:S(2)}) collective-permute-start(bf16[320,256]{1,0:T(8,128)(2,1)S(1)} %get-tuple-element.70), channel_id=1, source_target_pairs={{0,2},{1,3},{2,0},{3,1},{4,6},{5,7},{6,4},{7,5},{8,10},{9,11},{10,... | collective-permute-start | bytes 491528 | tf_op jit(solution)/shard_map/ppermute | solution.py:273
  51.9 2.9 %collective-permute-done.11.refs_3_ = bf16[320,256]{1,0:T(8,128)(2,1)S(1)} collective-permute-done((bf16[320,256]{1,0:T(8,128)(2,1)S(1)}, bf16[320,256]{1,0:T(8,128)(2,1)S(1)}, u32[]{:S(2)}, u32[]{:S(2)}) %collective-permute-start.11) | collective-permute-done | bytes 163872 | tf_op jit(solution)/shard_map/ppermute | solution.py:273
  54.8 2.8 %collective-permute-done.12.refs_4_ = bf16[320,256]{1,0:T(8,128)(2,1)S(1)} collective-permute-done((bf16[320,256]{1,0:T(8,128)(2,1)S(1)}, bf16[320,256]{1,0:T(8,128)(2,1)S(1)}, u32[]{:S(2)}, u32[]{:S(2)}) %collective-permute-start.12) | collective-permute-done | bytes 163872 | tf_op jit(solution)/shard_map/ppermute | solution.py:273
  57.6 1.8 %shard_map.102 = (bf16[64,1024,128]{2,1,0:T(8,128)(2,1)S(1)}, bf16[2176,256]{1,0:T(8,128)(2,1)S(1)}, bf16[4,256,256]{2,1,0:T(8,128)(2,1)S(1)}, f32[64,256]{1,0:T(8,128)S(1)}) custom-call(s32[9]{0:T(128)S(1)} %stack.39.pos.refs_0_, bf16[64,1024,128]{2,1,0:T(8,128)(2,1)S(1)} %get-tuple-element.67.refs_1_, ...), custom_call_target="tpu_custom_call", output_to_operand_aliasing={{0}: (1, {})} | custom-call | flops 1000 | bytes 1000 | tf_op jit(solution)/shard_map/pallas_call | solution.py:61
  59.6 1.8 %shard_map.103 = (bf16[64,1024,128]{2,1,0:T(8,128)(2,1)S(1)}, bf16[2048,256]{1,0:T(8,128)(2,1)S(1)}) custom-call(s32[9]{0:T(128)S(1)} %stack.39.pos.refs_0_, bf16[64,1024,128]{2,1,0:T(8,128)(2,1)S(1)} %get-tuple-element.73.refs_1_, bf16[4,256,256]{2,1,0:T(8,128)(2,1)S(1)} %get-tuple-element.74.refs_2_), custom_call_target="tpu_custom_call", output_to_operand_aliasing={{0}: (1, {})} | custom-call | flops 1000 | bytes 1000 | tf_op jit(solution)/shard_map/pallas_call | solution.py:61
  62.3 1.8 %shard_map.104 = (bf16[64,1024,128]{2,1,0:T(8,128)(2,1)S(1)}, bf16[64,256]{1,0:T(8,128)(2,1)S(1)}, bf16[1024,256]{1,0:T(8,128)(2,1)S(1)}, f32[1024,256]{1,0:T(8,128)S(1)}) custom-call(s32[9]{0:T(128)S(1)} %stack.39.pos.refs_0_, bf16[64,1024,128]{2,1,0:T(8,128)(2,1)S(1)} %get-tuple-element.75.refs_1_, ...), custom_call_target="tpu_custom_call", output_to_operand_aliasing={{0}: (1, {})} | custom-call | flops 1000 | bytes 1000 | tf_op jit(solution)/shard_map/pallas_call | solution.py:61
  66.2 4.1 %collective-permute-start.15 = (bf16[1024,256]{1,0:T(8,128)(2,1)S(1)}, bf16[1024,256]{1,0:T(8,128)(2,1)S(1)}, u32[]{:S(2)}, u32[]{:S(2)}) collective-permute-start(bf16[1024,256]{1,0:T(8,128)(2,1)S(1)} %get-tuple-element.79), channel_id=1, source_target_pairs={{0,16},{4,68},{8,24},{12,76},{16,0},{20,84},{24,8},{28,92},{32,48}... | collective-permute-start | bytes 1572872 | tf_op jit(solution)/shard_map/ppermute | solution.py:290
  71.0 1.8 %shard_map.106 = (bf16[64,1024,128]{2,1,0:T(8,128)(2,1)S(1)}, bf16[64,256]{1,0:T(8,128)(2,1)S(1)}, bf16[1024,256]{1,0:T(8,128)(2,1)S(1)}, bf16[1024,256]{1,0:T(8,128)(2,1)S(1)}) custom-call(s32[9]{0:T(128)S(1)} %stack.39.pos.refs_0_, bf16[64,1024,128]{2,1,0:T(8,128)(2,1)S(1)} %get-tuple-element.80.refs_1_, ...), custom_call_target="tpu_custom_call", output_to_operand_aliasing={{0}: (1, {})} | custom-call | flops 1000 | bytes 1000 | tf_op jit(solution)/shard_map/pallas_call | solution.py:61
  73.6 2.6 %collective-permute-start.21 = (bf16[1024,256]{1,0:T(8,128)(2,1)S(1)}, bf16[1024,256]{1,0:T(8,128)(2,1)S(1)}, u32[]{:S(2)}, u32[]{:S(2)}) collective-permute-start(bf16[1024,256]{1,0:T(8,128)(2,1)S(1)} %get-tuple-element.84), channel_id=1, source_target_pairs={{0,24},{4,100},{8,0},{12,108},{16,8},{20,116},{24,16},{28,124},{32... | collective-permute-start | bytes 1572872 | tf_op jit(solution)/shard_map/ppermute | solution.py:290
  76.2 2.6 %collective-permute-start.24 = (bf16[64,256]{1,0:T(8,128)(2,1)S(1)}, bf16[64,256]{1,0:T(8,128)(2,1)S(1)}, u32[]{:S(2)}, u32[]{:S(2)}) collective-permute-start(bf16[64,256]{1,0:T(8,128)(2,1)S(1)} %get-tuple-element.85.q), channel_id=1, source_target_pairs={{0,96},{32,0},{64,32},{96,64},{1,97},{33,1},{65,33},{97,65},{2,98}... | collective-permute-start | bytes 98312 | tf_op jit(solution)/shard_map/ppermute | solution.py:273
  80.6 3.7 %collective-permute-done.23.q2 = bf16[64,256]{1,0:T(8,128)(2,1)S(1)} collective-permute-done((bf16[64,256]{1,0:T(8,128)(2,1)S(1)}, bf16[64,256]{1,0:T(8,128)(2,1)S(1)}, u32[]{:S(2)}, u32[]{:S(2)}) %collective-permute-start.23) | collective-permute-done | bytes 32800 | tf_op jit(solution)/shard_map/ppermute | solution.py:273
  85.4 1.8 %collective-permute-start.28 = (f32[64,256]{1,0:T(8,128)S(1)}, f32[64,256]{1,0:T(8,128)S(1)}, u32[]{:S(2)}, u32[]{:S(2)}) collective-permute-start(f32[64,256]{1,0:T(8,128)S(1)} %get-tuple-element.90), channel_id=1, source_target_pairs={{0,1},{1,0},{2,3},{3,2},{4,5},{5,4},{6,7},{7,6},{8,9},{9,8},{10,11... | collective-permute-start | bytes 196616 | tf_op jit(solution)/shard_map/ppermute | solution.py:277
  87.2 3.0 %collective-permute-start.26 = (bf16[256,256]{1,0:T(8,128)(2,1)S(1)}, bf16[256,256]{1,0:T(8,128)(2,1)S(1)}, u32[]{:S(2)}, u32[]{:S(2)}) collective-permute-start(bf16[256,256]{1,0:T(8,128)(2,1)S(1)} %get-tuple-element.88), channel_id=1, source_target_pairs={{0,64},{4,20},{8,72},{12,28},{16,80},{20,4},{24,88},{28,12},{32,96... | collective-permute-start | bytes 393224 | tf_op jit(solution)/shard_map/ppermute | solution.py:290
  95.6 2.2 %collective-permute-done.29.second = f32[128,256]{1,0:T(8,128)S(1)} collective-permute-done((f32[128,256]{1,0:T(8,128)S(1)}, f32[128,256]{1,0:T(8,128)S(1)}, u32[]{:S(2)}, u32[]{:S(2)}) %collective-permute-start.29) | collective-permute-done | bytes 131104 | tf_op jit(solution)/shard_map/ppermute | solution.py:277
  (64 shorter events, 31.1 us)
Async XLA Ops:
  0.6 8.1 %collective-permute-start.1 = (bf16[256,256]{1,0:T(8,128)(2,1)}, bf16[256,256]{1,0:T(8,128)(2,1)S(1)}, u32[]{:S(2)}, u32[]{:S(2)}) collective-permute-start(bf16[256,256]{1,0:T(8,128)(2,1)} %param.7), channel_id=1, source_target_pairs={{0,16},{4,68},{8,24},{12,76},{16,0},{20,84},{24,8},{28,92},{32,48}... | collective-permute-start | bytes 393224 | tf_op jit(solution)/shard_map/ppermute | solution.py:290
  5.0 6.4 %collective-permute-start.2 = (bf16[256,256]{1,0:T(8,128)(2,1)}, bf16[256,256]{1,0:T(8,128)(2,1)S(1)}, u32[]{:S(2)}, u32[]{:S(2)}) collective-permute-start(bf16[256,256]{1,0:T(8,128)(2,1)} %param.7), channel_id=1, source_target_pairs={{0,8},{4,36},{8,16},{12,44},{16,24},{20,52},{24,0},{28,60},{32,40}... | collective-permute-start | bytes 393224 | tf_op jit(solution)/shard_map/ppermute | solution.py:290
  11.4 14.2 %collective-permute-start.6 = (bf16[1024,256]{1,0:T(8,128)(2,1)S(1)}, bf16[1024,256]{1,0:T(8,128)(2,1)S(1)}, u32[]{:S(2)}, u32[]{:S(2)}) collective-permute-start(bf16[1024,256]{1,0:T(8,128)(2,1)S(1)} %pad_maximum_fusion.refs_2_), channel_id=1, source_target_pairs={{0,4},{4,0},{1,5},{5,1},{2,6},{6,2},{3,7},{7,3},{8,12},{12,8},{9,1... | collective-permute-start | bytes 1572872 | tf_op jit(solution)/shard_map/ppermute | solution.py:273
  11.5 14.1 %collective-permute-start.5 = (bf16[1024,256]{1,0:T(8,128)(2,1)S(1)}, bf16[1024,256]{1,0:T(8,128)(2,1)S(1)}, u32[]{:S(2)}, u32[]{:S(2)}) collective-permute-start(bf16[1024,256]{1,0:T(8,128)(2,1)S(1)} %pad_maximum_fusion.refs_2_), channel_id=1, source_target_pairs={{0,64},{4,20},{8,72},{12,28},{16,80},{20,4},{24,88},{28,12},{32,96... | collective-permute-start | bytes 1572872 | tf_op jit(solution)/shard_map/ppermute | solution.py:290
  15.4 12.8 %collective-permute-start.4 = (bf16[1024,256]{1,0:T(8,128)(2,1)S(1)}, bf16[1024,256]{1,0:T(8,128)(2,1)S(1)}, u32[]{:S(2)}, u32[]{:S(2)}) collective-permute-start(bf16[1024,256]{1,0:T(8,128)(2,1)S(1)} %pad_maximum_fusion.refs_2_), channel_id=1, source_target_pairs={{0,32},{4,12},{8,40},{12,20},{16,48},{20,28},{24,56},{28,4},{32,64... | collective-permute-start | bytes 1572872 | tf_op jit(solution)/shard_map/ppermute | solution.py:290
  16.5 12.8 %collective-permute-start.3 = (bf16[1024,256]{1,0:T(8,128)(2,1)S(1)}, bf16[1024,256]{1,0:T(8,128)(2,1)S(1)}, u32[]{:S(2)}, u32[]{:S(2)}) collective-permute-start(bf16[1024,256]{1,0:T(8,128)(2,1)S(1)} %pad_maximum_fusion.refs_2_), channel_id=1, source_target_pairs={{0,96},{4,28},{8,104},{12,4},{16,112},{20,12},{24,120},{28,20},{32... | collective-permute-start | bytes 1572872 | tf_op jit(solution)/shard_map/ppermute | solution.py:290
  34.4 7.5 %collective-permute-start.8 = (bf16[256,256]{1,0:T(8,128)(2,1)S(1)}, bf16[256,256]{1,0:T(8,128)(2,1)S(1)}, u32[]{:S(2)}, u32[]{:S(2)}) collective-permute-start(bf16[256,256]{1,0:T(8,128)(2,1)S(1)} %get-tuple-element.63), channel_id=1, source_target_pairs={{0,1},{1,2},{2,3},{3,0},{4,5},{5,6},{6,7},{7,4},{8,9},{9,10},{10,1... | collective-permute-start | bytes 393224 | tf_op jit(solution)/shard_map/ppermute | solution.py:273
  36.1 9.2 %collective-permute-start.9 = (bf16[256,256]{1,0:T(8,128)(2,1)S(1)}, bf16[256,256]{1,0:T(8,128)(2,1)S(1)}, u32[]{:S(2)}, u32[]{:S(2)}) collective-permute-start(bf16[256,256]{1,0:T(8,128)(2,1)S(1)} %get-tuple-element.64), channel_id=1, source_target_pairs={{0,2},{1,3},{2,0},{3,1},{4,6},{5,7},{6,4},{7,5},{8,10},{9,11},{10,... | collective-permute-start | bytes 393224 | tf_op jit(solution)/shard_map/ppermute | solution.py:273
  47.0 7.9 %collective-permute-start.11 = (bf16[320,256]{1,0:T(8,128)(2,1)S(1)}, bf16[320,256]{1,0:T(8,128)(2,1)S(1)}, u32[]{:S(2)}, u32[]{:S(2)}) collective-permute-start(bf16[320,256]{1,0:T(8,128)(2,1)S(1)} %get-tuple-element.69), channel_id=1, source_target_pairs={{0,1},{1,2},{2,3},{3,0},{4,5},{5,6},{6,7},{7,4},{8,9},{9,10},{10,1... | collective-permute-start | bytes 491528 | tf_op jit(solution)/shard_map/ppermute | solution.py:273
  48.7 9.0 %collective-permute-start.12 = (bf16[320,256]{1,0:T(8,128)(2,1)S(1)}, bf16[320,256]{1,0:T(8,128)(2,1)S(1)}, u32[]{:S(2)}, u32[]{:S(2)}) collective-permute-start(bf16[320,256]{1,0:T(8,128)(2,1)S(1)} %get-tuple-element.70), channel_id=1, source_target_pairs={{0,2},{1,3},{2,0},{3,1},{4,6},{5,7},{6,4},{7,5},{8,10},{9,11},{10,... | collective-permute-start | bytes 491528 | tf_op jit(solution)/shard_map/ppermute | solution.py:273
  51.0 6.6 %collective-permute-start.13 = (bf16[320,256]{1,0:T(8,128)(2,1)S(1)}, bf16[320,256]{1,0:T(8,128)(2,1)S(1)}, u32[]{:S(2)}, u32[]{:S(2)}) collective-permute-start(bf16[320,256]{1,0:T(8,128)(2,1)S(1)} %get-tuple-element.71), channel_id=1, source_target_pairs={{0,3},{1,0},{2,1},{3,2},{4,7},{5,4},{6,5},{7,6},{8,11},{9,8},{10,9... | collective-permute-start | bytes 491528 | tf_op jit(solution)/shard_map/ppermute | solution.py:273
  61.4 9.0 %collective-permute-start.16 = (bf16[2048,256]{1,0:T(8,128)(2,1)S(1)}, bf16[2048,256]{1,0:T(8,128)(2,1)S(1)}, u32[]{:S(2)}, u32[]{:S(2)}) collective-permute-start(bf16[2048,256]{1,0:T(8,128)(2,1)S(1)} %get-tuple-element.81), channel_id=1, source_target_pairs={{0,4},{4,0},{1,5},{5,1},{2,6},{6,2},{3,7},{7,3},{8,12},{12,8},{9,1... | collective-permute-start | bytes 3145736 | tf_op jit(solution)/shard_map/ppermute | solution.py:273
  64.1 6.2 %collective-permute-start.19 = (bf16[64,256]{1,0:T(8,128)(2,1)S(1)}, bf16[64,256]{1,0:T(8,128)(2,1)S(1)}, u32[]{:S(2)}, u32[]{:S(2)}) collective-permute-start(bf16[64,256]{1,0:T(8,128)(2,1)S(1)} %get-tuple-element.82.refs_4_), channel_id=1, source_target_pairs={{0,24},{8,0},{16,8},{24,16},{1,25},{9,1},{17,9},{25,17},{2,26},{10... | collective-permute-start | bytes 98312 | tf_op jit(solution)/shard_map/ppermute | solution.py:273
  64.5 5.9 %collective-permute-start.18 = (bf16[64,256]{1,0:T(8,128)(2,1)S(1)}, bf16[64,256]{1,0:T(8,128)(2,1)S(1)}, u32[]{:S(2)}, u32[]{:S(2)}) collective-permute-start(bf16[64,256]{1,0:T(8,128)(2,1)S(1)} %get-tuple-element.82.refs_4_), channel_id=1, source_target_pairs={{0,16},{8,24},{16,0},{24,8},{1,17},{9,25},{17,1},{25,9},{2,18},{10... | collective-permute-start | bytes 98312 | tf_op jit(solution)/shard_map/ppermute | solution.py:273
  66.2 13.1 %collective-permute-start.15 = (bf16[1024,256]{1,0:T(8,128)(2,1)S(1)}, bf16[1024,256]{1,0:T(8,128)(2,1)S(1)}, u32[]{:S(2)}, u32[]{:S(2)}) collective-permute-start(bf16[1024,256]{1,0:T(8,128)(2,1)S(1)} %get-tuple-element.79), channel_id=1, source_target_pairs={{0,16},{4,68},{8,24},{12,76},{16,0},{20,84},{24,8},{28,92},{32,48}... | collective-permute-start | bytes 1572872 | tf_op jit(solution)/shard_map/ppermute | solution.py:290
  72.9 11.7 %collective-permute-start.20 = (bf16[1024,256]{1,0:T(8,128)(2,1)S(1)}, bf16[1024,256]{1,0:T(8,128)(2,1)S(1)}, u32[]{:S(2)}, u32[]{:S(2)}) collective-permute-start(bf16[1024,256]{1,0:T(8,128)(2,1)S(1)} %get-tuple-element.83), channel_id=1, source_target_pairs={{0,8},{4,36},{8,16},{12,44},{16,24},{20,52},{24,0},{28,60},{32,40}... | collective-permute-start | bytes 1572872 | tf_op jit(solution)/shard_map/ppermute | solution.py:290
  73.6 11.0 %collective-permute-start.21 = (bf16[1024,256]{1,0:T(8,128)(2,1)S(1)}, bf16[1024,256]{1,0:T(8,128)(2,1)S(1)}, u32[]{:S(2)}, u32[]{:S(2)}) collective-permute-start(bf16[1024,256]{1,0:T(8,128)(2,1)S(1)} %get-tuple-element.84), channel_id=1, source_target_pairs={{0,24},{4,100},{8,0},{12,108},{16,8},{20,116},{24,16},{28,124},{32... | collective-permute-start | bytes 1572872 | tf_op jit(solution)/shard_map/ppermute | solution.py:290
  78.8 5.4 %collective-permute-start.23 = (bf16[64,256]{1,0:T(8,128)(2,1)S(1)}, bf16[64,256]{1,0:T(8,128)(2,1)S(1)}, u32[]{:S(2)}, u32[]{:S(2)}) collective-permute-start(bf16[64,256]{1,0:T(8,128)(2,1)S(1)} %get-tuple-element.85.q), channel_id=1, source_target_pairs={{0,64},{32,96},{64,0},{96,32},{1,65},{33,97},{65,1},{97,33},{2,66}... | collective-permute-start | bytes 98312 | tf_op jit(solution)/shard_map/ppermute | solution.py:273
  79.3 5.3 %collective-permute-start.22 = (bf16[64,256]{1,0:T(8,128)(2,1)S(1)}, bf16[64,256]{1,0:T(8,128)(2,1)S(1)}, u32[]{:S(2)}, u32[]{:S(2)}) collective-permute-start(bf16[64,256]{1,0:T(8,128)(2,1)S(1)} %get-tuple-element.85.q), channel_id=1, source_target_pairs={{0,32},{32,64},{64,96},{96,0},{1,33},{33,65},{65,97},{97,1},{2,34}... | collective-permute-start | bytes 98312 | tf_op jit(solution)/shard_map/ppermute | solution.py:273
  85.4 6.1 %collective-permute-start.28 = (f32[64,256]{1,0:T(8,128)S(1)}, f32[64,256]{1,0:T(8,128)S(1)}, u32[]{:S(2)}, u32[]{:S(2)}) collective-permute-start(f32[64,256]{1,0:T(8,128)S(1)} %get-tuple-element.90), channel_id=1, source_target_pairs={{0,1},{1,0},{2,3},{3,2},{4,5},{5,4},{6,7},{7,6},{8,9},{9,8},{10,11... | collective-permute-start | bytes 196616 | tf_op jit(solution)/shard_map/ppermute | solution.py:277
  87.2 7.6 %collective-permute-start.25 = (bf16[256,256]{1,0:T(8,128)(2,1)S(1)}, bf16[256,256]{1,0:T(8,128)(2,1)S(1)}, u32[]{:S(2)}, u32[]{:S(2)}) collective-permute-start(bf16[256,256]{1,0:T(8,128)(2,1)S(1)} %get-tuple-element.87), channel_id=1, source_target_pairs={{0,32},{4,12},{8,40},{12,20},{16,48},{20,28},{24,56},{28,4},{32,64... | collective-permute-start | bytes 393224 | tf_op jit(solution)/shard_map/ppermute | solution.py:290
  87.2 7.6 %collective-permute-start.26 = (bf16[256,256]{1,0:T(8,128)(2,1)S(1)}, bf16[256,256]{1,0:T(8,128)(2,1)S(1)}, u32[]{:S(2)}, u32[]{:S(2)}) collective-permute-start(bf16[256,256]{1,0:T(8,128)(2,1)S(1)} %get-tuple-element.88), channel_id=1, source_target_pairs={{0,64},{4,20},{8,72},{12,28},{16,80},{20,4},{24,88},{28,12},{32,96... | collective-permute-start | bytes 393224 | tf_op jit(solution)/shard_map/ppermute | solution.py:290
  90.1 5.5 %collective-permute-start.27 = (bf16[256,256]{1,0:T(8,128)(2,1)S(1)}, bf16[256,256]{1,0:T(8,128)(2,1)S(1)}, u32[]{:S(2)}, u32[]{:S(2)}) collective-permute-start(bf16[256,256]{1,0:T(8,128)(2,1)S(1)} %get-tuple-element.89), channel_id=1, source_target_pairs={{0,96},{4,28},{8,104},{12,4},{16,112},{20,12},{24,120},{28,20},{32... | collective-permute-start | bytes 393224 | tf_op jit(solution)/shard_map/ppermute | solution.py:290
  91.5 6.3 %collective-permute-start.29 = (f32[128,256]{1,0:T(8,128)S(1)}, f32[128,256]{1,0:T(8,128)S(1)}, u32[]{:S(2)}, u32[]{:S(2)}) collective-permute-start(f32[128,256]{1,0:T(8,128)S(1)} %constant_dynamic-update-slice_fusion.3.first), channel_id=1, source_target_pairs={{0,3},{1,2},{2,1},{3,0},{4,7},{5,6},{6,5},{7,4},{8,11},{9,10},{10,... | collective-permute-start | bytes 393224 | tf_op jit(solution)/shard_map/ppermute | solution.py:277
  (9 other events, 44.6 us)
